TPU v7x, 128 devices: a whole 4x4x4 slice. The times are simulated.
128 devices in a mesh: view: 4 (over y_lo, core), tile: 32 (over z, y_hi, x).
Axes of the slice: x: 4, y: 4 (y_hi: 2, y_lo: 2; y = y_hi * 2 + y_lo), z: 4, core: 2. Of those that a mesh axis runs over, the one named last changes fastest.
Arguments:
- source_features: bfloat16 [20, 32, 256, 128], P('view', None, 'tile'), may hold values from -6 to 6
- reference_features: bfloat16 [32, 32768], P(None, 'tile'), may hold values from -6 to 6
- interp: bfloat16 [20, 8, 4, 64, 64], P('view'), may hold values from -0.375 to 0.375
- source_tile: int32 [20, 8, 512, 4], P('view', None, 'tile'), may hold values from -1 to 1
- source_block: int32 [20, 8, 512, 4], P('view', None, 'tile'), may hold values from 0 to 15
- conv_weight: bfloat16 [3, 3, 3, 8, 32], replicated, may hold values from -0.21875 to 0.21875
- grad_regularized: bfloat16 [8, 8, 32768], P('view', None, 'tile'), may hold values from -6 to 6
Outputs:
- regularized: bfloat16 [8, 8, 32768], P('view', None, 'tile')
- grad_source: float32 [20, 32, 256, 128], P('view', None, 'tile')
Inputs may be any that keep to these rules, and one draw needn't show every extreme that they name: source_tile is the offset of a source block's row tile from the tile of the output block it feeds. source_block is the block's index within that row tile.
All inputs are finite; a program needn't handle non-finite values.
Results may differ from a plain program's by a relative error of at most 0.0056.
Values may be sent and summed in bfloat16 or wider, within the bound.
No kernel may reach another device: no remote copies, remote signals or barrier semaphores. Data moves between devices by JAX's collectives and lax.ppermute only.
A program may use at most 128 MiB of HBM per device.

v0:
```python
import jax
import jax.numpy as jnp
from jax import lax
from jax.sharding import PartitionSpec as P

BLK = 64
VIEW_DEV = 5
PANEL = 2
ROWS_DEV = 4
COLS = 256


def padded_2(array, sides, width):
    for axis, dim in sides:
        devices, length = (lax.axis_size(axis), array.shape[dim])
        up = [(i, (i + 1) % devices) for i in range(devices - 1)]
        down = [(j, i) for i, j in up]
        last = lax.slice_in_dim(array, length - width, length, axis=dim)
        initial = lax.slice_in_dim(array, 0, width, axis=dim)
        before = lax.ppermute(last, axis, up)
        after = lax.ppermute(initial, axis, down)
        array = jnp.concatenate([before, array, after], axis=dim)
    return array


def shift_cols(values, offset):
    pads = [(0, 0)] * (values.ndim - 1)
    if offset > 0:
        return jnp.pad(values[..., 1:], pads + [(0, 1)])
    return jnp.pad(values[..., :-1], pads + [(1, 0)])


def convolve(padded, conv_weight, count):
    rows = padded.shape[2] - 2
    result = jnp.zeros((count, conv_weight.shape[3], rows, padded.shape[3]), jnp.float32)
    for plane_tap in range(3):
        for row_tap in range(3):
            part = padded[plane_tap : plane_tap + count, :, row_tap : row_tap + rows, :]
            for col_tap in range(3):
                term = jnp.einsum(
                    "oh,phrx->porx",
                    conv_weight[plane_tap, row_tap, col_tap],
                    part,
                    preferred_element_type=jnp.float32,
                )
                if col_tap == 1:
                    result = result + term
                else:
                    result = result + shift_cols(term, col_tap - 1)
    return result


def convolve_back(padded, conv_weight, count):
    rows = padded.shape[2] - 2
    result = jnp.zeros((count, conv_weight.shape[4], rows, padded.shape[3]), jnp.float32)
    for plane_tap in range(3):
        for row_tap in range(3):
            part = padded[
                2 - plane_tap : 2 - plane_tap + count, :, 2 - row_tap : 2 - row_tap + rows, :
            ]
            for col_tap in range(3):
                term = jnp.einsum(
                    "oh,porx->phrx",
                    conv_weight[plane_tap, row_tap, col_tap],
                    part,
                    preferred_element_type=jnp.float32,
                )
                if col_tap == 1:
                    result = result + term
                else:
                    result = result + shift_cols(term, 1 - col_tap)
    return result


def one_hot_table(view_place, segments, dtype):
    flat_place = view_place.reshape(-1)
    slots = jnp.arange(segments, dtype=jnp.int32)
    return (flat_place[:, None] == slots[None, :]).astype(dtype)


def body(
    source_features,
    reference_features,
    interp,
    source_tile,
    source_block,
    conv_weight,
    grad_regularized,
):
    views = source_features.shape[0]
    channels = source_features.shape[1]
    strip = source_features.shape[2]
    height = source_features.shape[3]
    out_channels = conv_weight.shape[3]
    rows = ROWS_DEV
    tiles = lax.axis_size("tile")
    planes = PANEL * lax.axis_size("view")
    count = float(VIEW_DEV * lax.axis_size("view") + 1)
    pixels = COLS * rows
    blocks_tile = pixels // BLK
    segments = 3 * blocks_tile
    taps = interp.shape[2]
    padded_rows = jnp.pad(source_features, ((0, 0), (0, 0), (0, 0), (rows, rows)))
    bands = jnp.stack(
        [padded_rows[:, :, :, shift * rows : shift * rows + height] for shift in range(3)], axis=1
    )
    bands = bands.reshape(views, 3, channels, strip, tiles, rows).transpose(0, 1, 2, 4, 5, 3)
    arrived = lax.all_to_all(bands, "tile", split_axis=3, concat_axis=5, tiled=True)
    blocks = arrived.reshape(views, 3, channels, blocks_tile, BLK).transpose(0, 1, 3, 2, 4)
    blocks = blocks.reshape(views, segments, channels * BLK)
    place = (source_tile + 1) * blocks_tile + source_block

    def warp_view(view_blocks, view_place, view_interp):
        table = one_hot_table(view_place, segments, jnp.bfloat16)
        picked = jnp.dot(table, view_blocks, preferred_element_type=jnp.float32).astype(
            jnp.bfloat16
        )
        picked = picked.reshape(planes, blocks_tile, taps, channels, BLK)
        warped = jnp.einsum(
            "dgkci,dkij->dcgj", picked, view_interp, preferred_element_type=jnp.float32
        )
        return warped.reshape(planes, channels, pixels)

    zero_sum = jnp.zeros((planes, channels, pixels), jnp.float32)

    def forward_step(carry, inputs):
        warped = warp_view(inputs[0], inputs[1], inputs[2])
        return ((carry[0] + warped, carry[1] + warped * warped), warped)

    (first_sum, second_sum), stored = lax.scan(
        forward_step, (zero_sum, zero_sum), (blocks, place, interp)
    )
    ref_float = reference_features.astype(jnp.float32)
    first_part, second_part = (
        lax.psum_scatter(first_sum, "view", scatter_dimension=0, tiled=True),
        lax.psum_scatter(second_sum, "view", scatter_dimension=0, tiled=True),
    )
    first_part = first_part + ref_float
    second_part = second_part + ref_float * ref_float
    mean = first_part / count
    cost = (second_part / count - mean * mean).astype(jnp.bfloat16)
    joined = jnp.concatenate([cost, grad_regularized], axis=1).reshape(
        PANEL, channels + out_channels, rows, COLS
    )
    rimmed = padded_2(joined, (("view", 0), ("tile", 2)), 1)
    regularized = convolve(rimmed[:, :channels], conv_weight, PANEL)
    grad_cost = convolve_back(rimmed[:, channels:], conv_weight, PANEL).reshape(
        PANEL, channels, pixels
    )
    grad_square = (grad_cost / count).astype(jnp.bfloat16)
    grad_mean = (-2.0 * first_part / (count * count) * grad_cost).astype(jnp.bfloat16)
    grad_mean, grad_square = (
        lax.all_gather(grad_mean, "view", axis=0, tiled=True),
        lax.all_gather(grad_square, "view", axis=0, tiled=True),
    )
    regularized = regularized.reshape(PANEL, out_channels, pixels).astype(jnp.bfloat16)
    mean_float = grad_mean.astype(jnp.float32)
    square_float = grad_square.astype(jnp.float32)

    def land(warped, view_place, view_interp):
        grad_warped = (mean_float + 2.0 * warped * square_float).astype(jnp.bfloat16)
        spread = jnp.einsum(
            "dcgj,dkij->dgkci",
            grad_warped.reshape(planes, channels, blocks_tile, BLK),
            view_interp,
            preferred_element_type=jnp.float32,
        )
        table = one_hot_table(view_place, segments, jnp.float32)
        summed = jnp.dot(
            table.T,
            spread.reshape(-1, channels * BLK),
            precision=lax.Precision.HIGHEST,
            preferred_element_type=jnp.float32,
        )
        return summed.reshape(segments, channels, BLK)

    def backward_step(carry, inputs):
        return (carry, land(inputs[3], inputs[1], inputs[2]))

    unused, landed = lax.scan(
        backward_step, jnp.zeros((), jnp.float32), (blocks, place, interp, stored)
    )
    landed = landed.reshape(views, 3, blocks_tile, channels, BLK).transpose(0, 1, 3, 2, 4)
    landed = landed.reshape(views, 3, channels, 1, rows, COLS)
    returned = lax.all_to_all(landed, "tile", split_axis=5, concat_axis=3, tiled=True)
    returned = returned.transpose(0, 1, 2, 5, 3, 4).reshape(views, 3, channels, strip, height)
    combined = jnp.zeros((views, channels, strip, height + 2 * rows), jnp.float32)
    for shift in range(3):
        combined = combined + jnp.pad(
            returned[:, shift], ((0, 0), (0, 0), (0, 0), (shift * rows, (2 - shift) * rows))
        )
    grad_source = combined[:, :, :, rows : rows + height]
    return (regularized, grad_source)


def solution(mesh):
    return jax.shard_map(
        body,
        mesh=mesh,
        in_specs=(
            P("view", None, "tile", None),
            P(None, "tile"),
            P("view", None, None, None, None),
            P("view", None, "tile", None),
            P("view", None, "tile", None),
            P(),
            P("view", None, "tile"),
        ),
        out_specs=(P("view", None, "tile"), P("view", None, "tile", None)),
        check_vma=False,
    )
```

profile of v0, /device:TPU:32, one launch (start us, length us, event | category | flops | bytes accessed | tf_op | source)
XLA Modules:
  0.0 507.1 jit_solution(4648281187734101464)
XLA Ops:
  12.2 6.6 %reshape.113 = bf16[32,2,7680]{2,1,0:T(2,128)(2,1)} reshape(bf16[32,3,5,4,8,32]{5,4,3,2,1,0:T(8,128)(2,1)} %copy_bitcast_fusion.5) | data formatting | bytes 1966080
  18.9 10.7 %all-to-all-start = ((bf16[32,2,7680]{2,1,0:T(2,128)(2,1)}), bf16[32,2,7680]{2,1,0:T(2,128)(2,1)S(1)}, u32[]{:S(2)}, u32[]{:S(2)}) async-start(bf16[32,2,7680]{2,1,0:T(2,128)(2,1)} %reshape.113), calls=%async_computation | async-start | bytes 1966080 | tf_op jit(solution)/shard_map/all_to_all | solution.py:108
  30.8 14.9 %all-to-all-done = bf16[32,2,7680]{2,1,0:T(2,128)(2,1)S(1)} async-done(((bf16[32,2,7680]{2,1,0:T(2,128)(2,1)}), bf16[32,2,7680]{2,1,0:T(2,128)(2,1)S(1)}, u32[]{:S(2)}, u32[]{:S(2)}) %all-to-all-start) | async-done | bytes 983072 | tf_op jit(solution)/shard_map/all_to_all | solution.py:108
  61.0 84.5 %while.26 = (s32[]{:T(128)}, f32[8,32,1024]{2,1,0:T(8,128)}, f32[8,32,1024]{2,1,0:T(8,128)}, f32[5,8,32,1024]{3,2,1,0:T(8,128)}, bf16[5,8,4,64,64]{4,3,2,1,0:T(8...) while((s32[]{:T(128)}, f32[8,32,1024]{2,1,0:T(8,128)}, ...), condition=%wide.region_1.2_spmd.clone, body=%wide.region_0.1_spmd.clone.sunk | while | flops 237264896 | bytes 25897088 | solution.py:130
  146.3 17.1 %reduce-scatter.3.cloned.1.call-done = f32[2,32,1024]{2,1,0:T(8,128)} async-done(((f32[8,32,1024]{2,1,0:T(8,128)}), f32[2,32,1024]{2,1,0:T(8,128)}) %reduce-scatter.3.cloned.1.call-update) | async-done | bytes 262160 | tf_op jit(solution)/shard_map/reduce_scatter | solution.py:136
  163.4 23.9 %reduce-scatter.5.cloned.1.call-done = f32[2,32,1024]{2,1,0:T(8,128)} async-done(((f32[8,32,1024]{2,1,0:T(8,128)}), f32[2,32,1024]{2,1,0:T(8,128)}) %reduce-scatter.5.cloned.1.call-update) | async-done | bytes 262160 | tf_op jit(solution)/shard_map/reduce_scatter | solution.py:135
  197.0 6.8 %collective-permute-start.3 = (bf16[4,40,1,256]{3,1,2,0:T(8,128)(2,1)S(1)}, bf16[4,40,1,256]{3,1,2,0:T(8,128)(2,1)S(1)}, u32[]{:S(2)}, u32[]{:S(2)}) collective-permute-start(bf16[4,40,1,256]{3,1,2,0:T(8,128)(2,1)S(1)} %get-tuple-element.160), channel_id=1, source_target_pairs={{1,0},{2,1},{3,2},{4,3},{5,4},{6,5},{7,6},{8,7},{9,8},{10,9},{11,1... | collective-permute-start | bytes 245768 | tf_op jit(solution)/shard_map/ppermute | solution.py:21
  207.7 6.9 %collective-permute-done.2 = bf16[4,40,1,256]{3,1,2,0:T(8,128)(2,1)S(1)} collective-permute-done((bf16[4,40,1,256]{3,1,2,0:T(8,128)(2,1)S(1)}, bf16[4,40,1,256]{3,1,2,0:T(8,128)(2,1)S(1)}, u32[]{:S(2)}, u32[]{:S(2)}) %collective-permute-start.2) | collective-permute-done | bytes 81952 | tf_op jit(solution)/shard_map/ppermute | solution.py:20
  229.0 7.8 %all_gather.6 = bf16[8,32,1024]{2,1,0:T(8,128)(2,1)S(1)} all-gather(bf16[2,32,1024]{2,1,0:T(8,128)(2,1)S(1)} %get-tuple-element.163), channel_id=1, replica_groups=mesh['view'=4,'tile'=32] {'view'}, dimensions={0}, use_global_device_ids=true | all-gather | bytes 655360 | tf_op jit(solution)/shard_map/all_gather | solution.py:153
  237.9 7.3 %all_gather.7 = bf16[8,32,1024]{2,1,0:T(8,128)(2,1)S(1)} all-gather(bf16[2,32,1024]{2,1,0:T(8,128)(2,1)S(1)} %get-tuple-element.162), channel_id=1, replica_groups=mesh['view'=4,'tile'=32] {'view'}, dimensions={0}, use_global_device_ids=true | all-gather | bytes 655360 | tf_op jit(solution)/shard_map/all_gather | solution.py:154
  245.3 176.5 %while.25 = (s32[]{:T(128)}, f32[5,48,32,64]{3,1,2,0:T(8,128)}, s32[5,8,16,4]{3,2,1,0:T(8,128)S(1)}, bf16[5,8,4,64,64]{4,3,2,1,0:T(8,128)(2,1)}, f32[8,32,1024]{...) while((s32[]{:T(128)}, f32[5,48,32,64]{3,1,2,0:T(8,128)}, ...), condition=%wide.region_5.6_spmd, body=%wide.region_4.5_spmd.sunk | while | flops 739270656 | bytes 56895652 | solution.py:180
  261.1 7.8 %reshape.124 = f32[512,2048]{1,0:T(8,128)} reshape(f32[8,16,4,32,64]{4,3,2,1,0:T(8,128)} %copy.198) | data formatting | bytes 8388608 | tf_op jit(solution)/shard_map/while/body/eval_jaxpr/reshape | solution.py:171
  274.4 6.2 %fusion.260 = f32[5,48,32,64]{3,1,2,0:T(8,128)} fusion(f32[5,48,32,64]{3,1,2,0:T(8,128)} %get-tuple-element.299, s32[]{:T(128)S(6)} %copy.221, f32[32,64,512]{2,1,0:T(8,128)} %bitcast.645, s32[512]{0:T(512)S(1)} %eq.65), kind=kOutput, calls=%fused_computation.5.clone.1 | convolution fusion | flops 604004352 | bytes 4982788 | tf_op jit(solution)/shard_map/while/body/eval_jaxpr/dot_general | solution.py:169
  296.4 7.8 %reshape.124 = f32[512,2048]{1,0:T(8,128)} reshape(f32[8,16,4,32,64]{4,3,2,1,0:T(8,128)} %copy.198) | data formatting | bytes 8388608 | tf_op jit(solution)/shard_map/while/body/eval_jaxpr/reshape | solution.py:171
  309.7 6.2 %fusion.260 = f32[5,48,32,64]{3,1,2,0:T(8,128)} fusion(f32[5,48,32,64]{3,1,2,0:T(8,128)} %get-tuple-element.299, s32[]{:T(128)S(6)} %copy.221, f32[32,64,512]{2,1,0:T(8,128)} %bitcast.645, s32[512]{0:T(512)S(1)} %eq.65), kind=kOutput, calls=%fused_computation.5.clone.1 | convolution fusion | flops 604004352 | bytes 4982788 | tf_op jit(solution)/shard_map/while/body/eval_jaxpr/dot_general | solution.py:169
  331.7 7.8 %reshape.124 = f32[512,2048]{1,0:T(8,128)} reshape(f32[8,16,4,32,64]{4,3,2,1,0:T(8,128)} %copy.198) | data formatting | bytes 8388608 | tf_op jit(solution)/shard_map/while/body/eval_jaxpr/reshape | solution.py:171
  345.0 6.2 %fusion.260 = f32[5,48,32,64]{3,1,2,0:T(8,128)} fusion(f32[5,48,32,64]{3,1,2,0:T(8,128)} %get-tuple-element.299, s32[]{:T(128)S(6)} %copy.221, f32[32,64,512]{2,1,0:T(8,128)} %bitcast.645, s32[512]{0:T(512)S(1)} %eq.65), kind=kOutput, calls=%fused_computation.5.clone.1 | convolution fusion | flops 604004352 | bytes 4982788 | tf_op jit(solution)/shard_map/while/body/eval_jaxpr/dot_general | solution.py:169
  367.0 7.8 %reshape.124 = f32[512,2048]{1,0:T(8,128)} reshape(f32[8,16,4,32,64]{4,3,2,1,0:T(8,128)} %copy.198) | data formatting | bytes 8388608 | tf_op jit(solution)/shard_map/while/body/eval_jaxpr/reshape | solution.py:171
  402.3 7.8 %reshape.124 = f32[512,2048]{1,0:T(8,128)} reshape(f32[8,16,4,32,64]{4,3,2,1,0:T(8,128)} %copy.198) | data formatting | bytes 8388608 | tf_op jit(solution)/shard_map/while/body/eval_jaxpr/reshape | solution.py:171
  415.6 6.2 %fusion.260 = f32[5,48,32,64]{3,1,2,0:T(8,128)} fusion(f32[5,48,32,64]{3,1,2,0:T(8,128)} %get-tuple-element.299, s32[]{:T(128)S(6)} %copy.221, f32[32,64,512]{2,1,0:T(8,128)} %bitcast.645, s32[512]{0:T(512)S(1)} %eq.65), kind=kOutput, calls=%fused_computation.5.clone.1 | convolution fusion | flops 604004352 | bytes 4982788 | tf_op jit(solution)/shard_map/while/body/eval_jaxpr/dot_general | solution.py:169
  429.7 6.8 %copy.113 = f32[5,3,32,1,4,256]{2,4,1,0,3,5:T(4,128)} copy(f32[5,3,32,1,4,256]{5,4,2,1,0,3:T(4,128)S(1)} %reshape.77) | data formatting | bytes 3932160 | tf_op jit(solution)/shard_map/reshape | solution.py:184
  436.5 8.3 %reshape.115 = f32[32,1,15360]{2,1,0:T(1,128)} reshape(f32[256,1,5,3,4,32]{5,4,3,2,1,0:T(4,128)} %bitcast.646) | data formatting | bytes 3932160
  460.4 16.9 %all-to-all-done.1 = f32[32,1,15360]{2,1,0:T(1,128)S(1)} async-done(((f32[32,1,15360]{2,1,0:T(1,128)}), f32[32,1,15360]{2,1,0:T(1,128)S(1)}, u32[]{:S(2)}, u32[]{:S(2)}) %all-to-all-start.1) | async-done | bytes 1966112 | tf_op jit(solution)/shard_map/all_to_all | solution.py:185
  479.2 6.9 %reduce = f32[32,15360]{1,0:T(8,128)S(1)} reduce(f32[32,1,15360]{2,1,0:T(1,128)} %copy-done.2, f32[]{:T(128)} %broadcast.112), dimensions={1}, to_apply=%all_to_all.27.reduce_sub_computation | reduce | bytes 3932164 | tf_op jit(solution)/shard_map/all_to_all | solution.py:185
  (309 shorter events, 286.7 us)
Async XLA Ops:
  12.2 17.9 %copy-start.34 = (s32[5,8,16,4]{2,3,1,0:T(4,128)S(1)}, s32[5,8,16,4]{2,3,1,0:T(4,128)}, u32[]{:S(2)}) copy-start(s32[5,8,16,4]{2,3,1,0:T(4,128)} %param.15) | copy-start | bytes 30724
  12.2 18.2 %copy-start.35 = (s32[5,8,16,4]{2,3,1,0:T(4,128)S(1)}, s32[5,8,16,4]{2,3,1,0:T(4,128)}, u32[]{:S(2)}) copy-start(s32[5,8,16,4]{2,3,1,0:T(4,128)} %param.14) | copy-start | bytes 30724
  18.9 26.8 %all-to-all-start = ((bf16[32,2,7680]{2,1,0:T(2,128)(2,1)}), bf16[32,2,7680]{2,1,0:T(2,128)(2,1)S(1)}, u32[]{:S(2)}, u32[]{:S(2)}) async-start(bf16[32,2,7680]{2,1,0:T(2,128)(2,1)} %reshape.113), calls=%async_computation | async-start | bytes 1966080 | tf_op jit(solution)/shard_map/all_to_all | solution.py:108
  29.5 133.8 %reduce-scatter.3.cloned.1.call-start = ((), (), s32[]{:S(2)}) async-start(), calls=%async_computation.4 | async-start | bytes 1310720 | tf_op jit(solution)/shard_map/reduce_scatter | solution.py:136
  61.0 85.3 %copy-start.22 = (bf16[32,1024]{1,0:T(8,128)(2,1)S(1)}, bf16[32,1024]{1,0:T(8,128)(2,1)}, u32[]{:S(2)}) copy-start(bf16[32,1024]{1,0:T(8,128)(2,1)} %param.12) | copy-start | bytes 196612
  145.4 42.9 %copy-start.33 = (bf16[2,8,1024]{2,1,0:T(8,128)(2,1)S(1)}, bf16[2,8,1024]{2,1,0:T(8,128)(2,1)}, u32[]{:S(2)}) copy-start(bf16[2,8,1024]{2,1,0:T(8,128)(2,1)} %param.17) | copy-start | bytes 98308
  145.4 43.0 %copy-start.32 = (bf16[3,3,3,8,32]{4,3,2,1,0:T(8,128)(2,1)S(1)}, bf16[3,3,3,8,32]{4,3,2,1,0:T(8,128)(2,1)}, u32[]{:S(2)}) copy-start(bf16[3,3,3,8,32]{4,3,2,1,0:T(8,128)(2,1)} %param.16) | copy-start | bytes 41476
  145.5 41.8 %reduce-scatter.5.cloned.1.call-start = ((), (), s32[]{:S(2)}) async-start(), calls=%async_computation.5 | async-start | bytes 1310720 | tf_op jit(solution)/shard_map/reduce_scatter | solution.py:135
  188.4 39.2 %copy-start.3 = (bf16[2,5,4,8,256]{4,3,1,2,0:T(8,128)(2,1)}, bf16[2,5,4,8,256]{4,3,1,2,0:T(8,128)(2,1)S(1)}, u32[]{:S(2)}) copy-start(bf16[2,5,4,8,256]{4,3,1,2,0:T(8,128)(2,1)S(1)} %copy.186) | copy-start | bytes 491524
  189.7 4.5 collective-permute-start
  192.0 3.3 collective-permute-start.1
  194.2 13.5 %copy-start.19 = (bf16[3,40,4,256]{3,1,2,0:T(8,128)(2,1)}, bf16[3,40,4,256]{3,1,2,0:T(8,128)(2,1)S(1)}, u32[]{:S(2)}) copy-start(bf16[3,40,4,256]{3,1,2,0:T(8,128)(2,1)S(1)} %get-tuple-element.166) | copy-start | bytes 737284
  195.3 31.5 %copy-start.17 = (bf16[3,40,4,256]{3,1,2,0:T(8,128)(2,1)}, bf16[3,40,4,256]{3,1,2,0:T(8,128)(2,1)S(1)}, u32[]{:S(2)}) copy-start(bf16[3,40,4,256]{3,1,2,0:T(8,128)(2,1)S(1)} %get-tuple-element.169) | copy-start | bytes 737284
  197.0 10.7 %collective-permute-start.3 = (bf16[4,40,1,256]{3,1,2,0:T(8,128)(2,1)S(1)}, bf16[4,40,1,256]{3,1,2,0:T(8,128)(2,1)S(1)}, u32[]{:S(2)}, u32[]{:S(2)}) collective-permute-start(bf16[4,40,1,256]{3,1,2,0:T(8,128)(2,1)S(1)} %get-tuple-element.160), channel_id=1, source_target_pairs={{1,0},{2,1},{3,2},{4,3},{5,4},{6,5},{7,6},{8,7},{9,8},{10,9},{11,1... | collective-permute-start | bytes 245768 | tf_op jit(solution)/shard_map/ppermute | solution.py:21
  203.8 10.8 %collective-permute-start.2 = (bf16[4,40,1,256]{3,1,2,0:T(8,128)(2,1)S(1)}, bf16[4,40,1,256]{3,1,2,0:T(8,128)(2,1)S(1)}, u32[]{:S(2)}, u32[]{:S(2)}) collective-permute-start(bf16[4,40,1,256]{3,1,2,0:T(8,128)(2,1)S(1)} %get-tuple-element.161), channel_id=1, source_target_pairs={{0,1},{1,2},{2,3},{3,4},{4,5},{5,6},{6,7},{7,8},{8,9},{9,10},{10,1... | collective-permute-start | bytes 245768 | tf_op jit(solution)/shard_map/ppermute | solution.py:20
  214.7 9.8 %copy-start.5 = (bf16[2,32,4,256]{3,1,2,0:T(8,128)(2,1)}, bf16[2,32,4,256]{3,1,2,0:T(8,128)(2,1)S(1)}, u32[]{:S(2)}) copy-start(bf16[2,32,4,256]{3,1,2,0:T(8,128)(2,1)S(1)} %get-tuple-element.159) | copy-start | bytes 393220
  214.7 9.8 %copy-start.7 = (bf16[2,32,4,256]{3,1,2,0:T(8,128)(2,1)}, bf16[2,32,4,256]{3,1,2,0:T(8,128)(2,1)S(1)}, u32[]{:S(2)}) copy-start(bf16[2,32,4,256]{3,1,2,0:T(8,128)(2,1)S(1)} %get-tuple-element.151) | copy-start | bytes 393220
  214.7 9.8 %copy-start.9 = (bf16[2,32,4,256]{3,1,2,0:T(8,128)(2,1)}, bf16[2,32,4,256]{3,1,2,0:T(8,128)(2,1)S(1)}, u32[]{:S(2)}) copy-start(bf16[2,32,4,256]{3,1,2,0:T(8,128)(2,1)S(1)} %get-tuple-element.157) | copy-start | bytes 393220
  214.7 9.8 %copy-start.11 = (bf16[2,32,4,256]{3,1,2,0:T(8,128)(2,1)}, bf16[2,32,4,256]{3,1,2,0:T(8,128)(2,1)S(1)}, u32[]{:S(2)}) copy-start(bf16[2,32,4,256]{3,1,2,0:T(8,128)(2,1)S(1)} %get-tuple-element.150) | copy-start | bytes 393220
  444.9 10.5 %copy-start.4 = (bf16[2,5,4,8,256]{4,3,1,2,0:T(8,128)(2,1)S(1)}, bf16[2,5,4,8,256]{4,3,1,2,0:T(8,128)(2,1)}, u32[]{:S(2)}) copy-start(bf16[2,5,4,8,256]{4,3,1,2,0:T(8,128)(2,1)} %copy-done.3) | copy-start | bytes 491524
  444.9 11.5 %copy-start.8 = (bf16[2,32,4,256]{3,1,2,0:T(8,128)(2,1)S(1)}, bf16[2,32,4,256]{3,1,2,0:T(8,128)(2,1)}, u32[]{:S(2)}) copy-start(bf16[2,32,4,256]{3,1,2,0:T(8,128)(2,1)} %copy-done.7) | copy-start | bytes 393220
  444.9 12.4 %copy-start.6 = (bf16[2,32,4,256]{3,1,2,0:T(8,128)(2,1)S(1)}, bf16[2,32,4,256]{3,1,2,0:T(8,128)(2,1)}, u32[]{:S(2)}) copy-start(bf16[2,32,4,256]{3,1,2,0:T(8,128)(2,1)} %copy-done.5) | copy-start | bytes 393220
  444.9 12.4 %copy-start.28 = (f32[2,8,4,256]{3,1,2,0:T(8,128)S(1)}, f32[2,8,4,256]{3,1,2,0:T(8,128)}, u32[]{:S(2)}) copy-start(f32[2,8,4,256]{3,1,2,0:T(8,128)} %convolution_bitcast_fusion.35) | copy-start | bytes 196612
  444.9 32.4 %all-to-all-start.1 = ((f32[32,1,15360]{2,1,0:T(1,128)}), f32[32,1,15360]{2,1,0:T(1,128)S(1)}, u32[]{:S(2)}, u32[]{:S(2)}) async-start(f32[32,1,15360]{2,1,0:T(1,128)} %reshape.115), calls=%async_computation.3 | async-start | bytes 3932160 | tf_op jit(solution)/shard_map/all_to_all | solution.py:185
  (28 other events, 165.3 us)
Sparse Core Ops, SparseCore 0:
  145.6 17.7 reduce-scatter.2
  165.9 21.3 reduce-scatter.4
where the time goes:
time: 517 us; the launch traced here: 507 us
  local copies, waits for them, and re-layouts  229 us (44%)
  matrix products  104 us (20%)
  waiting for transfers between devices  80.5 us (16%)
  other arithmetic  33.5 us (6%)
  starting transfers between devices  29.5 us (6%)
  between operations  15.4 us (3%)
  blocking collectives  15.1 us (3%)
    reshape x5, local copies, waits for them, and re-layouts, land(): spread.reshape(-1, channels * BLK)  39.2 us
    dot_general x5, matrix products, land(): jnp.dot(table.T, spread.reshape(-1, channels * BLK), precision=lax.Precis...  30.9 us
    unnamed x78, local copies, waits for them, and re-layouts  30.4 us
    dot_general x5, local copies, waits for them, and re-layouts, land(): jnp.dot(table.T, spread.reshape(-1, channels * BLK), precision=lax.Precis...  26.7 us
    reshape x5, local copies, waits for them, and re-layouts, warp_view(): picked = picked.reshape(planes, blocks_tile, taps, channels, BLK)  26.6 us
    reduce_scatter x1, waiting for transfers between devices, body(): lax.psum_scatter(first_sum, 'view', scatter_dimension=0, tiled=True)  23.9 us
    dot_general x5, matrix products, land(): jnp.einsum('dcgj,dkij->dgkci', grad_warped.reshape(planes, channels, bloc...  22.6 us
    transpose x5, local copies, waits for them, and re-layouts, land(): jnp.einsum('dcgj,dkij->dgkci', grad_warped.reshape(planes, channels, bloc...  21.7 us
  transfers between devices with their start and end apart: 8, of which 5 were waited for; matrix products, arithmetic and copies ran while one was open for 3% of the time, Pallas kernels for 0%

commit v1 on v0

v1 whole, which is shorter than its diff:
```python
import functools

import jax
import jax.numpy as jnp
from jax import lax
from jax.experimental import pallas as pl
from jax.experimental.pallas import tpu as pltpu
from jax.sharding import PartitionSpec as P

BF = jnp.bfloat16
F32 = jnp.float32
VIEWS = 5
PLANES = 8
COUNT = 21.0
SEGS = 48
VMEM_LIMIT = 48 * 1024 * 1024
NT = (((1,), (1,)), ((), ()))
NN = (((1,), (0,)), ((), ()))
TN = (((0,), (0,)), ((), ()))


def params():
    return pltpu.CompilerParams(vmem_limit_bytes=VMEM_LIMIT)


def whole():
    return pl.BlockSpec(memory_space=pltpu.VMEM)


def iota(shape, dim):
    return lax.broadcasted_iota(jnp.int32, shape, dim)


def band_table():
    row, lane = iota((96, 128), 0), iota((96, 128), 1)
    return ((lane >> 2) == (row & 31) + (row >> 5) - 1).astype(F32).astype(BF)


def row_mask():
    return (iota((128, 128), 0) >> 5) == (iota((128, 128), 1) & 3)


def strips_kernel(src_ref, out_ref, wide, stage):
    wide[...] = src_ref[...].astype(F32)
    table = band_table()
    mask = row_mask()
    for x in range(8):
        own = wide[pl.ds(x, 160, stride=8), :]
        parts = []
        for v in range(VIEWS):
            part = own[v * 32 : (v + 1) * 32]
            parts.append(jnp.where(mask, jnp.concatenate([part] * 4, axis=0), 0.0).astype(BF))
        stacked = jnp.concatenate(parts, axis=0)
        moved = lax.dot_general(table, stacked, NT, preferred_element_type=F32)
        for v in range(VIEWS):
            for band in range(3):
                stage[v * 3 + band, pl.ds(x, 32, stride=8), :] = moved[
                    band * 32 : (band + 1) * 32, v * 128 : (v + 1) * 128
                ]
    for piece in range(VIEWS * 3):
        out_ref[:, piece * 128 : (piece + 1) * 128] = stage[piece].astype(BF)


def strips(source):
    return pl.pallas_call(
        strips_kernel,
        out_shape=jax.ShapeDtypeStruct((256, VIEWS * 384), BF),
        in_specs=[whole()],
        out_specs=whole(),
        scratch_shapes=[pltpu.VMEM((1280, 128), F32), pltpu.VMEM((VIEWS * 3, 256, 128), F32)],
        compiler_params=params(),
        name="strips",
    )(source)


def unstrips_kernel(in_ref, out_ref, wide):
    for piece in range(VIEWS * 3):
        wide[piece] = in_ref[:, piece * 128 : (piece + 1) * 128].astype(F32)
    table = band_table()
    mask = row_mask()
    for x in range(8):
        columns = []
        for v in range(VIEWS):
            bands = [wide[v * 3 + band, pl.ds(x, 32, stride=8), :] for band in range(3)]
            columns.append(jnp.concatenate(bands, axis=0).astype(BF))
        stacked = jnp.concatenate(columns, axis=1)
        moved = lax.dot_general(stacked, table, TN, preferred_element_type=F32)
        parts = []
        for v in range(VIEWS):
            part = jnp.where(mask, moved[v * 128 : (v + 1) * 128], 0.0)
            parts.append((part[0:32] + part[32:64]) + (part[64:96] + part[96:128]))
        out_ref[pl.ds(x, 160, stride=8), :] = jnp.concatenate(parts, axis=0)


def unstrips(arrived):
    return pl.pallas_call(
        unstrips_kernel,
        out_shape=jax.ShapeDtypeStruct((1280, 128), F32),
        in_specs=[whole()],
        out_specs=whole(),
        scratch_shapes=[pltpu.VMEM((VIEWS * 3, 256, 128), F32)],
        compiler_params=params(),
        name="unstrips",
    )(arrived)


def half_mask(rows):
    return iota((rows, 128), 1) < 64


def spread_interp(values):
    parts = []
    zero = jnp.zeros((64, 64), BF)
    for k in range(4):
        parts.append(jnp.concatenate([values[k], zero], axis=1))
        parts.append(jnp.concatenate([zero, values[k]], axis=1))
    return jnp.concatenate(parts, axis=0)


def pair_swap(low, high):
    mask = half_mask(low.shape[0])
    first = jnp.where(mask, low, pltpu.roll(high, 64, 1))
    second = jnp.where(mask, pltpu.roll(low, 64, 1), high)
    return first, second


def warp_kernel(
    place_ref, order_ref, in_ref, interp_ref, first_o, first_m, second_o, second_m, warped_ref, blocks
):
    view = pl.program_id(0)
    turned = in_ref[...].astype(F32).T
    for band_row in range(12):
        upper = turned[band_row * 32 : band_row * 32 + 16]
        lower = turned[band_row * 32 + 16 : band_row * 32 + 32]
        for half in range(2):
            even, odd = pair_swap(
                upper[:, half * 128 : half * 128 + 128], lower[:, half * 128 : half * 128 + 128]
            )
            blocks[band_row * 4 + half * 2] = even.astype(BF)
            blocks[band_row * 4 + half * 2 + 1] = odd.astype(BF)

    @pl.when(view == 0)
    def _():
        for ref in (first_o, first_m, second_o, second_m):
            ref[...] = jnp.zeros_like(ref)

    for group, (first_ref, second_ref) in enumerate(((first_o, second_o), (first_m, second_m))):

        def step(e, unused, group=group, first_ref=first_ref, second_ref=second_ref):
            plane = order_ref[group * 4 + e]
            base = (view * PLANES + plane) * 64
            rows = []
            for g in range(16):
                taps = [blocks[place_ref[base + g * 4 + k]] for k in range(4)]
                rows.append(jnp.concatenate(taps, axis=1))
            picked = jnp.concatenate(rows, axis=0)
            matrix = spread_interp(interp_ref[0, plane])
            warped = lax.dot_general(picked, matrix, NN, preferred_element_type=F32)
            first_ref[e] += warped
            second_ref[e] += warped * warped
            warped_ref[0, group * 4 + e] = warped.astype(BF)
            return unused

        lax.fori_loop(0, 4, step, 0)


def warp(place, order, arrived, interp):
    sums = jax.ShapeDtypeStruct((4, 256, 128), F32)
    sum_spec = pl.BlockSpec((4, 256, 128), lambda v, p, o: (0, 0, 0))
    return pl.pallas_call(
        warp_kernel,
        grid_spec=pltpu.PrefetchScalarGridSpec(
            num_scalar_prefetch=2,
            grid=(VIEWS,),
            in_specs=[
                pl.BlockSpec((256, 384), lambda v, p, o: (0, v)),
                pl.BlockSpec((1, PLANES, 4, 64, 64), lambda v, p, o: (v, 0, 0, 0, 0)),
            ],
            out_specs=[sum_spec] * 4
            + [pl.BlockSpec((1, PLANES, 256, 128), lambda v, p, o: (v, 0, 0, 0))],
            scratch_shapes=[pltpu.VMEM((SEGS, 16, 128), BF)],
        ),
        out_shape=[sums] * 4 + [jax.ShapeDtypeStruct((VIEWS, PLANES, 256, 128), BF)],
        compiler_params=params(),
        name="warp",
    )(place, order, arrived, interp)


CHAINS = 4


def land_kernel(
    place_ref, order_ref, warped_ref, interp_ref, mean_o, mean_m, grad_ref, out_ref, *accs
):
    view = pl.program_id(0)
    for acc in accs:
        acc[...] = jnp.zeros_like(acc)

    for group, mean_ref in enumerate((mean_o, mean_m)):

        def step(e, unused, group=group, mean_ref=mean_ref):
            plane = order_ref[group * 4 + e]
            base = (view * PLANES + plane) * 64
            warped = warped_ref[0, group * 4 + e].astype(F32)
            grad = (grad_ref[plane] * (warped - mean_ref[e].astype(F32))).astype(BF)
            matrix = spread_interp(interp_ref[0, plane])
            spread = lax.dot_general(grad, matrix, NT, preferred_element_type=F32)
            for g in range(16):
                for k in range(4):
                    where = place_ref[base + g * 4 + k]
                    accs[k][where] += spread[g * 16 : (g + 1) * 16, k * 128 : (k + 1) * 128]
            return unused

        lax.fori_loop(0, 4, step, 0)

    bands = []
    for band_row in range(12):
        columns_up, columns_low = [], []
        for half in range(2):
            at = band_row * 4 + half * 2
            even = (accs[0][at] + accs[1][at]) + (accs[2][at] + accs[3][at])
            odd = (accs[0][at + 1] + accs[1][at + 1]) + (accs[2][at + 1] + accs[3][at + 1])
            up, low = pair_swap(even, odd)
            columns_up.append(up)
            columns_low.append(low)
        bands.append(jnp.concatenate(columns_up, axis=1))
        bands.append(jnp.concatenate(columns_low, axis=1))
    out_ref[...] = jnp.concatenate(bands, axis=0).T.astype(BF)


def land(place, order, warped, interp, mean_other, mean_mine, grad):
    mean_spec = pl.BlockSpec((4, 256, 128), lambda v, p, o: (0, 0, 0))
    return pl.pallas_call(
        land_kernel,
        grid_spec=pltpu.PrefetchScalarGridSpec(
            num_scalar_prefetch=2,
            grid=(VIEWS,),
            in_specs=[
                pl.BlockSpec((1, PLANES, 256, 128), lambda v, p, o: (v, 0, 0, 0)),
                pl.BlockSpec((1, PLANES, 4, 64, 64), lambda v, p, o: (v, 0, 0, 0, 0)),
                mean_spec,
                mean_spec,
                pl.BlockSpec((PLANES, 256, 128), lambda v, p, o: (0, 0, 0)),
            ],
            out_specs=pl.BlockSpec((256, 384), lambda v, p, o: (0, v)),
            scratch_shapes=[pltpu.VMEM((SEGS, 16, 128), F32)] * CHAINS,
        ),
        out_shape=jax.ShapeDtypeStruct((256, VIEWS * 384), BF),
        compiler_params=params(),
        name="land",
    )(place, order, warped, interp, mean_other, mean_mine, grad)


def shifted(values, offset):
    lanes = values.shape[1]
    col = iota(values.shape, 1) & 255
    if offset > 0:
        return jnp.where(col == 255, 0.0, pltpu.roll(values, lanes - 1, 1))
    return jnp.where(col == 0, 0.0, pltpu.roll(values, 1, 1))


def grad_cost_kernel(view_ref, own_ref, top_ref, bottom_ref, weight_ref, out_ref):
    view = view_ref[0]
    padded = []
    for plane in range(PLANES):
        slot = jnp.bitwise_xor(view, plane // 2)
        line = jnp.concatenate(
            [
                top_ref[slot, plane % 2].astype(F32),
                own_ref[slot, plane % 2].astype(F32),
                bottom_ref[slot, plane % 2].astype(F32),
            ],
            axis=1,
        )
        padded.append(jnp.concatenate([shifted(line, 1), line, shifted(line, -1)], axis=0))
    zero = jnp.zeros_like(padded[0])
    weight = weight_ref[...]
    for plane in range(PLANES):
        near = [padded[p] if 0 <= p < PLANES else zero for p in (plane + 1, plane, plane - 1)]
        result = lax.dot_general(
            weight, jnp.concatenate(near, axis=0).astype(BF), NN, preferred_element_type=F32
        )
        grad = result[0:32, 512:1536] + result[32:64, 256:1280] + result[64:96, 0:1024]
        grad = grad * (2.0 / COUNT)
        for pair in range(8):
            upper = grad[0:16, pair * 128 : pair * 128 + 128]
            lower = grad[16:32, pair * 128 : pair * 128 + 128]
            even, odd = pair_swap(upper, lower)
            out_ref[plane, pair * 32 : pair * 32 + 16] = even
            out_ref[plane, pair * 32 + 16 : pair * 32 + 32] = odd


def grad_cost(view, own, top, bottom, weight):
    return pl.pallas_call(
        grad_cost_kernel,
        out_shape=jax.ShapeDtypeStruct((PLANES, 256, 128), F32),
        in_specs=[pl.BlockSpec(memory_space=pltpu.SMEM)] + [whole()] * 4,
        out_specs=whole(),
        compiler_params=params(),
        name="grad_cost",
    )(view, own, top, bottom, weight)


def conv_kernel(below_ref, own_ref, above_ref, top_ref, bottom_ref, weight_ref, out_ref):
    weight = weight_ref[...]
    results = []
    for local in range(4):
        if local == 0:
            middle = below_ref[0]
        elif local == 3:
            middle = above_ref[0]
        else:
            middle = own_ref[local - 1]
        tall = jnp.concatenate([top_ref[local], middle, bottom_ref[local]], axis=0).astype(F32)
        upper, lower = [], []
        for pair in range(12):
            even = tall[pair * 32 : pair * 32 + 16]
            odd = tall[pair * 32 + 16 : pair * 32 + 32]
            up, low = pair_swap(even, odd)
            upper.append(up)
            lower.append(low)
        line = jnp.concatenate(
            [jnp.concatenate(upper, axis=1), jnp.concatenate(lower, axis=1)], axis=0
        )
        wide = jnp.concatenate([shifted(line, -1), line, shifted(line, 1)], axis=0).astype(BF)
        results.append(lax.dot_general(weight, wide, NN, preferred_element_type=F32))
    for plane in range(2):
        total = None
        for a in range(3):
            for b in range(3):
                at = (a * 3 + b) * 8
                part = results[plane + a][at : at + 8, b * 256 : b * 256 + 1024]
                total = part if total is None else total + part
        out_ref[plane] = total.astype(BF)


def conv(below, own, above, top, bottom, weight):
    return pl.pallas_call(
        conv_kernel,
        out_shape=jax.ShapeDtypeStruct((2, 8, 1024), BF),
        in_specs=[whole()] * 6,
        out_specs=whole(),
        compiler_params=params(),
        name="conv",
    )(below, own, above, top, bottom, weight)


def body(
    source_features,
    reference_features,
    interp,
    source_tile,
    source_block,
    conv_weight,
    grad_regularized,
):
    tiles = lax.axis_size("tile")
    views = lax.axis_size("view")
    view = lax.axis_index("view")
    up = [(i, i + 1) for i in range(tiles - 1)]
    down = [(i + 1, i) for i in range(tiles - 1)]

    def other(array, mask):
        return lax.ppermute(array, "view", [(i, i ^ mask) for i in range(views)])

    slots = jnp.arange(8, dtype=jnp.int32)
    y_low, core = view // 2, view % 2
    order = (
        ((slots // 2) % 2 ^ 1 ^ y_low) * 4 + ((slots // 4) ^ 1 ^ core) * 2 + slots % 2
    ).astype(jnp.int32)
    place = ((source_tile + 1) * 16 + source_block).reshape(-1)

    operand = strips(source_features.reshape(1280, 128))
    arrived = lax.all_to_all(operand, "tile", split_axis=0, concat_axis=0, tiled=True)

    own = grad_regularized
    cotangent = jnp.stack([own, other(own, 1), other(own, 2), other(own, 3)])
    top = lax.ppermute(cotangent[..., 768:], "tile", up)
    bottom = lax.ppermute(cotangent[..., :256], "tile", down)
    back_weight = conv_weight.transpose(1, 4, 0, 2, 3).reshape(96, 72)
    grad = grad_cost(view.astype(jnp.int32).reshape(1), cotangent, top, bottom, back_weight)

    first_o, first_m, second_o, second_m, warped = warp(place, order, arrived, interp)
    first_chip = first_m + other(first_o, 1)
    second_chip = second_m + other(second_o, 1)
    first_there = other(first_chip.astype(BF), 2).astype(F32)
    second_there = other(second_chip[:2], 2)
    ref = (
        reference_features.astype(F32).reshape(2, 16, 16, 64).transpose(2, 1, 0, 3).reshape(256, 128)
    )
    first = first_chip + jnp.concatenate([first_there[2:], first_there[:2]], axis=0) + ref
    mean = first / COUNT
    mean_mine = mean.astype(BF)
    mean_other = other(mean_mine, 1)
    second = second_chip[2:] + second_there + ref * ref
    cost = (second / COUNT - mean[2:] * mean[2:]).astype(BF)

    landed = land(place, order, warped, interp, mean_other, mean_mine, grad)
    returned = lax.all_to_all(landed, "tile", split_axis=0, concat_axis=0, tiled=True)

    view_up = [(i, i + 1) for i in range(views - 1)]
    view_down = [(i + 1, i) for i in range(views - 1)]
    below = lax.ppermute(cost[1:], "view", view_up)
    above = lax.ppermute(cost[:1], "view", view_down)
    last = jnp.concatenate([below[:, 192:], cost[:, 192:], above[:, 192:]], axis=0)
    initial = jnp.concatenate([below[:, :64], cost[:, :64], above[:, :64]], axis=0)
    cost_top = lax.ppermute(last, "tile", up)
    cost_bottom = lax.ppermute(initial, "tile", down)
    weight = conv_weight.transpose(0, 1, 3, 2, 4).reshape(72, 96)
    regularized = conv(below, cost, above, cost_top, cost_bottom, weight)

    grad_source = unstrips(returned).reshape(source_features.shape)
    return regularized, grad_source


def solution(mesh):
    return jax.shard_map(
        body,
        mesh=mesh,
        in_specs=(
            P("view", None, "tile", None),
            P(None, "tile"),
            P("view", None, None, None, None),
            P("view", None, "tile", None),
            P("view", None, "tile", None),
            P(),
            P("view", None, "tile"),
        ),
        out_specs=(P("view", None, "tile"), P("view", None, "tile", None)),
        check_vma=False,
    )
```

time: 517 us -> 129 us (0.25)
  the two profiles are of different devices: /device:TPU:32 before, /device:TPU:30 now
where the time goes in v1:
time: 129 us; the launch traced here: 128 us
  waiting for transfers between devices  44.5 us (34%)
  starting transfers between devices  41.1 us (32%)
  Pallas kernels  36.5 us (28%)
  local copies, waits for them, and re-layouts  3.96 us (3%)
    pallas_call x1, Pallas kernels, land(): pl.pallas_call(land_kernel, grid_spec=pltpu.PrefetchScalarGridSpec(num_sc...  16 us
    pallas_call x1, Pallas kernels, warp(): pl.pallas_call(warp_kernel, grid_spec=pltpu.PrefetchScalarGridSpec(num_sc...  14.7 us
    all_to_all x1, waiting for transfers between devices, body(): lax.all_to_all(operand, 'tile', split_axis=0, concat_axis=0, tiled=True)  13.4 us
    all_to_all x1, starting transfers between devices, body(): lax.all_to_all(operand, 'tile', split_axis=0, concat_axis=0, tiled=True)  10.8 us
    ppermute x1, waiting for transfers between devices, body(): below = lax.ppermute(cost[1:], 'view', view_up)  10.2 us
    all_to_all x1, starting transfers between devices, body(): lax.all_to_all(landed, 'tile', split_axis=0, concat_axis=0, tiled=True)  8.93 us
    ppermute x1, waiting for transfers between devices, body(): bottom = lax.ppermute(cotangent[..., :256], 'tile', down)  7.56 us
    ppermute x8, waiting for transfers between devices, other(): return lax.ppermute(array, 'view', [(i, i ^ mask) for i in range(views)])  6.66 us
  transfers between devices with their start and end apart: 16, of which 7 were waited for; matrix products, arithmetic and copies ran while one was open for 2% of the time, Pallas kernels for 14%

profile of v1, /device:TPU:30, one launch (start us, length us, event | category | flops | bytes accessed | tf_op | source)
XLA Modules:
  0.0 128.1 jit_solution(2806058630514646290)
XLA Ops:
  0.6 1.0 copy-done.2
  1.6 1.9 %strips.1 = bf16[256,1920]{1,0:T(8,128)(2,1)} custom-call(bf16[1280,128]{1,0:T(8,128)(2,1)S(1)} %bitcast.20), custom_call_target="tpu_custom_call" | custom-call | tf_op jit(solution)/shard_map/strips/pallas_call | solution.py:65
  3.5 10.8 %all-to-all-start = ((bf16[32,8,1920]{2,1,0:T(8,128)(2,1)}), bf16[32,8,1920]{2,1,0:T(8,128)(2,1)S(1)}, u32[]{:S(2)}, u32[]{:S(2)}) async-start(bf16[32,8,1920]{2,1,0:T(8,128)(2,1)} %bitcast.1), calls=%async_computation | async-start | bytes 1966080 | tf_op jit(solution)/shard_map/all_to_all | solution.py:374
  14.9 13.4 %all-to-all-done = bf16[32,8,1920]{2,1,0:T(8,128)(2,1)S(1)} async-done(((bf16[32,8,1920]{2,1,0:T(8,128)(2,1)}), bf16[32,8,1920]{2,1,0:T(8,128)(2,1)S(1)}, u32[]{:S(2)}, u32[]{:S(2)}) %all-to-all-start) | async-done | bytes 983072 | tf_op jit(solution)/shard_map/all_to_all | solution.py:374
  28.3 14.7 %warp.1 = (f32[4,256,128]{2,1,0:T(8,128)S(1)}, f32[4,256,128]{2,1,0:T(8,128)S(1)}, f32[4,256,128]{2,1,0:T(8,128)S(1)}, f32[4,256,128]{2,1,0:T(8,128)S(1)}, bf16[5,8,256,128]{3,2,1,0:T(8,128)(2,1)S(1)}) custom-call(s32[2560]{0:T(1024)S(1)} %reshape.42.place_ref, s32[8]{0:T(128)S(1)} %fusion.6.order_ref, bf16[256,1920]{1,0:T(8,128)(2,1)S(1)} %bitcast.18, ...), custom_call_target="tpu_custom_call" | custom-call | tf_op jit(solution)/shard_map/warp/pallas_call | solution.py:170
  43.1 1.5 %copy-done = bf16[5,8,256,128]{3,2,1,0:T(8,128)(2,1)} copy-done((bf16[5,8,256,128]{3,2,1,0:T(8,128)(2,1)}, bf16[5,8,256,128]{3,2,1,0:T(8,128)(2,1)S(1)}, u32[]{:S(2)}) %copy-start) | copy-done | bytes 2621464
  44.6 0.9 collective-permute-start.11
  45.5 1.2 collective-permute-start.10
  48.0 0.8 collective-permute-start.3
  49.4 6.0 %collective-permute-start.12 = (bf16[4,2,8,256]{3,2,1,0:T(8,128)(2,1)S(1)}, bf16[4,2,8,256]{3,2,1,0:T(8,128)(2,1)S(1)}, u32[]{:S(2)}, u32[]{:S(2)}) collective-permute-start(bf16[4,2,8,256]{3,2,1,0:T(8,128)(2,1)S(1)} %get-tuple-element.19), channel_id=1, source_target_pairs={{0,1},{1,2},{2,3},{3,4},{4,5},{5,6},{6,7},{7,8},{8,9},{9,10},{10,1... | collective-permute-start | bytes 98312 | tf_op jit(solution)/shard_map/ppermute | solution.py:378
  55.5 1.9 %collective-permute-start.13 = (bf16[4,2,8,256]{3,2,1,0:T(8,128)(2,1)S(1)}, bf16[4,2,8,256]{3,2,1,0:T(8,128)(2,1)S(1)}, u32[]{:S(2)}, u32[]{:S(2)}) collective-permute-start(bf16[4,2,8,256]{3,2,1,0:T(8,128)(2,1)S(1)} %get-tuple-element.18), channel_id=1, source_target_pairs={{1,0},{2,1},{3,2},{4,3},{5,4},{6,5},{7,6},{8,7},{9,8},{10,9},{11,1... | collective-permute-start | bytes 98312 | tf_op jit(solution)/shard_map/ppermute | solution.py:379
  58.2 7.6 %collective-permute-done.13.bottom_ref = bf16[4,2,8,256]{3,2,1,0:T(8,128)(2,1)S(1)} collective-permute-done((bf16[4,2,8,256]{3,2,1,0:T(8,128)(2,1)S(1)}, bf16[4,2,8,256]{3,2,1,0:T(8,128)(2,1)S(1)}, u32[]{:S(2)}, u32[]{:S(2)}) %collective-permute-start.13) | collective-permute-done | bytes 32800 | tf_op jit(solution)/shard_map/ppermute | solution.py:379
  65.8 0.9 grad_cost.1.grad_ref
  67.2 6.1 %collective-permute-done.1 = f32[2,256,128]{2,1,0:T(8,128)S(1)} collective-permute-done((f32[2,256,128]{2,1,0:T(8,128)S(1)}, f32[2,256,128]{2,1,0:T(8,128)S(1)}, u32[]{:S(2)}, u32[]{:S(2)}) %collective-permute-start.1) | collective-permute-done | bytes 262176 | tf_op jit(solution)/shard_map/ppermute | solution.py:364
  73.3 1.9 %collective-permute-start.5 = (bf16[1,256,128]{2,1,0:T(8,128)(2,1)S(1)}, bf16[1,256,128]{2,1,0:T(8,128)(2,1)S(1)}, u32[]{:S(2)}, u32[]{:S(2)}) collective-permute-start(bf16[1,256,128]{2,1,0:T(8,128)(2,1)S(1)} %get-tuple-element.22), channel_id=1, source_target_pairs={{32,0},{64,32},{96,64},{33,1},{65,33},{97,65},{34,2},{66,34},{98,6... | collective-permute-start | bytes 196616 | tf_op jit(solution)/shard_map/ppermute | solution.py:404
  75.3 16.0 %land.1 = bf16[256,1920]{1,0:T(8,128)(2,1)} custom-call(s32[2560]{0:T(1024)S(1)} %reshape.42.place_ref, s32[8]{0:T(128)S(1)} %fusion.6.order_ref, bf16[5,8,256,128]{3,2,1,0:T(8,128)(2,1)S(1)} %copy-done.1, bf16[5,8,4,64,64]{4,3,2,1,0:T(8,128)(2,1)} %interp_ref.3, bf16[4,256,128]{2,1,0:T(8,128)(2,1)S(1)} %collective-permute-done.8.mean_o, ...), custom_call_target="tpu_custom_call" | custom-call | tf_op jit(solution)/shard_map/land/pallas_call | solution.py:233
  91.3 8.9 %all-to-all-start.1 = ((bf16[32,8,1920]{2,1,0:T(8,128)(2,1)}), bf16[32,8,1920]{2,1,0:T(8,128)(2,1)S(1)}, u32[]{:S(2)}, u32[]{:S(2)}) async-start(bf16[32,8,1920]{2,1,0:T(8,128)(2,1)} %bitcast.11), calls=%async_computation.1 | async-start | bytes 1966080 | tf_op jit(solution)/shard_map/all_to_all | solution.py:399
  100.3 1.9 %collective-permute-start.4 = (bf16[1,256,128]{2,1,0:T(8,128)(2,1)S(1)}, bf16[1,256,128]{2,1,0:T(8,128)(2,1)S(1)}, u32[]{:S(2)}, u32[]{:S(2)}) collective-permute-start(bf16[1,256,128]{2,1,0:T(8,128)(2,1)S(1)} %get-tuple-element.23), channel_id=1, source_target_pairs={{0,32},{32,64},{64,96},{1,33},{33,65},{65,97},{2,34},{34,66},{66,9... | collective-permute-start | bytes 196616 | tf_op jit(solution)/shard_map/ppermute | solution.py:403
  102.2 10.2 %collective-permute-done.4.below_ref = bf16[1,256,128]{2,1,0:T(8,128)(2,1)S(1)} collective-permute-done((bf16[1,256,128]{2,1,0:T(8,128)(2,1)S(1)}, bf16[1,256,128]{2,1,0:T(8,128)(2,1)S(1)}, u32[]{:S(2)}, u32[]{:S(2)}) %collective-permute-start.4) | collective-permute-done | bytes 65568 | tf_op jit(solution)/shard_map/ppermute | solution.py:403
  112.5 1.9 %collective-permute-start.6 = (bf16[4,64,128]{2,1,0:T(8,128)(2,1)S(1)}, bf16[4,64,128]{2,1,0:T(8,128)(2,1)S(1)}, u32[]{:S(2)}, u32[]{:S(2)}) collective-permute-start(bf16[4,64,128]{2,1,0:T(8,128)(2,1)S(1)} %pad_maximum_fusion.1), channel_id=1, source_target_pairs={{0,1},{1,2},{2,3},{3,4},{4,5},{5,6},{6,7},{7,8},{8,9},{9,10},{10,1... | collective-permute-start | bytes 196616 | tf_op jit(solution)/shard_map/ppermute | solution.py:407
  114.4 3.9 %collective-permute-start.7 = (bf16[4,64,128]{2,1,0:T(8,128)(2,1)S(1)}, bf16[4,64,128]{2,1,0:T(8,128)(2,1)S(1)}, u32[]{:S(2)}, u32[]{:S(2)}) collective-permute-start(bf16[4,64,128]{2,1,0:T(8,128)(2,1)S(1)} %pad_maximum_fusion.2), channel_id=1, source_target_pairs={{1,0},{2,1},{3,2},{4,3},{5,4},{6,5},{7,6},{8,7},{9,8},{10,9},{11,1... | collective-permute-start | bytes 196616 | tf_op jit(solution)/shard_map/ppermute | solution.py:408
  118.6 6.5 %collective-permute-done.7.bottom_ref = bf16[4,64,128]{2,1,0:T(8,128)(2,1)S(1)} collective-permute-done((bf16[4,64,128]{2,1,0:T(8,128)(2,1)S(1)}, bf16[4,64,128]{2,1,0:T(8,128)(2,1)S(1)}, u32[]{:S(2)}, u32[]{:S(2)}) %collective-permute-start.7) | collective-permute-done | bytes 65568 | tf_op jit(solution)/shard_map/ppermute | solution.py:408
  125.1 1.5 %conv.1 = bf16[2,8,1024]{2,1,0:T(8,128)(2,1)} custom-call(bf16[1,256,128]{2,1,0:T(8,128)(2,1)S(1)} %collective-permute-done.4.below_ref, bf16[2,256,128]{2,1,0:T(8,128)(2,1)S(1)} %fusion.3.own_ref, bf16[1,256,128]{2,1,0:T(8,128)(2,1)S(1)} %collective-permute-done.5.above_ref, bf16[4,64,128]{2,1,0:T(8,128)(2,1)S(1)} %collective-permute-done.6.top_ref, ...), custom_call_target="tpu_custom_call" | custom-call | tf_op jit(solution)/shard_map/conv/pallas_call | solution.py:338
  126.6 1.5 %unstrips.1 = f32[1280,128]{1,0:T(8,128)} custom-call(bf16[256,1920]{1,0:T(8,128)(2,1)S(1)} %bitcast.19), custom_call_target="tpu_custom_call" | custom-call | tf_op jit(solution)/shard_map/unstrips/pallas_call | solution.py:96
  (57 shorter events, 4.1 us)
Async XLA Ops:
  0.6 1.0 copy-start.2
  1.6 12.7 %copy-start.4 = (s32[5,8,16,4]{2,3,1,0:T(4,128)S(1)}, s32[5,8,16,4]{2,3,1,0:T(4,128)}, u32[]{:S(2)}) copy-start(s32[5,8,16,4]{2,3,1,0:T(4,128)} %param.11) | copy-start | bytes 30724
  1.6 12.7 %copy-start.5 = (s32[5,8,16,4]{2,3,1,0:T(4,128)S(1)}, s32[5,8,16,4]{2,3,1,0:T(4,128)}, u32[]{:S(2)}) copy-start(s32[5,8,16,4]{2,3,1,0:T(4,128)} %param.10) | copy-start | bytes 30724
  3.5 24.8 %all-to-all-start = ((bf16[32,8,1920]{2,1,0:T(8,128)(2,1)}), bf16[32,8,1920]{2,1,0:T(8,128)(2,1)S(1)}, u32[]{:S(2)}, u32[]{:S(2)}) async-start(bf16[32,8,1920]{2,1,0:T(8,128)(2,1)} %bitcast.1), calls=%async_computation | async-start | bytes 1966080 | tf_op jit(solution)/shard_map/all_to_all | solution.py:374
  14.3 30.3 %copy-start.7 = (bf16[2,8,1024]{2,1,0:T(8,128)(2,1)S(1)}, bf16[2,8,1024]{2,1,0:T(8,128)(2,1)}, u32[]{:S(2)}) copy-start(bf16[2,8,1024]{2,1,0:T(8,128)(2,1)} %param.13) | copy-start | bytes 98308
  28.3 29.1 %copy-start.6 = (bf16[32,1024]{1,0:T(8,128)(2,1)S(1)}, bf16[32,1024]{1,0:T(8,128)(2,1)}, u32[]{:S(2)}) copy-start(bf16[32,1024]{1,0:T(8,128)(2,1)} %param.8) | copy-start | bytes 196612
  43.0 1.5 %copy-start = (bf16[5,8,256,128]{3,2,1,0:T(8,128)(2,1)}, bf16[5,8,256,128]{3,2,1,0:T(8,128)(2,1)S(1)}, u32[]{:S(2)}) copy-start(bf16[5,8,256,128]{3,2,1,0:T(8,128)(2,1)S(1)} %get-tuple-element.11.warped_ref) | copy-start | bytes 7864324
  44.5 13.4 %copy-start.3 = (bf16[3,3,3,8,32]{4,3,2,1,0:T(8,128)(2,1)S(1)}, bf16[3,3,3,8,32]{4,3,2,1,0:T(8,128)(2,1)}, u32[]{:S(2)}) copy-start(bf16[3,3,3,8,32]{4,3,2,1,0:T(8,128)(2,1)} %param.12) | copy-start | bytes 41476
  44.5 2.7 %collective-permute-start.2 = (f32[4,256,128]{2,1,0:T(8,128)S(1)}, f32[4,256,128]{2,1,0:T(8,128)S(1)}, u32[]{:S(2)}, u32[]{:S(2)}) collective-permute-start(f32[4,256,128]{2,1,0:T(8,128)S(1)} %get-tuple-element.10), channel_id=1, source_target_pairs={{0,32},{32,0},{64,96},{96,64},{1,33},{33,1},{65,97},{97,65},{2,34}... | collective-permute-start | bytes 1572872 | tf_op jit(solution)/shard_map/ppermute | solution.py:364
  44.6 4.2 %collective-permute-start.11 = (bf16[2,8,1024]{2,1,0:T(8,128)(2,1)S(1)}, bf16[2,8,1024]{2,1,0:T(8,128)(2,1)S(1)}, u32[]{:S(2)}, u32[]{:S(2)}) collective-permute-start(bf16[2,8,1024]{2,1,0:T(8,128)(2,1)S(1)} %copy-done.7), channel_id=1, source_target_pairs={{0,96},{32,64},{64,32},{96,0},{1,97},{33,65},{65,33},{97,1},{2,98}... | collective-permute-start | bytes 98312 | tf_op jit(solution)/shard_map/ppermute | solution.py:364
  45.5 3.9 %collective-permute-start.10 = (bf16[2,8,1024]{2,1,0:T(8,128)(2,1)S(1)}, bf16[2,8,1024]{2,1,0:T(8,128)(2,1)S(1)}, u32[]{:S(2)}, u32[]{:S(2)}) collective-permute-start(bf16[2,8,1024]{2,1,0:T(8,128)(2,1)S(1)} %copy-done.7), channel_id=1, source_target_pairs={{0,64},{32,96},{64,0},{96,32},{1,65},{33,97},{65,1},{97,33},{2,66}... | collective-permute-start | bytes 98312 | tf_op jit(solution)/shard_map/ppermute | solution.py:364
  46.7 2.7 %collective-permute-start.9 = (bf16[2,8,1024]{2,1,0:T(8,128)(2,1)S(1)}, bf16[2,8,1024]{2,1,0:T(8,128)(2,1)S(1)}, u32[]{:S(2)}, u32[]{:S(2)}) collective-permute-start(bf16[2,8,1024]{2,1,0:T(8,128)(2,1)S(1)} %copy-done.7), channel_id=1, source_target_pairs={{0,32},{32,0},{64,96},{96,64},{1,33},{33,1},{65,97},{97,65},{2,34}... | collective-permute-start | bytes 98312 | tf_op jit(solution)/shard_map/ppermute | solution.py:364
  46.7 20.0 %collective-permute-start = (f32[4,256,128]{2,1,0:T(8,128)S(1)}, f32[4,256,128]{2,1,0:T(8,128)S(1)}, u32[]{:S(2)}, u32[]{:S(2)}) collective-permute-start(f32[4,256,128]{2,1,0:T(8,128)S(1)} %get-tuple-element.8), channel_id=1, source_target_pairs={{0,32},{32,0},{64,96},{96,64},{1,33},{33,1},{65,97},{97,65},{2,34}... | collective-permute-start | bytes 1572872 | tf_op jit(solution)/shard_map/ppermute | solution.py:364
  48.0 19.0 %collective-permute-start.3 = (bf16[4,256,128]{2,1,0:T(8,128)(2,1)}, bf16[4,256,128]{2,1,0:T(8,128)(2,1)S(1)}, u32[]{:S(2)}, u32[]{:S(2)}) collective-permute-start(bf16[4,256,128]{2,1,0:T(8,128)(2,1)} %get-tuple-element.14), channel_id=1, source_target_pairs={{0,64},{32,96},{64,0},{96,32},{1,65},{33,97},{65,1},{97,33},{2,66}... | collective-permute-start | bytes 786440 | tf_op jit(solution)/shard_map/ppermute | solution.py:364
  49.4 8.8 %collective-permute-start.12 = (bf16[4,2,8,256]{3,2,1,0:T(8,128)(2,1)S(1)}, bf16[4,2,8,256]{3,2,1,0:T(8,128)(2,1)S(1)}, u32[]{:S(2)}, u32[]{:S(2)}) collective-permute-start(bf16[4,2,8,256]{3,2,1,0:T(8,128)(2,1)S(1)} %get-tuple-element.19), channel_id=1, source_target_pairs={{0,1},{1,2},{2,3},{3,4},{4,5},{5,6},{6,7},{7,8},{8,9},{9,10},{10,1... | collective-permute-start | bytes 98312 | tf_op jit(solution)/shard_map/ppermute | solution.py:378
  55.5 10.3 %collective-permute-start.13 = (bf16[4,2,8,256]{3,2,1,0:T(8,128)(2,1)S(1)}, bf16[4,2,8,256]{3,2,1,0:T(8,128)(2,1)S(1)}, u32[]{:S(2)}, u32[]{:S(2)}) collective-permute-start(bf16[4,2,8,256]{3,2,1,0:T(8,128)(2,1)S(1)} %get-tuple-element.18), channel_id=1, source_target_pairs={{1,0},{2,1},{3,2},{4,3},{5,4},{6,5},{7,6},{8,7},{9,8},{10,9},{11,1... | collective-permute-start | bytes 98312 | tf_op jit(solution)/shard_map/ppermute | solution.py:379
  66.8 8.5 %copy-start.1 = (bf16[5,8,256,128]{3,2,1,0:T(8,128)(2,1)S(1)}, bf16[5,8,256,128]{3,2,1,0:T(8,128)(2,1)}, u32[]{:S(2)}) copy-start(bf16[5,8,256,128]{3,2,1,0:T(8,128)(2,1)} %copy-done) | copy-start | bytes 7864324
  66.8 6.5 %collective-permute-start.1 = (f32[2,256,128]{2,1,0:T(8,128)S(1)}, f32[2,256,128]{2,1,0:T(8,128)S(1)}, u32[]{:S(2)}, u32[]{:S(2)}) collective-permute-start(f32[2,256,128]{2,1,0:T(8,128)S(1)} %slice.62), channel_id=1, source_target_pairs={{0,64},{32,96},{64,0},{96,32},{1,65},{33,97},{65,1},{97,33},{2,66}... | collective-permute-start | bytes 786440 | tf_op jit(solution)/shard_map/ppermute | solution.py:364
  67.1 8.2 %collective-permute-start.8 = (bf16[4,256,128]{2,1,0:T(8,128)(2,1)S(1)}, bf16[4,256,128]{2,1,0:T(8,128)(2,1)S(1)}, u32[]{:S(2)}, u32[]{:S(2)}) collective-permute-start(bf16[4,256,128]{2,1,0:T(8,128)(2,1)S(1)} %get-tuple-element.12.mean_m), channel_id=1, source_target_pairs={{0,32},{32,0},{64,96},{96,64},{1,33},{33,1},{65,97},{97,65},{2,34}... | collective-permute-start | bytes 786440 | tf_op jit(solution)/shard_map/ppermute | solution.py:364
  73.3 28.9 %collective-permute-start.5 = (bf16[1,256,128]{2,1,0:T(8,128)(2,1)S(1)}, bf16[1,256,128]{2,1,0:T(8,128)(2,1)S(1)}, u32[]{:S(2)}, u32[]{:S(2)}) collective-permute-start(bf16[1,256,128]{2,1,0:T(8,128)(2,1)S(1)} %get-tuple-element.22), channel_id=1, source_target_pairs={{32,0},{64,32},{96,64},{33,1},{65,33},{97,65},{34,2},{66,34},{98,6... | collective-permute-start | bytes 196616 | tf_op jit(solution)/shard_map/ppermute | solution.py:404
  91.3 35.2 %all-to-all-start.1 = ((bf16[32,8,1920]{2,1,0:T(8,128)(2,1)}), bf16[32,8,1920]{2,1,0:T(8,128)(2,1)S(1)}, u32[]{:S(2)}, u32[]{:S(2)}) async-start(bf16[32,8,1920]{2,1,0:T(8,128)(2,1)} %bitcast.11), calls=%async_computation.1 | async-start | bytes 1966080 | tf_op jit(solution)/shard_map/all_to_all | solution.py:399
  100.3 12.2 %collective-permute-start.4 = (bf16[1,256,128]{2,1,0:T(8,128)(2,1)S(1)}, bf16[1,256,128]{2,1,0:T(8,128)(2,1)S(1)}, u32[]{:S(2)}, u32[]{:S(2)}) collective-permute-start(bf16[1,256,128]{2,1,0:T(8,128)(2,1)S(1)} %get-tuple-element.23), channel_id=1, source_target_pairs={{0,32},{32,64},{64,96},{1,33},{33,65},{65,97},{2,34},{34,66},{66,9... | collective-permute-start | bytes 196616 | tf_op jit(solution)/shard_map/ppermute | solution.py:403
  112.5 6.2 %collective-permute-start.6 = (bf16[4,64,128]{2,1,0:T(8,128)(2,1)S(1)}, bf16[4,64,128]{2,1,0:T(8,128)(2,1)S(1)}, u32[]{:S(2)}, u32[]{:S(2)}) collective-permute-start(bf16[4,64,128]{2,1,0:T(8,128)(2,1)S(1)} %pad_maximum_fusion.1), channel_id=1, source_target_pairs={{0,1},{1,2},{2,3},{3,4},{4,5},{5,6},{6,7},{7,8},{8,9},{9,10},{10,1... | collective-permute-start | bytes 196616 | tf_op jit(solution)/shard_map/ppermute | solution.py:407
  114.4 10.7 %collective-permute-start.7 = (bf16[4,64,128]{2,1,0:T(8,128)(2,1)S(1)}, bf16[4,64,128]{2,1,0:T(8,128)(2,1)S(1)}, u32[]{:S(2)}, u32[]{:S(2)}) collective-permute-start(bf16[4,64,128]{2,1,0:T(8,128)(2,1)S(1)} %pad_maximum_fusion.2), channel_id=1, source_target_pairs={{1,0},{2,1},{3,2},{4,3},{5,4},{6,5},{7,6},{8,7},{9,8},{10,9},{11,1... | collective-permute-start | bytes 196616 | tf_op jit(solution)/shard_map/ppermute | solution.py:408

commit v2 on v1

--- a/solution.py
+++ b/solution.py
@@ -13,7 +13,7 @@
 PLANES = 8
 COUNT = 21.0
 SEGS = 48
-VMEM_LIMIT = 48 * 1024 * 1024
+VMEM_LIMIT = 4 * 1024 * 1024
 NT = (((1,), (1,)), ((), ()))
 NN = (((1,), (0,)), ((), ()))
 TN = (((0,), (0,)), ((), ()))
@@ -25,6 +25,12 @@
 
 def whole():
     return pl.BlockSpec(memory_space=pltpu.VMEM)
+
+
+def cost_us(microseconds):
+    return pl.CostEstimate(
+        flops=int(microseconds * 1.0e9), bytes_accessed=int(microseconds * 3.0e6), transcendentals=0
+    )
 
 
 def iota(shape, dim):
@@ -124,131 +130,299 @@
     return first, second
 
 
-def warp_kernel(
-    place_ref, order_ref, in_ref, interp_ref, first_o, first_m, second_o, second_m, warped_ref, blocks
-):
-    view = pl.program_id(0)
-    turned = in_ref[...].astype(F32).T
-    for band_row in range(12):
-        upper = turned[band_row * 32 : band_row * 32 + 16]
-        lower = turned[band_row * 32 + 16 : band_row * 32 + 32]
-        for half in range(2):
-            even, odd = pair_swap(
-                upper[:, half * 128 : half * 128 + 128], lower[:, half * 128 : half * 128 + 128]
-            )
-            blocks[band_row * 4 + half * 2] = even.astype(BF)
-            blocks[band_row * 4 + half * 2 + 1] = odd.astype(BF)
-
-    @pl.when(view == 0)
-    def _():
-        for ref in (first_o, first_m, second_o, second_m):
-            ref[...] = jnp.zeros_like(ref)
-
-    for group, (first_ref, second_ref) in enumerate(((first_o, second_o), (first_m, second_m))):
-
-        def step(e, unused, group=group, first_ref=first_ref, second_ref=second_ref):
+def turn_kernel(in_ref, blocks_ref):
+    for view in range(VIEWS):
+        turned = in_ref[:, view * 384 : (view + 1) * 384].astype(F32).T
+        for band_row in range(12):
+            upper = turned[band_row * 32 : band_row * 32 + 16]
+            lower = turned[band_row * 32 + 16 : band_row * 32 + 32]
+            for half in range(2):
+                even, odd = pair_swap(
+                    upper[:, half * 128 : half * 128 + 128], lower[:, half * 128 : half * 128 + 128]
+                )
+                at = view * SEGS + band_row * 4 + half * 2
+                blocks_ref[at] = even.astype(BF)
+                blocks_ref[at + 1] = odd.astype(BF)
+
+
+def warp_planes(group, place_ref, order_ref, blocks_ref, interp_ref, first_ref, second_ref, warped_ref):
+    first_ref[...] = jnp.zeros_like(first_ref)
+    second_ref[...] = jnp.zeros_like(second_ref)
+
+    def step(view, unused):
+        for e in range(4):
             plane = order_ref[group * 4 + e]
             base = (view * PLANES + plane) * 64
             rows = []
             for g in range(16):
-                taps = [blocks[place_ref[base + g * 4 + k]] for k in range(4)]
+                taps = [blocks_ref[view * SEGS + place_ref[base + g * 4 + k]] for k in range(4)]
                 rows.append(jnp.concatenate(taps, axis=1))
             picked = jnp.concatenate(rows, axis=0)
-            matrix = spread_interp(interp_ref[0, plane])
+            matrix = spread_interp(interp_ref[view, plane])
             warped = lax.dot_general(picked, matrix, NN, preferred_element_type=F32)
             first_ref[e] += warped
             second_ref[e] += warped * warped
-            warped_ref[0, group * 4 + e] = warped.astype(BF)
-            return unused
-
-        lax.fori_loop(0, 4, step, 0)
-
-
-def warp(place, order, arrived, interp):
-    sums = jax.ShapeDtypeStruct((4, 256, 128), F32)
-    sum_spec = pl.BlockSpec((4, 256, 128), lambda v, p, o: (0, 0, 0))
-    return pl.pallas_call(
-        warp_kernel,
-        grid_spec=pltpu.PrefetchScalarGridSpec(
-            num_scalar_prefetch=2,
-            grid=(VIEWS,),
-            in_specs=[
-                pl.BlockSpec((256, 384), lambda v, p, o: (0, v)),
-                pl.BlockSpec((1, PLANES, 4, 64, 64), lambda v, p, o: (v, 0, 0, 0, 0)),
-            ],
-            out_specs=[sum_spec] * 4
-            + [pl.BlockSpec((1, PLANES, 256, 128), lambda v, p, o: (v, 0, 0, 0))],
-            scratch_shapes=[pltpu.VMEM((SEGS, 16, 128), BF)],
-        ),
-        out_shape=[sums] * 4 + [jax.ShapeDtypeStruct((VIEWS, PLANES, 256, 128), BF)],
-        compiler_params=params(),
-        name="warp",
+            warped_ref[view, e] = warped.astype(BF)
+        return unused
+
+    lax.fori_loop(0, VIEWS, step, 0, unroll=UNROLL)
+
+
+def warp_other_kernel(
+    place_ref, order_ref, in_ref, interp_ref, blocks_ref, first_ref, second_ref, warped_ref
+):
+    turn_kernel(in_ref, blocks_ref)
+    warp_planes(0, place_ref, order_ref, blocks_ref, interp_ref, first_ref, second_ref, warped_ref)
+
+
+def warp_mine_kernel(
+    place_ref, order_ref, blocks_ref, interp_ref, first_ref, second_ref, warped_ref
+):
+    warp_planes(1, place_ref, order_ref, blocks_ref, interp_ref, first_ref, second_ref, warped_ref)
+
+
+UNROLL = 5
+SUMS = jax.ShapeDtypeStruct((4, 256, 128), F32)
+WARPED = jax.ShapeDtypeStruct((VIEWS, 4, 256, 128), BF)
+BLOCKS = jax.ShapeDtypeStruct((VIEWS * SEGS, 16, 128), BF)
+
+
+def smem():
+    return pl.BlockSpec(memory_space=pltpu.SMEM)
+
+
+def warp_other(place, order, arrived, interp):
+    return pl.pallas_call(
+        warp_other_kernel,
+        in_specs=[smem(), smem(), whole(), whole()],
+        out_specs=[whole()] * 4,
+        out_shape=[BLOCKS, SUMS, SUMS, WARPED],
+        compiler_params=params(),
+        name="warp_other",
     )(place, order, arrived, interp)
 
 
+def warp_mine(place, order, blocks, interp):
+    return pl.pallas_call(
+        warp_mine_kernel,
+        in_specs=[smem(), smem(), whole(), whole()],
+        out_specs=[whole()] * 3,
+        out_shape=[SUMS, SUMS, WARPED],
+        compiler_params=params(),
+        name="warp_mine",
+    )(place, order, blocks, interp)
+
+
 CHAINS = 4
 
 
-def land_kernel(
-    place_ref, order_ref, warped_ref, interp_ref, mean_o, mean_m, grad_ref, out_ref, *accs
+def land_views(
+    views, place_ref, order_ref, warped_o, warped_m, interp_ref, mean_o, mean_m, grad_ref, out_ref, accs
 ):
-    view = pl.program_id(0)
-    for acc in accs:
-        acc[...] = jnp.zeros_like(acc)
-
-    for group, mean_ref in enumerate((mean_o, mean_m)):
-
-        def step(e, unused, group=group, mean_ref=mean_ref):
-            plane = order_ref[group * 4 + e]
+    groups = ((warped_o, mean_o), (warped_m, mean_m))
+    for view in views:
+        for acc in accs:
+            acc[...] = jnp.zeros_like(acc)
+        for e in range(8):
+            warped_ref, mean_ref = groups[e // 4]
+            plane = order_ref[e]
             base = (view * PLANES + plane) * 64
-            warped = warped_ref[0, group * 4 + e].astype(F32)
-            grad = (grad_ref[plane] * (warped - mean_ref[e].astype(F32))).astype(BF)
-            matrix = spread_interp(interp_ref[0, plane])
+            warped = warped_ref[view, e % 4].astype(F32)
+            grad = (grad_ref[plane] * (warped - mean_ref[e % 4].astype(F32))).astype(BF)
+            matrix = spread_interp(interp_ref[view, plane])
             spread = lax.dot_general(grad, matrix, NT, preferred_element_type=F32)
             for g in range(16):
                 for k in range(4):
                     where = place_ref[base + g * 4 + k]
                     accs[k][where] += spread[g * 16 : (g + 1) * 16, k * 128 : (k + 1) * 128]
-            return unused
-
-        lax.fori_loop(0, 4, step, 0)
-
-    bands = []
-    for band_row in range(12):
-        columns_up, columns_low = [], []
-        for half in range(2):
-            at = band_row * 4 + half * 2
-            even = (accs[0][at] + accs[1][at]) + (accs[2][at] + accs[3][at])
-            odd = (accs[0][at + 1] + accs[1][at + 1]) + (accs[2][at + 1] + accs[3][at + 1])
-            up, low = pair_swap(even, odd)
-            columns_up.append(up)
-            columns_low.append(low)
-        bands.append(jnp.concatenate(columns_up, axis=1))
-        bands.append(jnp.concatenate(columns_low, axis=1))
-    out_ref[...] = jnp.concatenate(bands, axis=0).T.astype(BF)
-
-
-def land(place, order, warped, interp, mean_other, mean_mine, grad):
-    mean_spec = pl.BlockSpec((4, 256, 128), lambda v, p, o: (0, 0, 0))
-    return pl.pallas_call(
-        land_kernel,
-        grid_spec=pltpu.PrefetchScalarGridSpec(
-            num_scalar_prefetch=2,
-            grid=(VIEWS,),
-            in_specs=[
-                pl.BlockSpec((1, PLANES, 256, 128), lambda v, p, o: (v, 0, 0, 0)),
-                pl.BlockSpec((1, PLANES, 4, 64, 64), lambda v, p, o: (v, 0, 0, 0, 0)),
-                mean_spec,
-                mean_spec,
-                pl.BlockSpec((PLANES, 256, 128), lambda v, p, o: (0, 0, 0)),
-            ],
-            out_specs=pl.BlockSpec((256, 384), lambda v, p, o: (0, v)),
-            scratch_shapes=[pltpu.VMEM((SEGS, 16, 128), F32)] * CHAINS,
-        ),
-        out_shape=jax.ShapeDtypeStruct((256, VIEWS * 384), BF),
-        compiler_params=params(),
+        bands = []
+        for band_row in range(12):
+            columns_up, columns_low = [], []
+            for half in range(2):
+                at = band_row * 4 + half * 2
+                even = (accs[0][at] + accs[1][at]) + (accs[2][at] + accs[3][at])
+                odd = (accs[0][at + 1] + accs[1][at + 1]) + (accs[2][at + 1] + accs[3][at + 1])
+                up, low = pair_swap(even, odd)
+                columns_up.append(up)
+                columns_low.append(low)
+            bands.append(jnp.concatenate(columns_up, axis=1))
+            bands.append(jnp.concatenate(columns_low, axis=1))
+        out_ref[:, view * 384 : (view + 1) * 384] = jnp.concatenate(bands, axis=0).T.astype(BF)
+
+
+def land_first_kernel(views, *refs):
+    land_views(views, *refs[:9], refs[9:])
+
+
+def land_next_kernel(views, *refs):
+    land_views(views, *refs[:8], refs[9], refs[10:])
+
+
+LANDED = jax.ShapeDtypeStruct((256, VIEWS * 384), BF)
+
+
+def land(views, place, order, warped_o, warped_m, interp, mean_o, mean_m, grad, earlier=None):
+    operands = [place, order, warped_o, warped_m, interp, mean_o, mean_m, grad]
+    specs = [smem(), smem()] + [whole()] * 6
+    if earlier is None:
+        kernel, aliases = land_first_kernel, {}
+    else:
+        kernel, aliases = land_next_kernel, {8: 0}
+        operands.append(earlier)
+        specs.append(whole())
+    return pl.pallas_call(
+        functools.partial(kernel, views),
+        in_specs=specs,
+        out_specs=whole(),
+        out_shape=LANDED,
+        scratch_shapes=[pltpu.VMEM((SEGS, 16, 128), F32)] * CHAINS,
+        input_output_aliases=aliases,
+        compiler_params=params(),
+        cost_estimate=cost_us(1.4 * len(views)),
         name="land",
-    )(place, order, warped, interp, mean_other, mean_mine, grad)
+    )(*operands)
+
+
+def chip_first_kernel(mine_ref, arrived_ref, sum_ref, send_ref):
+    total = mine_ref[...] + arrived_ref[...]
+    sum_ref[...] = total
+    send_ref[...] = total.astype(BF)
+
+
+def chip_second_kernel(where_ref, mine_ref, arrived_ref, own_ref, send_ref):
+    core = where_ref[1]
+    own_ref[0:2] = mine_ref[2:4] + arrived_ref[2:4]
+    own_ref[2] = mine_ref[core] + arrived_ref[core]
+    send_ref[0:2] = mine_ref[0:2] + arrived_ref[0:2]
+    send_ref[2] = mine_ref[2 + core] + arrived_ref[2 + core]
+
+
+def chip_first(mine, arrived):
+    return pl.pallas_call(
+        chip_first_kernel,
+        in_specs=[whole()] * 2,
+        out_specs=[whole()] * 2,
+        out_shape=[SUMS, jax.ShapeDtypeStruct(SUMS.shape, BF)],
+        compiler_params=params(),
+        name="chip_first",
+    )(mine, arrived)
+
+
+def chip_second(where, mine, arrived):
+    return pl.pallas_call(
+        chip_second_kernel,
+        in_specs=[smem()] + [whole()] * 2,
+        out_specs=[whole()] * 2,
+        out_shape=[jax.ShapeDtypeStruct((3, 256, 128), F32)] * 2,
+        compiler_params=params(),
+        name="chip_second",
+    )(where, mine, arrived)
+
+
+def turned_reference(ref_ref, pair):
+    lanes = slice(pair * 128, pair * 128 + 128)
+    even, odd = pair_swap(ref_ref[0:16, lanes].astype(F32), ref_ref[16:32, lanes].astype(F32))
+    return jnp.concatenate([even, odd], axis=0)
+
+
+def mean_kernel(sum_ref, there_ref, ref_ref, mean_ref):
+    for pair in range(8):
+        rows = slice(pair * 32, pair * 32 + 32)
+        ref = turned_reference(ref_ref, pair)
+        for e in range(4):
+            total = sum_ref[e, rows] + there_ref[e ^ 2, rows].astype(F32) + ref
+            mean_ref[e, rows] = (total * (1.0 / COUNT)).astype(BF)
+
+
+def mean_of(sums, there, reference):
+    return pl.pallas_call(
+        mean_kernel,
+        in_specs=[whole()] * 3,
+        out_specs=whole(),
+        out_shape=jax.ShapeDtypeStruct(SUMS.shape, BF),
+        compiler_params=params(),
+        name="mean",
+    )(sums, there, reference)
+
+
+def cost_kernel(
+    where_ref, first_ref, first_there, second_ref, second_there, ref_ref, low_ref, high_ref, send_ref
+):
+    y_low, core = where_ref[0], where_ref[1]
+    inside = jnp.where(y_low == core, 1.0, 0.0)
+    for pair in range(8):
+        rows = slice(pair * 32, pair * 32 + 32)
+        ref = turned_reference(ref_ref, pair)
+        square = ref * ref
+
+        def plane_cost(mine, there, slot):
+            first = first_ref[mine, rows] + first_there[there, rows].astype(F32) + ref
+            second = second_ref[slot, rows] + second_there[slot, rows] + square
+            mean = first * (1.0 / COUNT)
+            return second * (1.0 / COUNT) - mean * mean
+
+        low = plane_cost(2, 0, 0)
+        high = plane_cost(3, 1, 1)
+        far = plane_cost(core, 2 + core, 2)
+        low_ref[0, rows] = low.astype(BF)
+        high_ref[0, rows] = high.astype(BF)
+        send_ref[0, rows] = jnp.where(core == 1, low, high).astype(BF)
+        send_ref[1, rows] = (far * inside).astype(BF)
+
+
+def edges_kernel(where_ref, low_ref, high_ref, near_ref, outer_ref, last_ref, initial_ref):
+    core = where_ref[1]
+    outer_ref[0] = near_ref[1 - core]
+    outer_ref[1] = near_ref[core]
+    for local, plane in ((0, outer_ref[0]), (1, low_ref[0]), (2, high_ref[0]), (3, outer_ref[1])):
+        last_ref[local] = plane[192:256]
+        initial_ref[local] = plane[0:64]
+
+
+PLANE = jax.ShapeDtypeStruct((1, 256, 128), BF)
+PAIR = jax.ShapeDtypeStruct((2, 256, 128), BF)
+EDGES = jax.ShapeDtypeStruct((4, 64, 128), BF)
+
+
+def cost_of(where, first, first_there, second, second_there, reference):
+    return pl.pallas_call(
+        cost_kernel,
+        in_specs=[smem()] + [whole()] * 5,
+        out_specs=[whole()] * 3,
+        out_shape=[PLANE, PLANE, PAIR],
+        compiler_params=params(),
+        name="cost",
+    )(where, first, first_there, second, second_there, reference)
+
+
+def edges_of(where, low, high, near):
+    return pl.pallas_call(
+        edges_kernel,
+        in_specs=[smem()] + [whole()] * 3,
+        out_specs=[whole()] * 3,
+        out_shape=[PAIR, EDGES, EDGES],
+        compiler_params=params(),
+        name="edges",
+    )(where, low, high, near)
+
+
+def slots_kernel(*refs):
+    for slot in range(4):
+        refs[4][slot] = refs[slot][...]
+        refs[5][slot] = refs[slot][:, :, 768:1024]
+        refs[6][slot] = refs[slot][:, :, 0:256]
+
+
+def slots_of(parts):
+    row = jax.ShapeDtypeStruct((4, 2, 8, 256), BF)
+    return pl.pallas_call(
+        slots_kernel,
+        in_specs=[whole()] * 4,
+        out_specs=[whole()] * 3,
+        out_shape=[jax.ShapeDtypeStruct((4, 2, 8, 1024), BF), row, row],
+        compiler_params=params(),
+        name="slots",
+    )(*parts)
 
 
 def shifted(values, offset):
@@ -301,16 +475,11 @@
     )(view, own, top, bottom, weight)
 
 
-def conv_kernel(below_ref, own_ref, above_ref, top_ref, bottom_ref, weight_ref, out_ref):
+def conv_kernel(outer_ref, low_ref, high_ref, top_ref, bottom_ref, weight_ref, out_ref):
     weight = weight_ref[...]
     results = []
     for local in range(4):
-        if local == 0:
-            middle = below_ref[0]
-        elif local == 3:
-            middle = above_ref[0]
-        else:
-            middle = own_ref[local - 1]
+        middle = (outer_ref, low_ref, high_ref, outer_ref)[local][1 if local == 3 else 0]
         tall = jnp.concatenate([top_ref[local], middle, bottom_ref[local]], axis=0).astype(F32)
         upper, lower = [], []
         for pair in range(12):
@@ -334,7 +503,7 @@
         out_ref[plane] = total.astype(BF)
 
 
-def conv(below, own, above, top, bottom, weight):
+def conv(outer, low, high, top, bottom, weight):
     return pl.pallas_call(
         conv_kernel,
         out_shape=jax.ShapeDtypeStruct((2, 8, 1024), BF),
@@ -342,7 +511,7 @@
         out_specs=whole(),
         compiler_params=params(),
         name="conv",
-    )(below, own, above, top, bottom, weight)
+    )(outer, low, high, top, bottom, weight)
 
 
 def body(
@@ -370,44 +539,45 @@
     ).astype(jnp.int32)
     place = ((source_tile + 1) * 16 + source_block).reshape(-1)
 
+    where = jnp.stack([y_low, core]).astype(jnp.int32)
+    own = grad_regularized
+    parts = (own, other(own, 1), other(own, 2), other(own, 3))
     operand = strips(source_features.reshape(1280, 128))
+    cotangent, last, initial = slots_of(parts)
+    operand, last, initial = lax.optimization_barrier((operand, last, initial))
     arrived = lax.all_to_all(operand, "tile", split_axis=0, concat_axis=0, tiled=True)
-
-    own = grad_regularized
-    cotangent = jnp.stack([own, other(own, 1), other(own, 2), other(own, 3)])
-    top = lax.ppermute(cotangent[..., 768:], "tile", up)
-    bottom = lax.ppermute(cotangent[..., :256], "tile", down)
+    top = lax.ppermute(last, "tile", up)
+    bottom = lax.ppermute(initial, "tile", down)
     back_weight = conv_weight.transpose(1, 4, 0, 2, 3).reshape(96, 72)
+    weight = conv_weight.transpose(0, 1, 3, 2, 4).reshape(72, 96)
     grad = grad_cost(view.astype(jnp.int32).reshape(1), cotangent, top, bottom, back_weight)
-
-    first_o, first_m, second_o, second_m, warped = warp(place, order, arrived, interp)
-    first_chip = first_m + other(first_o, 1)
-    second_chip = second_m + other(second_o, 1)
-    first_there = other(first_chip.astype(BF), 2).astype(F32)
-    second_there = other(second_chip[:2], 2)
-    ref = (
-        reference_features.astype(F32).reshape(2, 16, 16, 64).transpose(2, 1, 0, 3).reshape(256, 128)
+    arrived, grad, weight = lax.optimization_barrier((arrived, grad, weight))
+
+    blocks, first_o, second_o, warped_o = warp_other(place, order, arrived, interp)
+    first_m, second_m, warped_m = warp_mine(place, order, blocks, interp)
+    first_chip, first_send = chip_first(first_m, other(first_o, 1))
+    first_there = other(first_send, 2)
+    second_own, second_send = chip_second(where, second_m, other(second_o, 1))
+    second_there = other(second_send, 2)
+    first_there, second_own = lax.optimization_barrier((first_there, second_own))
+    mean_mine = mean_of(first_chip, first_there, reference_features)
+    mean_other = other(mean_mine, 1)
+
+    shared = (place, order, warped_o, warped_m, interp, mean_other, mean_mine, grad)
+    landed = land((0, 1, 2), *shared)
+    landed, second_there = lax.optimization_barrier((landed, second_there))
+    low, high, send = cost_of(
+        where, first_chip, first_there, second_own, second_there, reference_features
     )
-    first = first_chip + jnp.concatenate([first_there[2:], first_there[:2]], axis=0) + ref
-    mean = first / COUNT
-    mean_mine = mean.astype(BF)
-    mean_other = other(mean_mine, 1)
-    second = second_chip[2:] + second_there + ref * ref
-    cost = (second / COUNT - mean[2:] * mean[2:]).astype(BF)
-
-    landed = land(place, order, warped, interp, mean_other, mean_mine, grad)
+    near = other(send, 1)
+    landed = land((3, 4), *shared, landed)
+    landed, near = lax.optimization_barrier((landed, near))
+    outer, cost_last, cost_initial = edges_of(where, low, high, near)
+    landed, cost_last, cost_initial = lax.optimization_barrier((landed, cost_last, cost_initial))
     returned = lax.all_to_all(landed, "tile", split_axis=0, concat_axis=0, tiled=True)
-
-    view_up = [(i, i + 1) for i in range(views - 1)]
-    view_down = [(i + 1, i) for i in range(views - 1)]
-    below = lax.ppermute(cost[1:], "view", view_up)
-    above = lax.ppermute(cost[:1], "view", view_down)
-    last = jnp.concatenate([below[:, 192:], cost[:, 192:], above[:, 192:]], axis=0)
-    initial = jnp.concatenate([below[:, :64], cost[:, :64], above[:, :64]], axis=0)
-    cost_top = lax.ppermute(last, "tile", up)
-    cost_bottom = lax.ppermute(initial, "tile", down)
-    weight = conv_weight.transpose(0, 1, 3, 2, 4).reshape(72, 96)
-    regularized = conv(below, cost, above, cost_top, cost_bottom, weight)
+    cost_top = lax.ppermute(cost_last, "tile", up)
+    cost_bottom = lax.ppermute(cost_initial, "tile", down)
+    regularized = conv(outer, low, high, cost_top, cost_bottom, weight)
 
     grad_source = unstrips(returned).reshape(source_features.shape)
     return regularized, grad_source

time: 129 us -> 95.3 us (0.74)
  the two profiles are of different devices: /device:TPU:30 before, /device:TPU:32 now
where the time goes in v2:
time: 95.3 us; the launch traced here: 94.8 us
  starting transfers between devices  42.2 us (44%)
  waiting for transfers between devices  26.7 us (28%)
  Pallas kernels  21 us (22%)
  local copies, waits for them, and re-layouts  3.8 us (4%)
    ppermute x9, waiting for transfers between devices, other(): return lax.ppermute(array, 'view', [(i, i ^ mask) for i in range(views)])  13.9 us
    all_to_all x1, starting transfers between devices, body(): lax.all_to_all(operand, 'tile', split_axis=0, concat_axis=0, tiled=True)  10.6 us
    ppermute x1, waiting for transfers between devices, body(): cost_top = lax.ppermute(cost_last, 'tile', up)  7.5 us
    pallas_call x2, Pallas kernels, land(): pl.pallas_call(functools.partial(kernel, views), in_specs=specs, out_spec...  7.07 us
    ppermute x1, starting transfers between devices, body(): bottom = lax.ppermute(initial, 'tile', down)  6.98 us
    ppermute x1, starting transfers between devices, body(): cost_bottom = lax.ppermute(cost_initial, 'tile', down)  6.98 us
    all_to_all x1, starting transfers between devices, body(): lax.all_to_all(landed, 'tile', split_axis=0, concat_axis=0, tiled=True)  6.37 us
    ppermute x1, waiting for transfers between devices, body(): top = lax.ppermute(last, 'tile', up)  5.3 us
  transfers between devices with their start and end apart: 15, of which 6 were waited for; matrix products, arithmetic and copies ran while one was open for 1% of the time, Pallas kernels for 15%

profile of v2, /device:TPU:32, one launch (start us, length us, event | category | flops | bytes accessed | tf_op | source)
XLA Modules:
  0.0 94.8 jit_solution(4341596553336554156)
XLA Ops:
  0.7 1.7 %collective-permute-start.1 = (bf16[2,8,1024]{2,1,0:T(8,128)(2,1)}, bf16[2,8,1024]{2,1,0:T(8,128)(2,1)S(1)}, u32[]{:S(2)}, u32[]{:S(2)}) collective-permute-start(bf16[2,8,1024]{2,1,0:T(8,128)(2,1)} %refs_0_.1), channel_id=1, source_target_pairs={{0,64},{32,96},{64,0},{96,32},{1,65},{33,97},{65,1},{97,33},{2,66}... | collective-permute-start | bytes 98312 | tf_op jit(solution)/shard_map/ppermute | solution.py:533
  2.6 1.0 %copy-done.4 = bf16[5,32,8,128]{3,2,1,0:T(8,128)(2,1)S(1)} copy-done((bf16[5,32,8,128]{3,2,1,0:T(8,128)(2,1)S(1)}, bf16[5,32,8,128]{3,2,1,0:T(8,128)(2,1)}, u32[]{:S(2)}) %copy-start.4) | copy-done | bytes 327704
  3.6 1.9 %strips.1 = bf16[256,1920]{1,0:T(8,128)(2,1)} custom-call(bf16[1280,128]{1,0:T(8,128)(2,1)S(1)} %bitcast.17), custom_call_target="tpu_custom_call" | custom-call | tf_op jit(solution)/shard_map/strips/pallas_call | solution.py:71
  6.0 10.6 %all-to-all-start = ((bf16[32,8,1920]{2,1,0:T(8,128)(2,1)}), bf16[32,8,1920]{2,1,0:T(8,128)(2,1)}, u32[]{:S(2)}, u32[]{:S(2)}) async-start(bf16[32,8,1920]{2,1,0:T(8,128)(2,1)} %bitcast.3), calls=%async_computation | async-start | bytes 1966080 | tf_op jit(solution)/shard_map/all_to_all | solution.py:548
  16.6 3.5 %collective-permute-start.3 = (bf16[4,2,8,256]{3,2,1,0:T(8,128)(2,1)S(1)}, bf16[4,2,8,256]{3,2,1,0:T(8,128)(2,1)S(1)}, u32[]{:S(2)}, u32[]{:S(2)}) collective-permute-start(bf16[4,2,8,256]{3,2,1,0:T(8,128)(2,1)S(1)} %get-tuple-element.41), channel_id=1, source_target_pairs={{0,1},{1,2},{2,3},{3,4},{4,5},{5,6},{6,7},{7,8},{8,9},{9,10},{10,1... | collective-permute-start | bytes 98312 | tf_op jit(solution)/shard_map/ppermute | solution.py:549
  20.2 7.0 %collective-permute-start.4 = (bf16[4,2,8,256]{3,2,1,0:T(8,128)(2,1)S(1)}, bf16[4,2,8,256]{3,2,1,0:T(8,128)(2,1)S(1)}, u32[]{:S(2)}, u32[]{:S(2)}) collective-permute-start(bf16[4,2,8,256]{3,2,1,0:T(8,128)(2,1)S(1)} %get-tuple-element.42), channel_id=1, source_target_pairs={{1,0},{2,1},{3,2},{4,3},{5,4},{6,5},{7,6},{8,7},{9,8},{10,9},{11,1... | collective-permute-start | bytes 98312 | tf_op jit(solution)/shard_map/ppermute | solution.py:550
  28.1 5.3 %collective-permute-done.3.top_ref = bf16[4,2,8,256]{3,2,1,0:T(8,128)(2,1)S(1)} collective-permute-done((bf16[4,2,8,256]{3,2,1,0:T(8,128)(2,1)S(1)}, bf16[4,2,8,256]{3,2,1,0:T(8,128)(2,1)S(1)}, u32[]{:S(2)}, u32[]{:S(2)}) %collective-permute-start.3) | collective-permute-done | bytes 32800 | tf_op jit(solution)/shard_map/ppermute | solution.py:549
  33.4 0.9 grad_cost.1.refs_7_
  34.3 1.0 %copy-done.1 = f32[8,256,128]{2,1,0:T(8,128)} copy-done((f32[8,256,128]{2,1,0:T(8,128)}, f32[8,256,128]{2,1,0:T(8,128)S(1)}, u32[]{:S(2)}) %copy-start.1) | copy-done | bytes 1048600
  35.3 3.6 %warp_other.1 = (bf16[240,16,128]{2,1,0:T(8,128)(2,1)S(1)}, f32[4,256,128]{2,1,0:T(8,128)S(1)}, f32[4,256,128]{2,1,0:T(8,128)S(1)}, bf16[5,4,256,128]{3,2,1,0:T(8,128)(2,1)S(1)}) custom-call(s32[2560]{0:T(1024)S(1)} %reshape.26.place_ref.refs_0_, s32[8]{0:T(128)S(1)} %fusion.order_ref.refs_1_, bf16[256,1920]{1,0:T(8,128)(2,1)} %bitcast.4.in_ref, ...), custom_call_target="tpu_custom_call" | custom-call | tf_op jit(solution)/shard_map/warp_other/pallas_call | solution.py:195
  39.5 2.5 %warp_mine.1 = (f32[4,256,128]{2,1,0:T(8,128)S(1)}, f32[4,256,128]{2,1,0:T(8,128)S(1)}, bf16[5,4,256,128]{3,2,1,0:T(8,128)(2,1)S(1)}) custom-call(s32[2560]{0:T(1024)S(1)} %reshape.26.place_ref.refs_0_, s32[8]{0:T(128)S(1)} %fusion.order_ref.refs_1_, bf16[240,16,128]{2,1,0:T(8,128)(2,1)S(1)} %get-tuple-element.44.blocks_ref, ...), custom_call_target="tpu_custom_call" | custom-call | tf_op jit(solution)/shard_map/warp_mine/pallas_call | solution.py:206
  42.1 0.8 collective-permute-start.6
  43.5 6.9 %collective-permute-done.6.there_ref.first_there = bf16[4,256,128]{2,1,0:T(8,128)(2,1)S(1)} collective-permute-done((bf16[4,256,128]{2,1,0:T(8,128)(2,1)S(1)}, bf16[4,256,128]{2,1,0:T(8,128)(2,1)S(1)}, u32[]{:S(2)}, u32[]{:S(2)}) %collective-permute-start.6) | collective-permute-done | bytes 262176 | tf_op jit(solution)/shard_map/ppermute | solution.py:533
  50.7 0.9 collective-permute-start.9
  52.2 4.1 %land.2.refs_8_ = bf16[256,1920]{1,0:T(8,128)(2,1)S(1)} custom-call(s32[2560]{0:T(1024)S(1)} %reshape.26.place_ref.refs_0_, s32[8]{0:T(128)S(1)} %fusion.order_ref.refs_1_, bf16[5,4,256,128]{3,2,1,0:T(8,128)(2,1)S(1)} %get-tuple-element.54.refs_2_, bf16[5,4,256,128]{3,2,1,0:T(8,128)(2,1)S(1)} %get-tuple-element.55.refs_3_, ...), custom_call_target="tpu_custom_call" | custom-call | flops 4200000000 | bytes 12599999 | tf_op jit(solution)/shard_map/land/pallas_call | solution.py:273
  56.3 5.9 %collective-permute-done.9.second_there = f32[3,256,128]{2,1,0:T(8,128)S(1)} collective-permute-done((f32[3,256,128]{2,1,0:T(8,128)S(1)}, f32[3,256,128]{2,1,0:T(8,128)S(1)}, u32[]{:S(2)}, u32[]{:S(2)}) %collective-permute-start.9) | collective-permute-done | bytes 393248 | tf_op jit(solution)/shard_map/ppermute | solution.py:533
  63.0 3.0 %land.3 = bf16[256,1920]{1,0:T(8,128)(2,1)S(1)} custom-call(s32[2560]{0:T(1024)S(1)} %reshape.26.place_ref.refs_0_, s32[8]{0:T(128)S(1)} %fusion.order_ref.refs_1_, bf16[5,4,256,128]{3,2,1,0:T(8,128)(2,1)S(1)} %get-tuple-element.54.refs_2_, bf16[5,4,256,128]{3,2,1,0:T(8,128)(2,1)S(1)} %get-tuple-element.55.refs_3_, ...), custom_call_target="tpu_custom_call", output_to_operand_aliasing={{}: (8, {})} | custom-call | flops 2800000000 | bytes 8400000 | tf_op jit(solution)/shard_map/land/pallas_call | solution.py:273
  66.0 0.9 copy-done.3
  67.6 6.4 %all-to-all-start.1 = ((bf16[32,8,1920]{2,1,0:T(8,128)(2,1)}), bf16[32,8,1920]{2,1,0:T(8,128)(2,1)S(1)}, u32[]{:S(2)}, u32[]{:S(2)}) async-start(bf16[32,8,1920]{2,1,0:T(8,128)(2,1)} %bitcast.16), calls=%async_computation.1 | async-start | bytes 1966080 | tf_op jit(solution)/shard_map/all_to_all | solution.py:577
  73.9 3.4 %collective-permute-start.11 = (bf16[4,64,128]{2,1,0:T(8,128)(2,1)S(1)}, bf16[4,64,128]{2,1,0:T(8,128)(2,1)S(1)}, u32[]{:S(2)}, u32[]{:S(2)}) collective-permute-start(bf16[4,64,128]{2,1,0:T(8,128)(2,1)S(1)} %get-tuple-element.68), channel_id=1, source_target_pairs={{0,1},{1,2},{2,3},{3,4},{4,5},{5,6},{6,7},{7,8},{8,9},{9,10},{10,1... | collective-permute-start | bytes 196616 | tf_op jit(solution)/shard_map/ppermute | solution.py:578
  77.3 7.0 %collective-permute-start.12 = (bf16[4,64,128]{2,1,0:T(8,128)(2,1)S(1)}, bf16[4,64,128]{2,1,0:T(8,128)(2,1)S(1)}, u32[]{:S(2)}, u32[]{:S(2)}) collective-permute-start(bf16[4,64,128]{2,1,0:T(8,128)(2,1)S(1)} %get-tuple-element.69), channel_id=1, source_target_pairs={{1,0},{2,1},{3,2},{4,3},{5,4},{6,5},{7,6},{8,7},{9,8},{10,9},{11,1... | collective-permute-start | bytes 196616 | tf_op jit(solution)/shard_map/ppermute | solution.py:579
  84.3 7.5 %collective-permute-done.11.top_ref = bf16[4,64,128]{2,1,0:T(8,128)(2,1)S(1)} collective-permute-done((bf16[4,64,128]{2,1,0:T(8,128)(2,1)S(1)}, bf16[4,64,128]{2,1,0:T(8,128)(2,1)S(1)}, u32[]{:S(2)}, u32[]{:S(2)}) %collective-permute-start.11) | collective-permute-done | bytes 65568 | tf_op jit(solution)/shard_map/ppermute | solution.py:578
  91.8 1.5 %conv.1 = bf16[2,8,1024]{2,1,0:T(8,128)(2,1)} custom-call(bf16[2,256,128]{2,1,0:T(8,128)(2,1)S(1)} %get-tuple-element.64.outer_ref, bf16[1,256,128]{2,1,0:T(8,128)(2,1)S(1)} %get-tuple-element.59.low_ref, bf16[1,256,128]{2,1,0:T(8,128)(2,1)S(1)} %get-tuple-element.60.high_ref, bf16[4,64,128]{2,1,0:T(8,128)(2,1)S(1)} %collective-permute-done.11.top_ref, ...), custom_call_target="tpu_custom_call" | custom-call | tf_op jit(solution)/shard_map/conv/pallas_call | solution.py:507
  93.3 1.5 %unstrips.1 = f32[1280,128]{1,0:T(8,128)} custom-call(bf16[256,1920]{1,0:T(8,128)(2,1)S(1)} %bitcast.15), custom_call_target="tpu_custom_call" | custom-call | tf_op jit(solution)/shard_map/unstrips/pallas_call | solution.py:102
  (50 shorter events, 5.3 us)
Async XLA Ops:
  0.6 4.8 %collective-permute-start = (bf16[2,8,1024]{2,1,0:T(8,128)(2,1)}, bf16[2,8,1024]{2,1,0:T(8,128)(2,1)S(1)}, u32[]{:S(2)}, u32[]{:S(2)}) collective-permute-start(bf16[2,8,1024]{2,1,0:T(8,128)(2,1)} %refs_0_.1), channel_id=1, source_target_pairs={{0,32},{32,0},{64,96},{96,64},{1,33},{33,1},{65,97},{97,65},{2,34}... | collective-permute-start | bytes 98312 | tf_op jit(solution)/shard_map/ppermute | solution.py:533
  0.7 4.7 %collective-permute-start.1 = (bf16[2,8,1024]{2,1,0:T(8,128)(2,1)}, bf16[2,8,1024]{2,1,0:T(8,128)(2,1)S(1)}, u32[]{:S(2)}, u32[]{:S(2)}) collective-permute-start(bf16[2,8,1024]{2,1,0:T(8,128)(2,1)} %refs_0_.1), channel_id=1, source_target_pairs={{0,64},{32,96},{64,0},{96,32},{1,65},{33,97},{65,1},{97,33},{2,66}... | collective-permute-start | bytes 98312 | tf_op jit(solution)/shard_map/ppermute | solution.py:533
  2.4 3.6 %collective-permute-start.2 = (bf16[2,8,1024]{2,1,0:T(8,128)(2,1)}, bf16[2,8,1024]{2,1,0:T(8,128)(2,1)S(1)}, u32[]{:S(2)}, u32[]{:S(2)}) collective-permute-start(bf16[2,8,1024]{2,1,0:T(8,128)(2,1)} %refs_0_.1), channel_id=1, source_target_pairs={{0,96},{32,64},{64,32},{96,0},{1,97},{33,65},{65,33},{97,1},{2,98}... | collective-permute-start | bytes 98312 | tf_op jit(solution)/shard_map/ppermute | solution.py:533
  2.6 1.0 %copy-start.4 = (bf16[5,32,8,128]{3,2,1,0:T(8,128)(2,1)S(1)}, bf16[5,32,8,128]{3,2,1,0:T(8,128)(2,1)}, u32[]{:S(2)}) copy-start(bf16[5,32,8,128]{3,2,1,0:T(8,128)(2,1)} %param.7) | copy-start | bytes 983044
  3.6 2.4 %copy-start.6 = (bf16[2,8,1024]{2,1,0:T(8,128)(2,1)S(1)}, bf16[2,8,1024]{2,1,0:T(8,128)(2,1)}, u32[]{:S(2)}) copy-start(bf16[2,8,1024]{2,1,0:T(8,128)(2,1)} %refs_0_.1) | copy-start | bytes 98308
  5.4 11.1 %copy-start.8 = (s32[5,8,16,4]{2,3,1,0:T(4,128)S(1)}, s32[5,8,16,4]{2,3,1,0:T(4,128)}, u32[]{:S(2)}) copy-start(s32[5,8,16,4]{2,3,1,0:T(4,128)} %param.11) | copy-start | bytes 30724
  5.4 11.2 %copy-start.9 = (s32[5,8,16,4]{2,3,1,0:T(4,128)S(1)}, s32[5,8,16,4]{2,3,1,0:T(4,128)}, u32[]{:S(2)}) copy-start(s32[5,8,16,4]{2,3,1,0:T(4,128)} %param.10) | copy-start | bytes 30724
  6.0 21.7 %copy-start.7 = (bf16[3,3,3,8,32]{4,3,2,1,0:T(8,128)(2,1)S(1)}, bf16[3,3,3,8,32]{4,3,2,1,0:T(8,128)(2,1)}, u32[]{:S(2)}) copy-start(bf16[3,3,3,8,32]{4,3,2,1,0:T(8,128)(2,1)} %param.12) | copy-start | bytes 41476
  6.0 29.3 %all-to-all-start = ((bf16[32,8,1920]{2,1,0:T(8,128)(2,1)}), bf16[32,8,1920]{2,1,0:T(8,128)(2,1)}, u32[]{:S(2)}, u32[]{:S(2)}) async-start(bf16[32,8,1920]{2,1,0:T(8,128)(2,1)} %bitcast.3), calls=%async_computation | async-start | bytes 1966080 | tf_op jit(solution)/shard_map/all_to_all | solution.py:548
  16.6 18.7 %copy-start = (bf16[5,8,4,64,64]{4,3,2,1,0:T(8,128)(2,1)S(1)}, bf16[5,8,4,64,64]{4,3,2,1,0:T(8,128)(2,1)}, u32[]{:S(2)}) copy-start(bf16[5,8,4,64,64]{4,3,2,1,0:T(8,128)(2,1)} %refs_4_.3) | copy-start | bytes 3932164
  16.6 16.7 %collective-permute-start.3 = (bf16[4,2,8,256]{3,2,1,0:T(8,128)(2,1)S(1)}, bf16[4,2,8,256]{3,2,1,0:T(8,128)(2,1)S(1)}, u32[]{:S(2)}, u32[]{:S(2)}) collective-permute-start(bf16[4,2,8,256]{3,2,1,0:T(8,128)(2,1)S(1)} %get-tuple-element.41), channel_id=1, source_target_pairs={{0,1},{1,2},{2,3},{3,4},{4,5},{5,6},{6,7},{7,8},{8,9},{9,10},{10,1... | collective-permute-start | bytes 98312 | tf_op jit(solution)/shard_map/ppermute | solution.py:549
  20.2 13.2 %collective-permute-start.4 = (bf16[4,2,8,256]{3,2,1,0:T(8,128)(2,1)S(1)}, bf16[4,2,8,256]{3,2,1,0:T(8,128)(2,1)S(1)}, u32[]{:S(2)}, u32[]{:S(2)}) collective-permute-start(bf16[4,2,8,256]{3,2,1,0:T(8,128)(2,1)S(1)} %get-tuple-element.42), channel_id=1, source_target_pairs={{1,0},{2,1},{3,2},{4,3},{5,4},{6,5},{7,6},{8,7},{9,8},{10,9},{11,1... | collective-permute-start | bytes 98312 | tf_op jit(solution)/shard_map/ppermute | solution.py:550
  34.3 1.0 %copy-start.1 = (f32[8,256,128]{2,1,0:T(8,128)}, f32[8,256,128]{2,1,0:T(8,128)S(1)}, u32[]{:S(2)}) copy-start(f32[8,256,128]{2,1,0:T(8,128)S(1)} %grad_cost.1.refs_7_) | copy-start | bytes 3145732
  38.9 3.1 %collective-permute-start.5 = (f32[4,256,128]{2,1,0:T(8,128)S(1)}, f32[4,256,128]{2,1,0:T(8,128)S(1)}, u32[]{:S(2)}, u32[]{:S(2)}) collective-permute-start(f32[4,256,128]{2,1,0:T(8,128)S(1)} %get-tuple-element.46), channel_id=1, source_target_pairs={{0,32},{32,0},{64,96},{96,64},{1,33},{33,1},{65,97},{97,65},{2,34}... | collective-permute-start | bytes 1572872 | tf_op jit(solution)/shard_map/ppermute | solution.py:533
  39.0 4.0 %collective-permute-start.7 = (f32[4,256,128]{2,1,0:T(8,128)S(1)}, f32[4,256,128]{2,1,0:T(8,128)S(1)}, u32[]{:S(2)}, u32[]{:S(2)}) collective-permute-start(f32[4,256,128]{2,1,0:T(8,128)S(1)} %get-tuple-element.50), channel_id=1, source_target_pairs={{0,32},{32,0},{64,96},{96,64},{1,33},{33,1},{65,97},{97,65},{2,34}... | collective-permute-start | bytes 1572872 | tf_op jit(solution)/shard_map/ppermute | solution.py:533
  42.0 8.5 %copy-start.5 = (bf16[32,1024]{1,0:T(8,128)(2,1)S(1)}, bf16[32,1024]{1,0:T(8,128)(2,1)}, u32[]{:S(2)}) copy-start(bf16[32,1024]{1,0:T(8,128)(2,1)} %ref_ref.3) | copy-start | bytes 196612
  42.0 10.1 %copy-start.2 = (f32[8,256,128]{2,1,0:T(8,128)S(1)}, f32[8,256,128]{2,1,0:T(8,128)}, u32[]{:S(2)}) copy-start(f32[8,256,128]{2,1,0:T(8,128)} %copy-done.1) | copy-start | bytes 3145732
  42.1 8.4 %collective-permute-start.6 = (bf16[4,256,128]{2,1,0:T(8,128)(2,1)S(1)}, bf16[4,256,128]{2,1,0:T(8,128)(2,1)S(1)}, u32[]{:S(2)}, u32[]{:S(2)}) collective-permute-start(bf16[4,256,128]{2,1,0:T(8,128)(2,1)S(1)} %get-tuple-element.48), channel_id=1, source_target_pairs={{0,64},{32,96},{64,0},{96,32},{1,65},{33,97},{65,1},{97,33},{2,66}... | collective-permute-start | bytes 786440 | tf_op jit(solution)/shard_map/ppermute | solution.py:533
  50.6 1.6 %collective-permute-start.8 = (bf16[4,256,128]{2,1,0:T(8,128)(2,1)S(1)}, bf16[4,256,128]{2,1,0:T(8,128)(2,1)S(1)}, u32[]{:S(2)}, u32[]{:S(2)}) collective-permute-start(bf16[4,256,128]{2,1,0:T(8,128)(2,1)S(1)} %mean.1.refs_6_), channel_id=1, source_target_pairs={{0,32},{32,0},{64,96},{96,64},{1,33},{33,1},{65,97},{97,65},{2,34}... | collective-permute-start | bytes 786440 | tf_op jit(solution)/shard_map/ppermute | solution.py:533
  50.7 11.5 %collective-permute-start.9 = (f32[3,256,128]{2,1,0:T(8,128)S(1)}, f32[3,256,128]{2,1,0:T(8,128)S(1)}, u32[]{:S(2)}, u32[]{:S(2)}) collective-permute-start(f32[3,256,128]{2,1,0:T(8,128)S(1)} %get-tuple-element.57), channel_id=1, source_target_pairs={{0,64},{32,96},{64,0},{96,32},{1,65},{33,97},{65,1},{97,33},{2,66}... | collective-permute-start | bytes 1179656 | tf_op jit(solution)/shard_map/ppermute | solution.py:533
  62.9 4.1 %collective-permute-start.10 = (bf16[2,256,128]{2,1,0:T(8,128)(2,1)S(1)}, bf16[2,256,128]{2,1,0:T(8,128)(2,1)S(1)}, u32[]{:S(2)}, u32[]{:S(2)}) collective-permute-start(bf16[2,256,128]{2,1,0:T(8,128)(2,1)S(1)} %get-tuple-element.62), channel_id=1, source_target_pairs={{0,32},{32,0},{64,96},{96,64},{1,33},{33,1},{65,97},{97,65},{2,34}... | collective-permute-start | bytes 393224 | tf_op jit(solution)/shard_map/ppermute | solution.py:533
  67.6 25.7 %all-to-all-start.1 = ((bf16[32,8,1920]{2,1,0:T(8,128)(2,1)}), bf16[32,8,1920]{2,1,0:T(8,128)(2,1)S(1)}, u32[]{:S(2)}, u32[]{:S(2)}) async-start(bf16[32,8,1920]{2,1,0:T(8,128)(2,1)} %bitcast.16), calls=%async_computation.1 | async-start | bytes 1966080 | tf_op jit(solution)/shard_map/all_to_all | solution.py:577
  73.9 17.9 %collective-permute-start.11 = (bf16[4,64,128]{2,1,0:T(8,128)(2,1)S(1)}, bf16[4,64,128]{2,1,0:T(8,128)(2,1)S(1)}, u32[]{:S(2)}, u32[]{:S(2)}) collective-permute-start(bf16[4,64,128]{2,1,0:T(8,128)(2,1)S(1)} %get-tuple-element.68), channel_id=1, source_target_pairs={{0,1},{1,2},{2,3},{3,4},{4,5},{5,6},{6,7},{7,8},{8,9},{9,10},{10,1... | collective-permute-start | bytes 196616 | tf_op jit(solution)/shard_map/ppermute | solution.py:578
  77.3 14.5 %collective-permute-start.12 = (bf16[4,64,128]{2,1,0:T(8,128)(2,1)S(1)}, bf16[4,64,128]{2,1,0:T(8,128)(2,1)S(1)}, u32[]{:S(2)}, u32[]{:S(2)}) collective-permute-start(bf16[4,64,128]{2,1,0:T(8,128)(2,1)S(1)} %get-tuple-element.69), channel_id=1, source_target_pairs={{1,0},{2,1},{3,2},{4,3},{5,4},{6,5},{7,6},{8,7},{9,8},{10,9},{11,1... | collective-permute-start | bytes 196616 | tf_op jit(solution)/shard_map/ppermute | solution.py:579
  (1 other events, 1.0 us)

commit v3 on v2

--- a/solution.py
+++ b/solution.py
@@ -13,7 +13,7 @@
 PLANES = 8
 COUNT = 21.0
 SEGS = 48
-VMEM_LIMIT = 4 * 1024 * 1024
+VMEM_LIMIT = 8 * 1024 * 1024
 NT = (((1,), (1,)), ((), ()))
 NN = (((1,), (0,)), ((), ()))
 TN = (((0,), (0,)), ((), ()))
@@ -27,10 +27,7 @@
     return pl.BlockSpec(memory_space=pltpu.VMEM)
 
 
-def cost_us(microseconds):
-    return pl.CostEstimate(
-        flops=int(microseconds * 1.0e9), bytes_accessed=int(microseconds * 3.0e6), transcendentals=0
-    )
+SMALL = pl.CostEstimate(flops=1000, bytes_accessed=1000, transcendentals=0)
 
 
 def iota(shape, dim):
@@ -51,29 +48,23 @@
     table = band_table()
     mask = row_mask()
     for x in range(8):
-        own = wide[pl.ds(x, 160, stride=8), :]
-        parts = []
-        for v in range(VIEWS):
-            part = own[v * 32 : (v + 1) * 32]
-            parts.append(jnp.where(mask, jnp.concatenate([part] * 4, axis=0), 0.0).astype(BF))
-        stacked = jnp.concatenate(parts, axis=0)
-        moved = lax.dot_general(table, stacked, NT, preferred_element_type=F32)
-        for v in range(VIEWS):
-            for band in range(3):
-                stage[v * 3 + band, pl.ds(x, 32, stride=8), :] = moved[
-                    band * 32 : (band + 1) * 32, v * 128 : (v + 1) * 128
-                ]
-    for piece in range(VIEWS * 3):
-        out_ref[:, piece * 128 : (piece + 1) * 128] = stage[piece].astype(BF)
+        own = wide[pl.ds(x, 32, stride=8), :]
+        tall = jnp.where(mask, jnp.concatenate([own] * 4, axis=0), 0.0).astype(BF)
+        moved = lax.dot_general(table, tall, NT, preferred_element_type=F32)
+        for band in range(3):
+            stage[band, pl.ds(x, 32, stride=8), :] = moved[band * 32 : (band + 1) * 32]
+    for band in range(3):
+        out_ref[:, band * 128 : (band + 1) * 128] = stage[band].astype(BF)
 
 
 def strips(source):
     return pl.pallas_call(
         strips_kernel,
-        out_shape=jax.ShapeDtypeStruct((256, VIEWS * 384), BF),
-        in_specs=[whole()],
-        out_specs=whole(),
-        scratch_shapes=[pltpu.VMEM((1280, 128), F32), pltpu.VMEM((VIEWS * 3, 256, 128), F32)],
+        grid=(VIEWS,),
+        out_shape=pltpu.HBM((256, VIEWS * 384), BF),
+        in_specs=[pl.BlockSpec((256, 128), lambda v: (v, 0))],
+        out_specs=pl.BlockSpec((256, 384), lambda v: (0, v)),
+        scratch_shapes=[pltpu.VMEM((256, 128), F32), pltpu.VMEM((3, 256, 128), F32)],
         compiler_params=params(),
         name="strips",
     )(source)
@@ -145,12 +136,29 @@
                 blocks_ref[at + 1] = odd.astype(BF)
 
 
-def warp_planes(group, place_ref, order_ref, blocks_ref, interp_ref, first_ref, second_ref, warped_ref):
+def warp_planes(group, place_ref, order_ref, blocks_ref, interp_hbm, first_ref, second_ref,
+                warped_hbm, interp_ref, warped_ref, in_sem, out_sem, prepare):
+    loads = []
+    for view in range(VIEWS):
+        for pair in range(2):
+            plane = order_ref[group * 4 + pair * 2]
+            loads.append(
+                pltpu.make_async_copy(
+                    interp_hbm.at[view, pl.ds(plane, 2)],
+                    interp_ref.at[view, pl.ds(pair * 2, 2)],
+                    in_sem.at[view, pair],
+                )
+            )
+    for load in loads:
+        load.start()
+    prepare()
     first_ref[...] = jnp.zeros_like(first_ref)
     second_ref[...] = jnp.zeros_like(second_ref)
-
-    def step(view, unused):
+    stores = []
+    for view in range(VIEWS):
         for e in range(4):
+            if e % 2 == 0:
+                loads[view * 2 + e // 2].wait()
             plane = order_ref[group * 4 + e]
             base = (view * PLANES + plane) * 64
             rows = []
@@ -158,32 +166,35 @@
                 taps = [blocks_ref[view * SEGS + place_ref[base + g * 4 + k]] for k in range(4)]
                 rows.append(jnp.concatenate(taps, axis=1))
             picked = jnp.concatenate(rows, axis=0)
-            matrix = spread_interp(interp_ref[view, plane])
+            matrix = spread_interp(interp_ref[view, e])
             warped = lax.dot_general(picked, matrix, NN, preferred_element_type=F32)
             first_ref[e] += warped
             second_ref[e] += warped * warped
             warped_ref[view, e] = warped.astype(BF)
-        return unused
-
-    lax.fori_loop(0, VIEWS, step, 0, unroll=UNROLL)
+        store = pltpu.make_async_copy(warped_ref.at[view], warped_hbm.at[view], out_sem.at[view])
+        store.start()
+        stores.append(store)
+    for store in stores:
+        store.wait()
 
 
 def warp_other_kernel(
-    place_ref, order_ref, in_ref, interp_ref, blocks_ref, first_ref, second_ref, warped_ref
+    place_ref, order_ref, in_ref, interp_hbm, blocks_ref, first_ref, second_ref, *rest
 ):
-    turn_kernel(in_ref, blocks_ref)
-    warp_planes(0, place_ref, order_ref, blocks_ref, interp_ref, first_ref, second_ref, warped_ref)
-
-
-def warp_mine_kernel(
-    place_ref, order_ref, blocks_ref, interp_ref, first_ref, second_ref, warped_ref
-):
-    warp_planes(1, place_ref, order_ref, blocks_ref, interp_ref, first_ref, second_ref, warped_ref)
-
-
-UNROLL = 5
+    warp_planes(
+        0, place_ref, order_ref, blocks_ref, interp_hbm, first_ref, second_ref, *rest,
+        lambda: turn_kernel(in_ref, blocks_ref),
+    )
+
+
+def warp_mine_kernel(place_ref, order_ref, blocks_ref, interp_hbm, first_ref, second_ref, *rest):
+    warp_planes(
+        1, place_ref, order_ref, blocks_ref, interp_hbm, first_ref, second_ref, *rest, lambda: None
+    )
+
+
 SUMS = jax.ShapeDtypeStruct((4, 256, 128), F32)
-WARPED = jax.ShapeDtypeStruct((VIEWS, 4, 256, 128), BF)
+WARPED = pltpu.HBM((VIEWS, 4, 256, 128), BF)
 BLOCKS = jax.ShapeDtypeStruct((VIEWS * SEGS, 16, 128), BF)
 
 
@@ -191,45 +202,81 @@
     return pl.BlockSpec(memory_space=pltpu.SMEM)
 
 
+def in_hbm(array):
+    return pltpu.with_memory_space_constraint(array, pltpu.HBM)
+
+
+def hbm():
+    return pl.BlockSpec(memory_space=pltpu.HBM)
+
+
+WARP_SCRATCH = [
+    pltpu.VMEM((VIEWS, 4, 4, 64, 64), BF),
+    pltpu.VMEM((VIEWS, 4, 256, 128), BF),
+    pltpu.SemaphoreType.DMA((VIEWS, 2)),
+    pltpu.SemaphoreType.DMA((VIEWS,)),
+]
+
+
 def warp_other(place, order, arrived, interp):
     return pl.pallas_call(
         warp_other_kernel,
-        in_specs=[smem(), smem(), whole(), whole()],
-        out_specs=[whole()] * 4,
+        in_specs=[smem(), smem(), whole(), hbm()],
+        out_specs=[whole()] * 3 + [hbm()],
+        scratch_shapes=WARP_SCRATCH,
         out_shape=[BLOCKS, SUMS, SUMS, WARPED],
         compiler_params=params(),
         name="warp_other",
-    )(place, order, arrived, interp)
+    )(place, order, arrived, in_hbm(interp))
 
 
 def warp_mine(place, order, blocks, interp):
     return pl.pallas_call(
         warp_mine_kernel,
-        in_specs=[smem(), smem(), whole(), whole()],
-        out_specs=[whole()] * 3,
+        in_specs=[smem(), smem(), whole(), hbm()],
+        out_specs=[whole()] * 2 + [hbm()],
+        scratch_shapes=WARP_SCRATCH,
         out_shape=[SUMS, SUMS, WARPED],
         compiler_params=params(),
         name="warp_mine",
-    )(place, order, blocks, interp)
+    )(place, order, blocks, in_hbm(interp))
 
 
 CHAINS = 4
 
 
-def land_views(
-    views, place_ref, order_ref, warped_o, warped_m, interp_ref, mean_o, mean_m, grad_ref, out_ref, accs
-):
-    groups = ((warped_o, mean_o), (warped_m, mean_m))
-    for view in views:
+def land_kernel(views, aliased, place_ref, order_ref, warped_o, warped_m, interp_hbm, mean_o, mean_m,
+                grad_ref, *rest):
+    out_hbm, warped_ref, interp_ref, out_ref, in_sem, out_sem, *accs = rest[aliased:]
+    loads = []
+    for at, view in enumerate(views):
+        loads.append(
+            [
+                pltpu.make_async_copy(interp_hbm.at[view], interp_ref.at[at], in_sem.at[at, 0]),
+                pltpu.make_async_copy(
+                    warped_o.at[view], warped_ref.at[at, pl.ds(0, 4)], in_sem.at[at, 1]
+                ),
+                pltpu.make_async_copy(
+                    warped_m.at[view], warped_ref.at[at, pl.ds(4, 4)], in_sem.at[at, 2]
+                ),
+            ]
+        )
+    for load in loads:
+        for copy in load:
+            copy.start()
+    stores = []
+    for at, view in enumerate(views):
         for acc in accs:
             acc[...] = jnp.zeros_like(acc)
+        for copy in loads[at]:
+            copy.wait()
         for e in range(8):
-            warped_ref, mean_ref = groups[e // 4]
+            mean_ref = (mean_o, mean_m)[e // 4]
             plane = order_ref[e]
             base = (view * PLANES + plane) * 64
-            warped = warped_ref[view, e % 4].astype(F32)
+            warped = warped_ref[at, e].astype(F32)
             grad = (grad_ref[plane] * (warped - mean_ref[e % 4].astype(F32))).astype(BF)
-            matrix = spread_interp(interp_ref[view, plane])
+            matrix = spread_interp(interp_ref[at, plane])
             spread = lax.dot_general(grad, matrix, NT, preferred_element_type=F32)
             for g in range(16):
                 for k in range(4):
@@ -239,46 +286,52 @@
         for band_row in range(12):
             columns_up, columns_low = [], []
             for half in range(2):
-                at = band_row * 4 + half * 2
-                even = (accs[0][at] + accs[1][at]) + (accs[2][at] + accs[3][at])
-                odd = (accs[0][at + 1] + accs[1][at + 1]) + (accs[2][at + 1] + accs[3][at + 1])
+                seg = band_row * 4 + half * 2
+                even = (accs[0][seg] + accs[1][seg]) + (accs[2][seg] + accs[3][seg])
+                odd = (accs[0][seg + 1] + accs[1][seg + 1]) + (accs[2][seg + 1] + accs[3][seg + 1])
                 up, low = pair_swap(even, odd)
                 columns_up.append(up)
                 columns_low.append(low)
             bands.append(jnp.concatenate(columns_up, axis=1))
             bands.append(jnp.concatenate(columns_low, axis=1))
-        out_ref[:, view * 384 : (view + 1) * 384] = jnp.concatenate(bands, axis=0).T.astype(BF)
-
-
-def land_first_kernel(views, *refs):
-    land_views(views, *refs[:9], refs[9:])
-
-
-def land_next_kernel(views, *refs):
-    land_views(views, *refs[:8], refs[9], refs[10:])
-
-
-LANDED = jax.ShapeDtypeStruct((256, VIEWS * 384), BF)
+        out_ref[at] = jnp.concatenate(bands, axis=0).T.astype(BF)
+        store = pltpu.make_async_copy(
+            out_ref.at[at], out_hbm.at[:, view * 384 : (view + 1) * 384], out_sem.at[at]
+        )
+        store.start()
+        stores.append(store)
+    for store in stores:
+        store.wait()
+
+
+LANDED = pltpu.HBM((256, VIEWS * 384), BF)
 
 
 def land(views, place, order, warped_o, warped_m, interp, mean_o, mean_m, grad, earlier=None):
+    warped_o, warped_m, interp = (in_hbm(a) for a in (warped_o, warped_m, interp))
     operands = [place, order, warped_o, warped_m, interp, mean_o, mean_m, grad]
-    specs = [smem(), smem()] + [whole()] * 6
-    if earlier is None:
-        kernel, aliases = land_first_kernel, {}
-    else:
-        kernel, aliases = land_next_kernel, {8: 0}
+    specs = [smem(), smem(), hbm(), hbm(), hbm(), whole(), whole(), whole()]
+    aliased = 0 if earlier is None else 1
+    if aliased:
         operands.append(earlier)
-        specs.append(whole())
-    return pl.pallas_call(
-        functools.partial(kernel, views),
+        specs.append(hbm())
+    count = len(views)
+    return pl.pallas_call(
+        functools.partial(land_kernel, views, aliased),
         in_specs=specs,
-        out_specs=whole(),
+        out_specs=hbm(),
         out_shape=LANDED,
-        scratch_shapes=[pltpu.VMEM((SEGS, 16, 128), F32)] * CHAINS,
-        input_output_aliases=aliases,
-        compiler_params=params(),
-        cost_estimate=cost_us(1.4 * len(views)),
+        scratch_shapes=[
+            pltpu.VMEM((count, PLANES, 256, 128), BF),
+            pltpu.VMEM((count, PLANES, 4, 64, 64), BF),
+            pltpu.VMEM((count, 256, 384), BF),
+            pltpu.SemaphoreType.DMA((count, 3)),
+            pltpu.SemaphoreType.DMA((count,)),
+        ]
+        + [pltpu.VMEM((SEGS, 16, 128), F32)] * CHAINS,
+        input_output_aliases={8: 0} if aliased else {},
+        compiler_params=params(),
+        cost_estimate=SMALL,
         name="land",
     )(*operands)
 
@@ -550,8 +603,9 @@
     bottom = lax.ppermute(initial, "tile", down)
     back_weight = conv_weight.transpose(1, 4, 0, 2, 3).reshape(96, 72)
     weight = conv_weight.transpose(0, 1, 3, 2, 4).reshape(72, 96)
-    grad = grad_cost(view.astype(jnp.int32).reshape(1), cotangent, top, bottom, back_weight)
-    arrived, grad, weight = lax.optimization_barrier((arrived, grad, weight))
+    arrived, top, bottom, weight, back_weight = lax.optimization_barrier(
+        (arrived, top, bottom, weight, back_weight)
+    )
 
     blocks, first_o, second_o, warped_o = warp_other(place, order, arrived, interp)
     first_m, second_m, warped_m = warp_mine(place, order, blocks, interp)
@@ -559,7 +613,8 @@
     first_there = other(first_send, 2)
     second_own, second_send = chip_second(where, second_m, other(second_o, 1))
     second_there = other(second_send, 2)
-    first_there, second_own = lax.optimization_barrier((first_there, second_own))
+    grad = grad_cost(view.astype(jnp.int32).reshape(1), cotangent, top, bottom, back_weight)
+    first_there, second_own, grad = lax.optimization_barrier((first_there, second_own, grad))
     mean_mine = mean_of(first_chip, first_there, reference_features)
     mean_other = other(mean_mine, 1)
 

time: 95.3 us -> 99.7 us (1.046)
  Pallas kernels: 21 us -> 33.3 us
  waiting for transfers between devices: 26.7 us -> 19.8 us
  local copies, waits for them, and re-layouts: 3.8 us -> 1.86 us
    pallas_call x5, Pallas kernels: 15 us -> 27.3 us  [the longest x2 11.5 us: land(): pl.pallas_call(functools.partial(land_kernel, views, aliased), in_specs=s...]
    ppermute x9, waiting for transfers between devices: 13.9 us -> 6.69 us  [other(): return lax.ppermute(array, 'view', [(i, i ^ mask) for i in range(views)])]
    unnamed x20 -> x12, local copies, waits for them, and re-layouts: 2.92 us -> 1 us
  transfers between devices with their start and end apart: 15 -> 15, of which waited for: 6 -> 4; matrix products, arithmetic and copies ran while one was open for 1% -> 1% of each run, Pallas kernels for 15% -> 24%
where the time goes in v3:
time: 99.7 us; the launch traced here: 99.1 us
  starting transfers between devices  43.1 us (43%)
  Pallas kernels  33.3 us (33%)
  waiting for transfers between devices  19.8 us (20%)
  local copies, waits for them, and re-layouts  1.86 us (2%)
    pallas_call x2, Pallas kernels, land(): pl.pallas_call(functools.partial(land_kernel, views, aliased), in_specs=s...  11.5 us
    all_to_all x1, starting transfers between devices, body(): lax.all_to_all(operand, 'tile', split_axis=0, concat_axis=0, tiled=True)  10.8 us
    ppermute x1, waiting for transfers between devices, body(): cost_top = lax.ppermute(cost_last, 'tile', up)  7.38 us
    ppermute x1, starting transfers between devices, body(): bottom = lax.ppermute(initial, 'tile', down)  6.98 us
    ppermute x1, starting transfers between devices, body(): cost_bottom = lax.ppermute(cost_initial, 'tile', down)  6.98 us
    ppermute x9, waiting for transfers between devices, other(): return lax.ppermute(array, 'view', [(i, i ^ mask) for i in range(views)])  6.69 us
    pallas_call x1, Pallas kernels, warp_other(): pl.pallas_call(warp_other_kernel, in_specs=[smem(), smem(), whole(), hbm(...  6.46 us
    all_to_all x1, starting transfers between devices, body(): lax.all_to_all(landed, 'tile', split_axis=0, concat_axis=0, tiled=True)  6.31 us
  transfers between devices with their start and end apart: 15, of which 4 were waited for; matrix products, arithmetic and copies ran while one was open for 1% of the time, Pallas kernels for 24%

profile of v3, /device:TPU:32, one launch (start us, length us, event | category | flops | bytes accessed | tf_op | source)
XLA Modules:
  0.0 99.1 jit_solution(5849815014223676820)
XLA Ops:
  0.7 1.7 %collective-permute-start.1 = (bf16[2,8,1024]{2,1,0:T(8,128)(2,1)}, bf16[2,8,1024]{2,1,0:T(8,128)(2,1)S(1)}, u32[]{:S(2)}, u32[]{:S(2)}) collective-permute-start(bf16[2,8,1024]{2,1,0:T(8,128)(2,1)} %refs_0_.1), channel_id=1, source_target_pairs={{0,64},{32,96},{64,0},{96,32},{1,65},{33,97},{65,1},{97,33},{2,66}... | collective-permute-start | bytes 98312 | tf_op jit(solution)/shard_map/ppermute | solution.py:586
  2.6 1.0 copy-done
  3.6 3.2 %strips.1 = bf16[256,1920]{1,0:T(8,128)(2,1)} custom-call(bf16[1280,128]{1,0:T(8,128)(2,1)S(1)} %bitcast.17), custom_call_target="tpu_custom_call" | custom-call | tf_op jit(solution)/shard_map/strips/pallas_call | solution.py:61
  6.8 10.8 %all-to-all-start = ((bf16[32,8,1920]{2,1,0:T(8,128)(2,1)}), bf16[32,8,1920]{2,1,0:T(8,128)(2,1)S(1)}, u32[]{:S(2)}, u32[]{:S(2)}) async-start(bf16[32,8,1920]{2,1,0:T(8,128)(2,1)} %bitcast.19), calls=%async_computation | async-start | bytes 1966080 | tf_op jit(solution)/shard_map/all_to_all | solution.py:601
  17.7 3.4 %collective-permute-start.3 = (bf16[4,2,8,256]{3,2,1,0:T(8,128)(2,1)S(1)}, bf16[4,2,8,256]{3,2,1,0:T(8,128)(2,1)S(1)}, u32[]{:S(2)}, u32[]{:S(2)}) collective-permute-start(bf16[4,2,8,256]{3,2,1,0:T(8,128)(2,1)S(1)} %get-tuple-element.43), channel_id=1, source_target_pairs={{0,1},{1,2},{2,3},{3,4},{4,5},{5,6},{6,7},{7,8},{8,9},{9,10},{10,1... | collective-permute-start | bytes 98312 | tf_op jit(solution)/shard_map/ppermute | solution.py:602
  21.1 7.0 %collective-permute-start.4 = (bf16[4,2,8,256]{3,2,1,0:T(8,128)(2,1)S(1)}, bf16[4,2,8,256]{3,2,1,0:T(8,128)(2,1)S(1)}, u32[]{:S(2)}, u32[]{:S(2)}) collective-permute-start(bf16[4,2,8,256]{3,2,1,0:T(8,128)(2,1)S(1)} %get-tuple-element.44), channel_id=1, source_target_pairs={{1,0},{2,1},{3,2},{4,3},{5,4},{6,5},{7,6},{8,7},{9,8},{10,9},{11,1... | collective-permute-start | bytes 98312 | tf_op jit(solution)/shard_map/ppermute | solution.py:603
  28.9 5.8 %collective-permute-done.3.top_ref = bf16[4,2,8,256]{3,2,1,0:T(8,128)(2,1)S(1)} collective-permute-done((bf16[4,2,8,256]{3,2,1,0:T(8,128)(2,1)S(1)}, bf16[4,2,8,256]{3,2,1,0:T(8,128)(2,1)S(1)}, u32[]{:S(2)}, u32[]{:S(2)}) %collective-permute-start.3) | collective-permute-done | bytes 32800 | tf_op jit(solution)/shard_map/ppermute | solution.py:602
  34.7 6.5 %warp_other.1 = (bf16[240,16,128]{2,1,0:T(8,128)(2,1)S(1)}, f32[4,256,128]{2,1,0:T(8,128)S(1)}, f32[4,256,128]{2,1,0:T(8,128)S(1)}, bf16[5,4,256,128]{3,2,1,0:T(8,128)(2,1)}) custom-call(s32[2560]{0:T(1024)S(1)} %reshape.26.place_ref, s32[8]{0:T(128)S(1)} %fusion.order_ref, bf16[256,1920]{1,0:T(8,128)(2,1)S(1)} %bitcast.15, bf16[5,8,4,64,64]{4,3,2,1,0:T(8,128)(2,1)} %interp_hbm.7), custom_call_target="tpu_custom_call" | custom-call | tf_op jit(solution)/shard_map/warp_other/pallas_call | solution.py:222
  41.7 6.1 %warp_mine.1 = (f32[4,256,128]{2,1,0:T(8,128)S(1)}, f32[4,256,128]{2,1,0:T(8,128)S(1)}, bf16[5,4,256,128]{3,2,1,0:T(8,128)(2,1)}) custom-call(s32[2560]{0:T(1024)S(1)} %reshape.26.place_ref, s32[8]{0:T(128)S(1)} %fusion.order_ref, bf16[240,16,128]{2,1,0:T(8,128)(2,1)S(1)} %get-tuple-element.46.blocks_ref, bf16[5,8,4,64,64]{4,3,2,1,0:T(8,128)(2,1)} %interp_hbm.7), custom_call_target="tpu_custom_call" | custom-call | tf_op jit(solution)/shard_map/warp_mine/pallas_call | solution.py:234
  48.0 0.8 collective-permute-start.6
  48.8 0.6 chip_second.1
  49.4 1.6 %collective-permute-start.9 = (f32[3,256,128]{2,1,0:T(8,128)S(1)}, f32[3,256,128]{2,1,0:T(8,128)S(1)}, u32[]{:S(2)}, u32[]{:S(2)}) collective-permute-start(f32[3,256,128]{2,1,0:T(8,128)S(1)} %get-tuple-element.63), channel_id=1, source_target_pairs={{0,64},{32,96},{64,0},{96,32},{1,65},{33,97},{65,1},{97,33},{2,66}... | collective-permute-start | bytes 1179656 | tf_op jit(solution)/shard_map/ppermute | solution.py:586
  51.2 0.9 grad_cost.1.grad_ref
  52.1 5.1 %collective-permute-done.6.there_ref.first_there = bf16[4,256,128]{2,1,0:T(8,128)(2,1)S(1)} collective-permute-done((bf16[4,256,128]{2,1,0:T(8,128)(2,1)S(1)}, bf16[4,256,128]{2,1,0:T(8,128)(2,1)S(1)}, u32[]{:S(2)}, u32[]{:S(2)}) %collective-permute-start.6) | collective-permute-done | bytes 262176 | tf_op jit(solution)/shard_map/ppermute | solution.py:586
  57.4 1.5 %collective-permute-done.8.mean_o = bf16[4,256,128]{2,1,0:T(8,128)(2,1)S(1)} collective-permute-done((bf16[4,256,128]{2,1,0:T(8,128)(2,1)S(1)}, bf16[4,256,128]{2,1,0:T(8,128)(2,1)S(1)}, u32[]{:S(2)}, u32[]{:S(2)}) %collective-permute-start.8) | collective-permute-done | bytes 262176 | tf_op jit(solution)/shard_map/ppermute | solution.py:586
  59.0 6.4 %land.2.rest_0_ = bf16[256,1920]{1,0:T(8,128)(2,1)} custom-call(s32[2560]{0:T(1024)S(1)} %reshape.26.place_ref, s32[8]{0:T(128)S(1)} %fusion.order_ref, bf16[5,4,256,128]{3,2,1,0:T(8,128)(2,1)} %get-tuple-element.60.warped_o, bf16[5,4,256,128]{3,2,1,0:T(8,128)(2,1)} %get-tuple-element.61.warped_m, bf16[5,8,4,64,64]{4,3,2,1,0:T(8,128)(2,1)} %interp_hbm.7, ...), custom_call_target="tpu_custom_call" | custom-call | flops 1000 | bytes 1000 | tf_op jit(solution)/shard_map/land/pallas_call | solution.py:319
  65.4 0.7 cost.1
  66.4 5.1 %land.3 = bf16[256,1920]{1,0:T(8,128)(2,1)} custom-call(s32[2560]{0:T(1024)S(1)} %reshape.26.place_ref, s32[8]{0:T(128)S(1)} %fusion.order_ref, bf16[5,4,256,128]{3,2,1,0:T(8,128)(2,1)} %get-tuple-element.60.warped_o, bf16[5,4,256,128]{3,2,1,0:T(8,128)(2,1)} %get-tuple-element.61.warped_m, ...), custom_call_target="tpu_custom_call", output_to_operand_aliasing={{}: (8, {})} | custom-call | flops 1000 | bytes 1000 | tf_op jit(solution)/shard_map/land/pallas_call | solution.py:319
  72.1 6.3 %all-to-all-start.1 = ((bf16[32,8,1920]{2,1,0:T(8,128)(2,1)}), bf16[32,8,1920]{2,1,0:T(8,128)(2,1)S(1)}, u32[]{:S(2)}, u32[]{:S(2)}) async-start(bf16[32,8,1920]{2,1,0:T(8,128)(2,1)} %bitcast.18), calls=%async_computation.1 | async-start | bytes 1966080 | tf_op jit(solution)/shard_map/all_to_all | solution.py:632
  78.4 3.4 %collective-permute-start.11 = (bf16[4,64,128]{2,1,0:T(8,128)(2,1)S(1)}, bf16[4,64,128]{2,1,0:T(8,128)(2,1)S(1)}, u32[]{:S(2)}, u32[]{:S(2)}) collective-permute-start(bf16[4,64,128]{2,1,0:T(8,128)(2,1)S(1)} %get-tuple-element.74), channel_id=1, source_target_pairs={{0,1},{1,2},{2,3},{3,4},{4,5},{5,6},{6,7},{7,8},{8,9},{9,10},{10,1... | collective-permute-start | bytes 196616 | tf_op jit(solution)/shard_map/ppermute | solution.py:633
  81.8 7.0 %collective-permute-start.12 = (bf16[4,64,128]{2,1,0:T(8,128)(2,1)S(1)}, bf16[4,64,128]{2,1,0:T(8,128)(2,1)S(1)}, u32[]{:S(2)}, u32[]{:S(2)}) collective-permute-start(bf16[4,64,128]{2,1,0:T(8,128)(2,1)S(1)} %get-tuple-element.75), channel_id=1, source_target_pairs={{1,0},{2,1},{3,2},{4,3},{5,4},{6,5},{7,6},{8,7},{9,8},{10,9},{11,1... | collective-permute-start | bytes 196616 | tf_op jit(solution)/shard_map/ppermute | solution.py:634
  88.8 7.4 %collective-permute-done.11.top_ref = bf16[4,64,128]{2,1,0:T(8,128)(2,1)S(1)} collective-permute-done((bf16[4,64,128]{2,1,0:T(8,128)(2,1)S(1)}, bf16[4,64,128]{2,1,0:T(8,128)(2,1)S(1)}, u32[]{:S(2)}, u32[]{:S(2)}) %collective-permute-start.11) | collective-permute-done | bytes 65568 | tf_op jit(solution)/shard_map/ppermute | solution.py:633
  96.1 1.5 %conv.1 = bf16[2,8,1024]{2,1,0:T(8,128)(2,1)} custom-call(bf16[2,256,128]{2,1,0:T(8,128)(2,1)S(1)} %get-tuple-element.70.outer_ref, bf16[1,256,128]{2,1,0:T(8,128)(2,1)S(1)} %get-tuple-element.65.low_ref, bf16[1,256,128]{2,1,0:T(8,128)(2,1)S(1)} %get-tuple-element.66.high_ref, bf16[4,64,128]{2,1,0:T(8,128)(2,1)S(1)} %collective-permute-done.11.top_ref, ...), custom_call_target="tpu_custom_call" | custom-call | tf_op jit(solution)/shard_map/conv/pallas_call | solution.py:560
  97.6 1.5 %unstrips.1 = f32[1280,128]{1,0:T(8,128)} custom-call(bf16[256,1920]{1,0:T(8,128)(2,1)S(1)} %bitcast.16), custom_call_target="tpu_custom_call" | custom-call | tf_op jit(solution)/shard_map/unstrips/pallas_call | solution.py:93
  (42 shorter events, 3.0 us)
Async XLA Ops:
  0.6 6.1 %collective-permute-start = (bf16[2,8,1024]{2,1,0:T(8,128)(2,1)}, bf16[2,8,1024]{2,1,0:T(8,128)(2,1)S(1)}, u32[]{:S(2)}, u32[]{:S(2)}) collective-permute-start(bf16[2,8,1024]{2,1,0:T(8,128)(2,1)} %refs_0_.1), channel_id=1, source_target_pairs={{0,32},{32,0},{64,96},{96,64},{1,33},{33,1},{65,97},{97,65},{2,34}... | collective-permute-start | bytes 98312 | tf_op jit(solution)/shard_map/ppermute | solution.py:586
  0.7 6.0 %collective-permute-start.1 = (bf16[2,8,1024]{2,1,0:T(8,128)(2,1)}, bf16[2,8,1024]{2,1,0:T(8,128)(2,1)S(1)}, u32[]{:S(2)}, u32[]{:S(2)}) collective-permute-start(bf16[2,8,1024]{2,1,0:T(8,128)(2,1)} %refs_0_.1), channel_id=1, source_target_pairs={{0,64},{32,96},{64,0},{96,32},{1,65},{33,97},{65,1},{97,33},{2,66}... | collective-permute-start | bytes 98312 | tf_op jit(solution)/shard_map/ppermute | solution.py:586
  2.4 4.4 %collective-permute-start.2 = (bf16[2,8,1024]{2,1,0:T(8,128)(2,1)}, bf16[2,8,1024]{2,1,0:T(8,128)(2,1)S(1)}, u32[]{:S(2)}, u32[]{:S(2)}) collective-permute-start(bf16[2,8,1024]{2,1,0:T(8,128)(2,1)} %refs_0_.1), channel_id=1, source_target_pairs={{0,96},{32,64},{64,32},{96,0},{1,97},{33,65},{65,33},{97,1},{2,98}... | collective-permute-start | bytes 98312 | tf_op jit(solution)/shard_map/ppermute | solution.py:586
  2.6 1.0 copy-start
  3.6 3.2 %copy-start.2 = (bf16[2,8,1024]{2,1,0:T(8,128)(2,1)S(1)}, bf16[2,8,1024]{2,1,0:T(8,128)(2,1)}, u32[]{:S(2)}) copy-start(bf16[2,8,1024]{2,1,0:T(8,128)(2,1)} %refs_0_.1) | copy-start | bytes 98308
  6.7 10.9 %copy-start.4 = (s32[5,8,16,4]{2,3,1,0:T(4,128)S(1)}, s32[5,8,16,4]{2,3,1,0:T(4,128)}, u32[]{:S(2)}) copy-start(s32[5,8,16,4]{2,3,1,0:T(4,128)} %param.11) | copy-start | bytes 30724
  6.7 10.9 %copy-start.5 = (s32[5,8,16,4]{2,3,1,0:T(4,128)S(1)}, s32[5,8,16,4]{2,3,1,0:T(4,128)}, u32[]{:S(2)}) copy-start(s32[5,8,16,4]{2,3,1,0:T(4,128)} %param.10) | copy-start | bytes 30724
  6.8 21.8 %copy-start.3 = (bf16[3,3,3,8,32]{4,3,2,1,0:T(8,128)(2,1)S(1)}, bf16[3,3,3,8,32]{4,3,2,1,0:T(8,128)(2,1)}, u32[]{:S(2)}) copy-start(bf16[3,3,3,8,32]{4,3,2,1,0:T(8,128)(2,1)} %param.12) | copy-start | bytes 41476
  6.8 27.9 %all-to-all-start = ((bf16[32,8,1920]{2,1,0:T(8,128)(2,1)}), bf16[32,8,1920]{2,1,0:T(8,128)(2,1)S(1)}, u32[]{:S(2)}, u32[]{:S(2)}) async-start(bf16[32,8,1920]{2,1,0:T(8,128)(2,1)} %bitcast.19), calls=%async_computation | async-start | bytes 1966080 | tf_op jit(solution)/shard_map/all_to_all | solution.py:601
  17.7 17.0 %collective-permute-start.3 = (bf16[4,2,8,256]{3,2,1,0:T(8,128)(2,1)S(1)}, bf16[4,2,8,256]{3,2,1,0:T(8,128)(2,1)S(1)}, u32[]{:S(2)}, u32[]{:S(2)}) collective-permute-start(bf16[4,2,8,256]{3,2,1,0:T(8,128)(2,1)S(1)} %get-tuple-element.43), channel_id=1, source_target_pairs={{0,1},{1,2},{2,3},{3,4},{4,5},{5,6},{6,7},{7,8},{8,9},{9,10},{10,1... | collective-permute-start | bytes 98312 | tf_op jit(solution)/shard_map/ppermute | solution.py:602
  21.1 13.6 %collective-permute-start.4 = (bf16[4,2,8,256]{3,2,1,0:T(8,128)(2,1)S(1)}, bf16[4,2,8,256]{3,2,1,0:T(8,128)(2,1)S(1)}, u32[]{:S(2)}, u32[]{:S(2)}) collective-permute-start(bf16[4,2,8,256]{3,2,1,0:T(8,128)(2,1)S(1)} %get-tuple-element.44), channel_id=1, source_target_pairs={{1,0},{2,1},{3,2},{4,3},{5,4},{6,5},{7,6},{8,7},{9,8},{10,9},{11,1... | collective-permute-start | bytes 98312 | tf_op jit(solution)/shard_map/ppermute | solution.py:603
  41.1 6.7 %collective-permute-start.5 = (f32[4,256,128]{2,1,0:T(8,128)S(1)}, f32[4,256,128]{2,1,0:T(8,128)S(1)}, u32[]{:S(2)}, u32[]{:S(2)}) collective-permute-start(f32[4,256,128]{2,1,0:T(8,128)S(1)} %get-tuple-element.48), channel_id=1, source_target_pairs={{0,32},{32,0},{64,96},{96,64},{1,33},{33,1},{65,97},{97,65},{2,34}... | collective-permute-start | bytes 1572872 | tf_op jit(solution)/shard_map/ppermute | solution.py:586
  41.2 7.6 %collective-permute-start.7 = (f32[4,256,128]{2,1,0:T(8,128)S(1)}, f32[4,256,128]{2,1,0:T(8,128)S(1)}, u32[]{:S(2)}, u32[]{:S(2)}) collective-permute-start(f32[4,256,128]{2,1,0:T(8,128)S(1)} %get-tuple-element.52), channel_id=1, source_target_pairs={{0,32},{32,0},{64,96},{96,64},{1,33},{33,1},{65,97},{97,65},{2,34}... | collective-permute-start | bytes 1572872 | tf_op jit(solution)/shard_map/ppermute | solution.py:586
  48.0 9.3 %copy-start.1 = (bf16[32,1024]{1,0:T(8,128)(2,1)S(1)}, bf16[32,1024]{1,0:T(8,128)(2,1)}, u32[]{:S(2)}) copy-start(bf16[32,1024]{1,0:T(8,128)(2,1)} %ref_ref.3) | copy-start | bytes 196612
  48.0 9.2 %collective-permute-start.6 = (bf16[4,256,128]{2,1,0:T(8,128)(2,1)S(1)}, bf16[4,256,128]{2,1,0:T(8,128)(2,1)S(1)}, u32[]{:S(2)}, u32[]{:S(2)}) collective-permute-start(bf16[4,256,128]{2,1,0:T(8,128)(2,1)S(1)} %get-tuple-element.50), channel_id=1, source_target_pairs={{0,64},{32,96},{64,0},{96,32},{1,65},{33,97},{65,1},{97,33},{2,66}... | collective-permute-start | bytes 786440 | tf_op jit(solution)/shard_map/ppermute | solution.py:586
  49.4 15.9 %collective-permute-start.9 = (f32[3,256,128]{2,1,0:T(8,128)S(1)}, f32[3,256,128]{2,1,0:T(8,128)S(1)}, u32[]{:S(2)}, u32[]{:S(2)}) collective-permute-start(f32[3,256,128]{2,1,0:T(8,128)S(1)} %get-tuple-element.63), channel_id=1, source_target_pairs={{0,64},{32,96},{64,0},{96,32},{1,65},{33,97},{65,1},{97,33},{2,66}... | collective-permute-start | bytes 1179656 | tf_op jit(solution)/shard_map/ppermute | solution.py:586
  57.4 1.6 %collective-permute-start.8 = (bf16[4,256,128]{2,1,0:T(8,128)(2,1)S(1)}, bf16[4,256,128]{2,1,0:T(8,128)(2,1)S(1)}, u32[]{:S(2)}, u32[]{:S(2)}) collective-permute-start(bf16[4,256,128]{2,1,0:T(8,128)(2,1)S(1)} %mean.1.mean_m), channel_id=1, source_target_pairs={{0,32},{32,0},{64,96},{96,64},{1,33},{33,1},{65,97},{97,65},{2,34}... | collective-permute-start | bytes 786440 | tf_op jit(solution)/shard_map/ppermute | solution.py:586
  66.1 5.4 %collective-permute-start.10 = (bf16[2,256,128]{2,1,0:T(8,128)(2,1)S(1)}, bf16[2,256,128]{2,1,0:T(8,128)(2,1)S(1)}, u32[]{:S(2)}, u32[]{:S(2)}) collective-permute-start(bf16[2,256,128]{2,1,0:T(8,128)(2,1)S(1)} %get-tuple-element.68), channel_id=1, source_target_pairs={{0,32},{32,0},{64,96},{96,64},{1,33},{33,1},{65,97},{97,65},{2,34}... | collective-permute-start | bytes 393224 | tf_op jit(solution)/shard_map/ppermute | solution.py:586
  72.1 25.5 %all-to-all-start.1 = ((bf16[32,8,1920]{2,1,0:T(8,128)(2,1)}), bf16[32,8,1920]{2,1,0:T(8,128)(2,1)S(1)}, u32[]{:S(2)}, u32[]{:S(2)}) async-start(bf16[32,8,1920]{2,1,0:T(8,128)(2,1)} %bitcast.18), calls=%async_computation.1 | async-start | bytes 1966080 | tf_op jit(solution)/shard_map/all_to_all | solution.py:632
  78.4 17.7 %collective-permute-start.11 = (bf16[4,64,128]{2,1,0:T(8,128)(2,1)S(1)}, bf16[4,64,128]{2,1,0:T(8,128)(2,1)S(1)}, u32[]{:S(2)}, u32[]{:S(2)}) collective-permute-start(bf16[4,64,128]{2,1,0:T(8,128)(2,1)S(1)} %get-tuple-element.74), channel_id=1, source_target_pairs={{0,1},{1,2},{2,3},{3,4},{4,5},{5,6},{6,7},{7,8},{8,9},{9,10},{10,1... | collective-permute-start | bytes 196616 | tf_op jit(solution)/shard_map/ppermute | solution.py:633
  81.8 14.4 %collective-permute-start.12 = (bf16[4,64,128]{2,1,0:T(8,128)(2,1)S(1)}, bf16[4,64,128]{2,1,0:T(8,128)(2,1)S(1)}, u32[]{:S(2)}, u32[]{:S(2)}) collective-permute-start(bf16[4,64,128]{2,1,0:T(8,128)(2,1)S(1)} %get-tuple-element.75), channel_id=1, source_target_pairs={{1,0},{2,1},{3,2},{4,3},{5,4},{6,5},{7,6},{8,7},{9,8},{10,9},{11,1... | collective-permute-start | bytes 196616 | tf_op jit(solution)/shard_map/ppermute | solution.py:634

commit v4 on v2

--- a/solution.py
+++ b/solution.py
@@ -27,10 +27,7 @@
     return pl.BlockSpec(memory_space=pltpu.VMEM)
 
 
-def cost_us(microseconds):
-    return pl.CostEstimate(
-        flops=int(microseconds * 1.0e9), bytes_accessed=int(microseconds * 3.0e6), transcendentals=0
-    )
+SMALL = pl.CostEstimate(flops=1000, bytes_accessed=1000, transcendentals=0)
 
 
 def iota(shape, dim):
@@ -278,7 +275,7 @@
         scratch_shapes=[pltpu.VMEM((SEGS, 16, 128), F32)] * CHAINS,
         input_output_aliases=aliases,
         compiler_params=params(),
-        cost_estimate=cost_us(1.4 * len(views)),
+        cost_estimate=SMALL,
         name="land",
     )(*operands)
 

time: 95.3 us -> 92 us (0.965)
  waiting for transfers between devices: 26.7 us -> 22.7 us
    ppermute x9, waiting for transfers between devices: 13.9 us -> 9.92 us  [other(): return lax.ppermute(array, 'view', [(i, i ^ mask) for i in range(views)])]
  transfers between devices with their start and end apart: 15 -> 15, of which waited for: 6 -> 6; matrix products, arithmetic and copies ran while one was open for 1% -> 1% of each run, Pallas kernels for 15% -> 16%
where the time goes in v4:
time: 92 us; the launch traced here: 91.5 us
  starting transfers between devices  42.8 us (47%)
  waiting for transfers between devices  22.7 us (25%)
  Pallas kernels  21 us (23%)
  local copies, waits for them, and re-layouts  3.8 us (4%)
  between operations  0.93 us (1%)
    all_to_all x1, starting transfers between devices, body(): lax.all_to_all(operand, 'tile', split_axis=0, concat_axis=0, tiled=True)  10.6 us
    ppermute x9, waiting for transfers between devices, other(): return lax.ppermute(array, 'view', [(i, i ^ mask) for i in range(views)])  9.92 us
    ppermute x1, waiting for transfers between devices, body(): cost_top = lax.ppermute(cost_last, 'tile', up)  7.51 us
    pallas_call x2, Pallas kernels, land(): pl.pallas_call(functools.partial(kernel, views), in_specs=specs, out_spec...  7.09 us
    ppermute x1, starting transfers between devices, body(): bottom = lax.ppermute(initial, 'tile', down)  6.98 us
    ppermute x1, starting transfers between devices, body(): cost_bottom = lax.ppermute(cost_initial, 'tile', down)  6.98 us
    all_to_all x1, starting transfers between devices, body(): lax.all_to_all(landed, 'tile', split_axis=0, concat_axis=0, tiled=True)  6.36 us
    ppermute x1, waiting for transfers between devices, body(): top = lax.ppermute(last, 'tile', up)  5.3 us
  transfers between devices with their start and end apart: 15, of which 6 were waited for; matrix products, arithmetic and copies ran while one was open for 1% of the time, Pallas kernels for 16%

profile of v4, /device:TPU:32, one launch (start us, length us, event | category | flops | bytes accessed | tf_op | source)
XLA Modules:
  0.0 91.5 jit_solution(16744598190117509896)
XLA Ops:
  0.7 1.7 %collective-permute-start.1 = (bf16[2,8,1024]{2,1,0:T(8,128)(2,1)}, bf16[2,8,1024]{2,1,0:T(8,128)(2,1)S(1)}, u32[]{:S(2)}, u32[]{:S(2)}) collective-permute-start(bf16[2,8,1024]{2,1,0:T(8,128)(2,1)} %refs_0_.1), channel_id=1, source_target_pairs={{0,64},{32,96},{64,0},{96,32},{1,65},{33,97},{65,1},{97,33},{2,66}... | collective-permute-start | bytes 98312 | tf_op jit(solution)/shard_map/ppermute | solution.py:530
  2.6 1.0 %copy-done.4 = bf16[5,32,8,128]{3,2,1,0:T(8,128)(2,1)S(1)} copy-done((bf16[5,32,8,128]{3,2,1,0:T(8,128)(2,1)S(1)}, bf16[5,32,8,128]{3,2,1,0:T(8,128)(2,1)}, u32[]{:S(2)}) %copy-start.4) | copy-done | bytes 327704
  3.6 1.9 %strips.1 = bf16[256,1920]{1,0:T(8,128)(2,1)} custom-call(bf16[1280,128]{1,0:T(8,128)(2,1)S(1)} %bitcast.17), custom_call_target="tpu_custom_call" | custom-call | tf_op jit(solution)/shard_map/strips/pallas_call | solution.py:68
  6.0 10.6 %all-to-all-start = ((bf16[32,8,1920]{2,1,0:T(8,128)(2,1)}), bf16[32,8,1920]{2,1,0:T(8,128)(2,1)}, u32[]{:S(2)}, u32[]{:S(2)}) async-start(bf16[32,8,1920]{2,1,0:T(8,128)(2,1)} %bitcast.3), calls=%async_computation | async-start | bytes 1966080 | tf_op jit(solution)/shard_map/all_to_all | solution.py:545
  16.6 3.5 %collective-permute-start.3 = (bf16[4,2,8,256]{3,2,1,0:T(8,128)(2,1)S(1)}, bf16[4,2,8,256]{3,2,1,0:T(8,128)(2,1)S(1)}, u32[]{:S(2)}, u32[]{:S(2)}) collective-permute-start(bf16[4,2,8,256]{3,2,1,0:T(8,128)(2,1)S(1)} %get-tuple-element.41), channel_id=1, source_target_pairs={{0,1},{1,2},{2,3},{3,4},{4,5},{5,6},{6,7},{7,8},{8,9},{9,10},{10,1... | collective-permute-start | bytes 98312 | tf_op jit(solution)/shard_map/ppermute | solution.py:546
  20.2 7.0 %collective-permute-start.4 = (bf16[4,2,8,256]{3,2,1,0:T(8,128)(2,1)S(1)}, bf16[4,2,8,256]{3,2,1,0:T(8,128)(2,1)S(1)}, u32[]{:S(2)}, u32[]{:S(2)}) collective-permute-start(bf16[4,2,8,256]{3,2,1,0:T(8,128)(2,1)S(1)} %get-tuple-element.42), channel_id=1, source_target_pairs={{1,0},{2,1},{3,2},{4,3},{5,4},{6,5},{7,6},{8,7},{9,8},{10,9},{11,1... | collective-permute-start | bytes 98312 | tf_op jit(solution)/shard_map/ppermute | solution.py:547
  28.1 5.3 %collective-permute-done.3.top_ref = bf16[4,2,8,256]{3,2,1,0:T(8,128)(2,1)S(1)} collective-permute-done((bf16[4,2,8,256]{3,2,1,0:T(8,128)(2,1)S(1)}, bf16[4,2,8,256]{3,2,1,0:T(8,128)(2,1)S(1)}, u32[]{:S(2)}, u32[]{:S(2)}) %collective-permute-start.3) | collective-permute-done | bytes 32800 | tf_op jit(solution)/shard_map/ppermute | solution.py:546
  33.4 0.9 grad_cost.1.refs_7_
  34.3 1.0 %copy-done.1 = f32[8,256,128]{2,1,0:T(8,128)} copy-done((f32[8,256,128]{2,1,0:T(8,128)}, f32[8,256,128]{2,1,0:T(8,128)S(1)}, u32[]{:S(2)}) %copy-start.1) | copy-done | bytes 1048600
  35.3 3.6 %warp_other.1 = (bf16[240,16,128]{2,1,0:T(8,128)(2,1)S(1)}, f32[4,256,128]{2,1,0:T(8,128)S(1)}, f32[4,256,128]{2,1,0:T(8,128)S(1)}, bf16[5,4,256,128]{3,2,1,0:T(8,128)(2,1)S(1)}) custom-call(s32[2560]{0:T(1024)S(1)} %reshape.26.place_ref.refs_0_, s32[8]{0:T(128)S(1)} %fusion.order_ref.refs_1_, bf16[256,1920]{1,0:T(8,128)(2,1)} %bitcast.4.in_ref, ...), custom_call_target="tpu_custom_call" | custom-call | tf_op jit(solution)/shard_map/warp_other/pallas_call | solution.py:192
  39.4 2.5 %warp_mine.1 = (f32[4,256,128]{2,1,0:T(8,128)S(1)}, f32[4,256,128]{2,1,0:T(8,128)S(1)}, bf16[5,4,256,128]{3,2,1,0:T(8,128)(2,1)S(1)}) custom-call(s32[2560]{0:T(1024)S(1)} %reshape.26.place_ref.refs_0_, s32[8]{0:T(128)S(1)} %fusion.order_ref.refs_1_, bf16[240,16,128]{2,1,0:T(8,128)(2,1)S(1)} %get-tuple-element.44.blocks_ref, ...), custom_call_target="tpu_custom_call" | custom-call | tf_op jit(solution)/shard_map/warp_mine/pallas_call | solution.py:203
  43.5 1.4 %collective-permute-start.9 = (f32[3,256,128]{2,1,0:T(8,128)S(1)}, f32[3,256,128]{2,1,0:T(8,128)S(1)}, u32[]{:S(2)}, u32[]{:S(2)}) collective-permute-start(f32[3,256,128]{2,1,0:T(8,128)S(1)} %get-tuple-element.57), channel_id=1, source_target_pairs={{0,64},{32,96},{64,0},{96,32},{1,65},{33,97},{65,1},{97,33},{2,66}... | collective-permute-start | bytes 1179656 | tf_op jit(solution)/shard_map/ppermute | solution.py:530
  44.9 6.3 %collective-permute-done.6.there_ref.first_there = bf16[4,256,128]{2,1,0:T(8,128)(2,1)S(1)} collective-permute-done((bf16[4,256,128]{2,1,0:T(8,128)(2,1)S(1)}, bf16[4,256,128]{2,1,0:T(8,128)(2,1)S(1)}, u32[]{:S(2)}, u32[]{:S(2)}) %collective-permute-start.6) | collective-permute-done | bytes 262176 | tf_op jit(solution)/shard_map/ppermute | solution.py:530
  51.7 1.5 %collective-permute-done.8.refs_5_ = bf16[4,256,128]{2,1,0:T(8,128)(2,1)S(1)} collective-permute-done((bf16[4,256,128]{2,1,0:T(8,128)(2,1)S(1)}, bf16[4,256,128]{2,1,0:T(8,128)(2,1)S(1)}, u32[]{:S(2)}, u32[]{:S(2)}) %collective-permute-start.8) | collective-permute-done | bytes 262176 | tf_op jit(solution)/shard_map/ppermute | solution.py:530
  53.2 4.1 %land.2.refs_8_ = bf16[256,1920]{1,0:T(8,128)(2,1)S(1)} custom-call(s32[2560]{0:T(1024)S(1)} %reshape.26.place_ref.refs_0_, s32[8]{0:T(128)S(1)} %fusion.order_ref.refs_1_, bf16[5,4,256,128]{3,2,1,0:T(8,128)(2,1)S(1)} %get-tuple-element.54.refs_2_, bf16[5,4,256,128]{3,2,1,0:T(8,128)(2,1)S(1)} %get-tuple-element.55.refs_3_, ...), custom_call_target="tpu_custom_call" | custom-call | flops 1000 | bytes 1000 | tf_op jit(solution)/shard_map/land/pallas_call | solution.py:270
  57.3 1.5 %collective-permute-done.9.second_there = f32[3,256,128]{2,1,0:T(8,128)S(1)} collective-permute-done((f32[3,256,128]{2,1,0:T(8,128)S(1)}, f32[3,256,128]{2,1,0:T(8,128)S(1)}, u32[]{:S(2)}, u32[]{:S(2)}) %collective-permute-start.9) | collective-permute-done | bytes 393248 | tf_op jit(solution)/shard_map/ppermute | solution.py:530
  59.7 3.0 %land.3 = bf16[256,1920]{1,0:T(8,128)(2,1)S(1)} custom-call(s32[2560]{0:T(1024)S(1)} %reshape.26.place_ref.refs_0_, s32[8]{0:T(128)S(1)} %fusion.order_ref.refs_1_, bf16[5,4,256,128]{3,2,1,0:T(8,128)(2,1)S(1)} %get-tuple-element.54.refs_2_, bf16[5,4,256,128]{3,2,1,0:T(8,128)(2,1)S(1)} %get-tuple-element.55.refs_3_, ...), custom_call_target="tpu_custom_call", output_to_operand_aliasing={{}: (8, {})} | custom-call | flops 1000 | bytes 1000 | tf_op jit(solution)/shard_map/land/pallas_call | solution.py:270
  62.7 0.9 %copy-done.3 = bf16[256,1920]{1,0:T(8,128)(2,1)} copy-done((bf16[256,1920]{1,0:T(8,128)(2,1)}, bf16[256,1920]{1,0:T(8,128)(2,1)S(1)}, u32[]{:S(2)}) %copy-start.3) | copy-done | bytes 983064
  64.2 6.4 %all-to-all-start.1 = ((bf16[32,8,1920]{2,1,0:T(8,128)(2,1)}), bf16[32,8,1920]{2,1,0:T(8,128)(2,1)S(1)}, u32[]{:S(2)}, u32[]{:S(2)}) async-start(bf16[32,8,1920]{2,1,0:T(8,128)(2,1)} %bitcast.15), calls=%async_computation.1 | async-start | bytes 1966080 | tf_op jit(solution)/shard_map/all_to_all | solution.py:574
  70.6 3.4 %collective-permute-start.11 = (bf16[4,64,128]{2,1,0:T(8,128)(2,1)S(1)}, bf16[4,64,128]{2,1,0:T(8,128)(2,1)S(1)}, u32[]{:S(2)}, u32[]{:S(2)}) collective-permute-start(bf16[4,64,128]{2,1,0:T(8,128)(2,1)S(1)} %get-tuple-element.68), channel_id=1, source_target_pairs={{0,1},{1,2},{2,3},{3,4},{4,5},{5,6},{6,7},{7,8},{8,9},{9,10},{10,1... | collective-permute-start | bytes 196616 | tf_op jit(solution)/shard_map/ppermute | solution.py:575
  74.0 7.0 %collective-permute-start.12 = (bf16[4,64,128]{2,1,0:T(8,128)(2,1)S(1)}, bf16[4,64,128]{2,1,0:T(8,128)(2,1)S(1)}, u32[]{:S(2)}, u32[]{:S(2)}) collective-permute-start(bf16[4,64,128]{2,1,0:T(8,128)(2,1)S(1)} %get-tuple-element.69), channel_id=1, source_target_pairs={{1,0},{2,1},{3,2},{4,3},{5,4},{6,5},{7,6},{8,7},{9,8},{10,9},{11,1... | collective-permute-start | bytes 196616 | tf_op jit(solution)/shard_map/ppermute | solution.py:576
  81.0 7.5 %collective-permute-done.11.top_ref = bf16[4,64,128]{2,1,0:T(8,128)(2,1)S(1)} collective-permute-done((bf16[4,64,128]{2,1,0:T(8,128)(2,1)S(1)}, bf16[4,64,128]{2,1,0:T(8,128)(2,1)S(1)}, u32[]{:S(2)}, u32[]{:S(2)}) %collective-permute-start.11) | collective-permute-done | bytes 65568 | tf_op jit(solution)/shard_map/ppermute | solution.py:575
  88.5 1.5 %conv.1 = bf16[2,8,1024]{2,1,0:T(8,128)(2,1)} custom-call(bf16[2,256,128]{2,1,0:T(8,128)(2,1)S(1)} %get-tuple-element.64.outer_ref, bf16[1,256,128]{2,1,0:T(8,128)(2,1)S(1)} %get-tuple-element.59.low_ref, bf16[1,256,128]{2,1,0:T(8,128)(2,1)S(1)} %get-tuple-element.60.high_ref, bf16[4,64,128]{2,1,0:T(8,128)(2,1)S(1)} %collective-permute-done.11.top_ref, ...), custom_call_target="tpu_custom_call" | custom-call | tf_op jit(solution)/shard_map/conv/pallas_call | solution.py:504
  89.9 1.5 %unstrips.1 = f32[1280,128]{1,0:T(8,128)} custom-call(bf16[256,1920]{1,0:T(8,128)(2,1)S(1)} %bitcast.16), custom_call_target="tpu_custom_call" | custom-call | tf_op jit(solution)/shard_map/unstrips/pallas_call | solution.py:99
  (50 shorter events, 5.7 us)
Async XLA Ops:
  0.6 4.8 %collective-permute-start = (bf16[2,8,1024]{2,1,0:T(8,128)(2,1)}, bf16[2,8,1024]{2,1,0:T(8,128)(2,1)S(1)}, u32[]{:S(2)}, u32[]{:S(2)}) collective-permute-start(bf16[2,8,1024]{2,1,0:T(8,128)(2,1)} %refs_0_.1), channel_id=1, source_target_pairs={{0,32},{32,0},{64,96},{96,64},{1,33},{33,1},{65,97},{97,65},{2,34}... | collective-permute-start | bytes 98312 | tf_op jit(solution)/shard_map/ppermute | solution.py:530
  0.7 4.7 %collective-permute-start.1 = (bf16[2,8,1024]{2,1,0:T(8,128)(2,1)}, bf16[2,8,1024]{2,1,0:T(8,128)(2,1)S(1)}, u32[]{:S(2)}, u32[]{:S(2)}) collective-permute-start(bf16[2,8,1024]{2,1,0:T(8,128)(2,1)} %refs_0_.1), channel_id=1, source_target_pairs={{0,64},{32,96},{64,0},{96,32},{1,65},{33,97},{65,1},{97,33},{2,66}... | collective-permute-start | bytes 98312 | tf_op jit(solution)/shard_map/ppermute | solution.py:530
  2.4 3.6 %collective-permute-start.2 = (bf16[2,8,1024]{2,1,0:T(8,128)(2,1)}, bf16[2,8,1024]{2,1,0:T(8,128)(2,1)S(1)}, u32[]{:S(2)}, u32[]{:S(2)}) collective-permute-start(bf16[2,8,1024]{2,1,0:T(8,128)(2,1)} %refs_0_.1), channel_id=1, source_target_pairs={{0,96},{32,64},{64,32},{96,0},{1,97},{33,65},{65,33},{97,1},{2,98}... | collective-permute-start | bytes 98312 | tf_op jit(solution)/shard_map/ppermute | solution.py:530
  2.6 1.0 %copy-start.4 = (bf16[5,32,8,128]{3,2,1,0:T(8,128)(2,1)S(1)}, bf16[5,32,8,128]{3,2,1,0:T(8,128)(2,1)}, u32[]{:S(2)}) copy-start(bf16[5,32,8,128]{3,2,1,0:T(8,128)(2,1)} %param.7) | copy-start | bytes 983044
  3.6 2.4 %copy-start.6 = (bf16[2,8,1024]{2,1,0:T(8,128)(2,1)S(1)}, bf16[2,8,1024]{2,1,0:T(8,128)(2,1)}, u32[]{:S(2)}) copy-start(bf16[2,8,1024]{2,1,0:T(8,128)(2,1)} %refs_0_.1) | copy-start | bytes 98308
  5.4 11.1 %copy-start.8 = (s32[5,8,16,4]{2,3,1,0:T(4,128)S(1)}, s32[5,8,16,4]{2,3,1,0:T(4,128)}, u32[]{:S(2)}) copy-start(s32[5,8,16,4]{2,3,1,0:T(4,128)} %param.11) | copy-start | bytes 30724
  5.4 11.2 %copy-start.9 = (s32[5,8,16,4]{2,3,1,0:T(4,128)S(1)}, s32[5,8,16,4]{2,3,1,0:T(4,128)}, u32[]{:S(2)}) copy-start(s32[5,8,16,4]{2,3,1,0:T(4,128)} %param.10) | copy-start | bytes 30724
  6.0 21.7 %copy-start.7 = (bf16[3,3,3,8,32]{4,3,2,1,0:T(8,128)(2,1)S(1)}, bf16[3,3,3,8,32]{4,3,2,1,0:T(8,128)(2,1)}, u32[]{:S(2)}) copy-start(bf16[3,3,3,8,32]{4,3,2,1,0:T(8,128)(2,1)} %param.12) | copy-start | bytes 41476
  6.0 29.3 %all-to-all-start = ((bf16[32,8,1920]{2,1,0:T(8,128)(2,1)}), bf16[32,8,1920]{2,1,0:T(8,128)(2,1)}, u32[]{:S(2)}, u32[]{:S(2)}) async-start(bf16[32,8,1920]{2,1,0:T(8,128)(2,1)} %bitcast.3), calls=%async_computation | async-start | bytes 1966080 | tf_op jit(solution)/shard_map/all_to_all | solution.py:545
  16.6 18.7 %copy-start = (bf16[5,8,4,64,64]{4,3,2,1,0:T(8,128)(2,1)S(1)}, bf16[5,8,4,64,64]{4,3,2,1,0:T(8,128)(2,1)}, u32[]{:S(2)}) copy-start(bf16[5,8,4,64,64]{4,3,2,1,0:T(8,128)(2,1)} %refs_4_.3) | copy-start | bytes 3932164
  16.6 16.7 %collective-permute-start.3 = (bf16[4,2,8,256]{3,2,1,0:T(8,128)(2,1)S(1)}, bf16[4,2,8,256]{3,2,1,0:T(8,128)(2,1)S(1)}, u32[]{:S(2)}, u32[]{:S(2)}) collective-permute-start(bf16[4,2,8,256]{3,2,1,0:T(8,128)(2,1)S(1)} %get-tuple-element.41), channel_id=1, source_target_pairs={{0,1},{1,2},{2,3},{3,4},{4,5},{5,6},{6,7},{7,8},{8,9},{9,10},{10,1... | collective-permute-start | bytes 98312 | tf_op jit(solution)/shard_map/ppermute | solution.py:546
  20.2 13.2 %collective-permute-start.4 = (bf16[4,2,8,256]{3,2,1,0:T(8,128)(2,1)S(1)}, bf16[4,2,8,256]{3,2,1,0:T(8,128)(2,1)S(1)}, u32[]{:S(2)}, u32[]{:S(2)}) collective-permute-start(bf16[4,2,8,256]{3,2,1,0:T(8,128)(2,1)S(1)} %get-tuple-element.42), channel_id=1, source_target_pairs={{1,0},{2,1},{3,2},{4,3},{5,4},{6,5},{7,6},{8,7},{9,8},{10,9},{11,1... | collective-permute-start | bytes 98312 | tf_op jit(solution)/shard_map/ppermute | solution.py:547
  34.3 1.0 %copy-start.1 = (f32[8,256,128]{2,1,0:T(8,128)}, f32[8,256,128]{2,1,0:T(8,128)S(1)}, u32[]{:S(2)}) copy-start(f32[8,256,128]{2,1,0:T(8,128)S(1)} %grad_cost.1.refs_7_) | copy-start | bytes 3145732
  38.8 3.1 %collective-permute-start.5 = (f32[4,256,128]{2,1,0:T(8,128)S(1)}, f32[4,256,128]{2,1,0:T(8,128)S(1)}, u32[]{:S(2)}, u32[]{:S(2)}) collective-permute-start(f32[4,256,128]{2,1,0:T(8,128)S(1)} %get-tuple-element.46), channel_id=1, source_target_pairs={{0,32},{32,0},{64,96},{96,64},{1,33},{33,1},{65,97},{97,65},{2,34}... | collective-permute-start | bytes 1572872 | tf_op jit(solution)/shard_map/ppermute | solution.py:530
  38.9 3.9 %collective-permute-start.7 = (f32[4,256,128]{2,1,0:T(8,128)S(1)}, f32[4,256,128]{2,1,0:T(8,128)S(1)}, u32[]{:S(2)}, u32[]{:S(2)}) collective-permute-start(f32[4,256,128]{2,1,0:T(8,128)S(1)} %get-tuple-element.50), channel_id=1, source_target_pairs={{0,32},{32,0},{64,96},{96,64},{1,33},{33,1},{65,97},{97,65},{2,34}... | collective-permute-start | bytes 1572872 | tf_op jit(solution)/shard_map/ppermute | solution.py:530
  41.9 9.3 %copy-start.5 = (bf16[32,1024]{1,0:T(8,128)(2,1)S(1)}, bf16[32,1024]{1,0:T(8,128)(2,1)}, u32[]{:S(2)}) copy-start(bf16[32,1024]{1,0:T(8,128)(2,1)} %ref_ref.3) | copy-start | bytes 196612
  42.0 11.2 %copy-start.2 = (f32[8,256,128]{2,1,0:T(8,128)S(1)}, f32[8,256,128]{2,1,0:T(8,128)}, u32[]{:S(2)}) copy-start(f32[8,256,128]{2,1,0:T(8,128)} %copy-done.1) | copy-start | bytes 3145732
  42.0 9.2 %collective-permute-start.6 = (bf16[4,256,128]{2,1,0:T(8,128)(2,1)S(1)}, bf16[4,256,128]{2,1,0:T(8,128)(2,1)S(1)}, u32[]{:S(2)}, u32[]{:S(2)}) collective-permute-start(bf16[4,256,128]{2,1,0:T(8,128)(2,1)S(1)} %get-tuple-element.48), channel_id=1, source_target_pairs={{0,64},{32,96},{64,0},{96,32},{1,65},{33,97},{65,1},{97,33},{2,66}... | collective-permute-start | bytes 786440 | tf_op jit(solution)/shard_map/ppermute | solution.py:530
  43.5 15.3 %collective-permute-start.9 = (f32[3,256,128]{2,1,0:T(8,128)S(1)}, f32[3,256,128]{2,1,0:T(8,128)S(1)}, u32[]{:S(2)}, u32[]{:S(2)}) collective-permute-start(f32[3,256,128]{2,1,0:T(8,128)S(1)} %get-tuple-element.57), channel_id=1, source_target_pairs={{0,64},{32,96},{64,0},{96,32},{1,65},{33,97},{65,1},{97,33},{2,66}... | collective-permute-start | bytes 1179656 | tf_op jit(solution)/shard_map/ppermute | solution.py:530
  51.4 1.8 %collective-permute-start.8 = (bf16[4,256,128]{2,1,0:T(8,128)(2,1)S(1)}, bf16[4,256,128]{2,1,0:T(8,128)(2,1)S(1)}, u32[]{:S(2)}, u32[]{:S(2)}) collective-permute-start(bf16[4,256,128]{2,1,0:T(8,128)(2,1)S(1)} %mean.1.refs_6_), channel_id=1, source_target_pairs={{0,32},{32,0},{64,96},{96,64},{1,33},{33,1},{65,97},{97,65},{2,34}... | collective-permute-start | bytes 786440 | tf_op jit(solution)/shard_map/ppermute | solution.py:530
  59.6 4.1 %collective-permute-start.10 = (bf16[2,256,128]{2,1,0:T(8,128)(2,1)S(1)}, bf16[2,256,128]{2,1,0:T(8,128)(2,1)S(1)}, u32[]{:S(2)}, u32[]{:S(2)}) collective-permute-start(bf16[2,256,128]{2,1,0:T(8,128)(2,1)S(1)} %get-tuple-element.62), channel_id=1, source_target_pairs={{0,32},{32,0},{64,96},{96,64},{1,33},{33,1},{65,97},{97,65},{2,34}... | collective-permute-start | bytes 393224 | tf_op jit(solution)/shard_map/ppermute | solution.py:530
  64.2 25.7 %all-to-all-start.1 = ((bf16[32,8,1920]{2,1,0:T(8,128)(2,1)}), bf16[32,8,1920]{2,1,0:T(8,128)(2,1)S(1)}, u32[]{:S(2)}, u32[]{:S(2)}) async-start(bf16[32,8,1920]{2,1,0:T(8,128)(2,1)} %bitcast.15), calls=%async_computation.1 | async-start | bytes 1966080 | tf_op jit(solution)/shard_map/all_to_all | solution.py:574
  70.6 17.9 %collective-permute-start.11 = (bf16[4,64,128]{2,1,0:T(8,128)(2,1)S(1)}, bf16[4,64,128]{2,1,0:T(8,128)(2,1)S(1)}, u32[]{:S(2)}, u32[]{:S(2)}) collective-permute-start(bf16[4,64,128]{2,1,0:T(8,128)(2,1)S(1)} %get-tuple-element.68), channel_id=1, source_target_pairs={{0,1},{1,2},{2,3},{3,4},{4,5},{5,6},{6,7},{7,8},{8,9},{9,10},{10,1... | collective-permute-start | bytes 196616 | tf_op jit(solution)/shard_map/ppermute | solution.py:575
  74.0 14.5 %collective-permute-start.12 = (bf16[4,64,128]{2,1,0:T(8,128)(2,1)S(1)}, bf16[4,64,128]{2,1,0:T(8,128)(2,1)S(1)}, u32[]{:S(2)}, u32[]{:S(2)}) collective-permute-start(bf16[4,64,128]{2,1,0:T(8,128)(2,1)S(1)} %get-tuple-element.69), channel_id=1, source_target_pairs={{1,0},{2,1},{3,2},{4,3},{5,4},{6,5},{7,6},{8,7},{9,8},{10,9},{11,1... | collective-permute-start | bytes 196616 | tf_op jit(solution)/shard_map/ppermute | solution.py:576
  (1 other events, 1.0 us)

commit v5 on v4

--- a/solution.py
+++ b/solution.py
@@ -244,39 +244,56 @@
                 columns_low.append(low)
             bands.append(jnp.concatenate(columns_up, axis=1))
             bands.append(jnp.concatenate(columns_low, axis=1))
-        out_ref[:, view * 384 : (view + 1) * 384] = jnp.concatenate(bands, axis=0).T.astype(BF)
+        lane = (view - views[0]) * 384
+        out_ref[:, lane : lane + 384] = jnp.concatenate(bands, axis=0).T.astype(BF)
 
 
 def land_first_kernel(views, *refs):
     land_views(views, *refs[:9], refs[9:])
 
 
-def land_next_kernel(views, *refs):
-    land_views(views, *refs[:8], refs[9], refs[10:])
-
-
-LANDED = jax.ShapeDtypeStruct((256, VIEWS * 384), BF)
-
-
-def land(views, place, order, warped_o, warped_m, interp, mean_o, mean_m, grad, earlier=None):
-    operands = [place, order, warped_o, warped_m, interp, mean_o, mean_m, grad]
-    specs = [smem(), smem()] + [whole()] * 6
-    if earlier is None:
-        kernel, aliases = land_first_kernel, {}
-    else:
-        kernel, aliases = land_next_kernel, {8: 0}
-        operands.append(earlier)
-        specs.append(whole())
-    return pl.pallas_call(
-        functools.partial(kernel, views),
-        in_specs=specs,
+def land_last_kernel(views, *refs):
+    earlier_ref, out_hbm, own_ref, sem = refs[8], refs[9], refs[10], refs[11]
+    lanes = earlier_ref.shape[1]
+    first = pltpu.make_async_copy(earlier_ref, out_hbm.at[:, 0:lanes], sem.at[0])
+    first.start()
+    land_views(views, *refs[:8], own_ref, refs[12:])
+    last = pltpu.make_async_copy(own_ref, out_hbm.at[:, lanes : VIEWS * 384], sem.at[1])
+    last.start()
+    first.wait()
+    last.wait()
+
+
+ACCUMULATORS = [pltpu.VMEM((SEGS, 16, 128), F32)] * CHAINS
+
+
+def land_first(views, *operands):
+    return pl.pallas_call(
+        functools.partial(land_first_kernel, views),
+        in_specs=[smem(), smem()] + [whole()] * 6,
         out_specs=whole(),
-        out_shape=LANDED,
-        scratch_shapes=[pltpu.VMEM((SEGS, 16, 128), F32)] * CHAINS,
-        input_output_aliases=aliases,
+        out_shape=jax.ShapeDtypeStruct((256, len(views) * 384), BF),
+        scratch_shapes=ACCUMULATORS,
         compiler_params=params(),
         cost_estimate=SMALL,
-        name="land",
+        name="land_first",
+    )(*operands)
+
+
+def land_last(views, *operands):
+    return pl.pallas_call(
+        functools.partial(land_last_kernel, views),
+        in_specs=[smem(), smem()] + [whole()] * 7,
+        out_specs=pl.BlockSpec(memory_space=pltpu.HBM),
+        out_shape=pltpu.HBM((256, VIEWS * 384), BF),
+        scratch_shapes=[
+            pltpu.VMEM((256, len(views) * 384), BF),
+            pltpu.SemaphoreType.DMA((2,)),
+        ]
+        + ACCUMULATORS,
+        compiler_params=params(),
+        cost_estimate=SMALL,
+        name="land_last",
     )(*operands)
 
 
@@ -430,7 +447,9 @@
     return jnp.where(col == 0, 0.0, pltpu.roll(values, 1, 1))
 
 
-def grad_cost_kernel(view_ref, own_ref, top_ref, bottom_ref, weight_ref, out_ref):
+def grad_cost_kernel(
+    view_ref, own_ref, top_ref, bottom_ref, weight_ref, out_hbm, out_ref, sem
+):
     view = view_ref[0]
     padded = []
     for plane in range(PLANES):
@@ -446,6 +465,7 @@
         padded.append(jnp.concatenate([shifted(line, 1), line, shifted(line, -1)], axis=0))
     zero = jnp.zeros_like(padded[0])
     weight = weight_ref[...]
+    stores = []
     for plane in range(PLANES):
         near = [padded[p] if 0 <= p < PLANES else zero for p in (plane + 1, plane, plane - 1)]
         result = lax.dot_general(
@@ -459,14 +479,23 @@
             even, odd = pair_swap(upper, lower)
             out_ref[plane, pair * 32 : pair * 32 + 16] = even
             out_ref[plane, pair * 32 + 16 : pair * 32 + 32] = odd
+        if plane % 4 == 3:
+            part = pl.ds(plane - 3, 4)
+            stores.append(
+                pltpu.make_async_copy(out_ref.at[part], out_hbm.at[part], sem.at[plane // 4])
+            )
+            stores[-1].start()
+    for store in stores:
+        store.wait()
 
 
 def grad_cost(view, own, top, bottom, weight):
     return pl.pallas_call(
         grad_cost_kernel,
-        out_shape=jax.ShapeDtypeStruct((PLANES, 256, 128), F32),
+        out_shape=pltpu.HBM((PLANES, 256, 128), F32),
         in_specs=[pl.BlockSpec(memory_space=pltpu.SMEM)] + [whole()] * 4,
-        out_specs=whole(),
+        out_specs=pl.BlockSpec(memory_space=pltpu.HBM),
+        scratch_shapes=[pltpu.VMEM((PLANES, 256, 128), F32), pltpu.SemaphoreType.DMA((2,))],
         compiler_params=params(),
         name="grad_cost",
     )(view, own, top, bottom, weight)
@@ -561,13 +590,13 @@
     mean_other = other(mean_mine, 1)
 
     shared = (place, order, warped_o, warped_m, interp, mean_other, mean_mine, grad)
-    landed = land((0, 1, 2), *shared)
+    landed = land_first((0, 1, 2, 3), *shared)
     landed, second_there = lax.optimization_barrier((landed, second_there))
     low, high, send = cost_of(
         where, first_chip, first_there, second_own, second_there, reference_features
     )
     near = other(send, 1)
-    landed = land((3, 4), *shared, landed)
+    landed = land_last((4,), *shared, landed)
     landed, near = lax.optimization_barrier((landed, near))
     outer, cost_last, cost_initial = edges_of(where, low, high, near)
     landed, cost_last, cost_initial = lax.optimization_barrier((landed, cost_last, cost_initial))

time: 92 us -> 90.7 us (0.986)
  local copies, waits for them, and re-layouts: 3.8 us -> 1.88 us
  Pallas kernels: 21 us -> 22.9 us
  waiting for transfers between devices: 22.7 us -> 21.6 us
    unnamed x20 -> x16, local copies, waits for them, and re-layouts: 2.92 us -> 1.01 us
    pallas_call x3, Pallas kernels: 7.98 us -> 9.81 us  [the longest x1 5.3 us: land_first(): pl.pallas_call(functools.partial(land_first_kernel, views), in_specs=[sme...]
    ppermute x9, waiting for transfers between devices: 9.92 us -> 8.73 us  [other(): return lax.ppermute(array, 'view', [(i, i ^ mask) for i in range(views)])]
  transfers between devices with their start and end apart: 15 -> 15, of which waited for: 6 -> 6; matrix products, arithmetic and copies ran while one was open for 1% -> 1% of each run, Pallas kernels for 16% -> 18%
where the time goes in v5:
time: 90.7 us; the launch traced here: 90.2 us
  starting transfers between devices  42.8 us (47%)
  Pallas kernels  22.9 us (25%)
  waiting for transfers between devices  21.6 us (24%)
  local copies, waits for them, and re-layouts  1.88 us (2%)
  between operations  0.93 us (1%)
    all_to_all x1, starting transfers between devices, body(): lax.all_to_all(operand, 'tile', split_axis=0, concat_axis=0, tiled=True)  10.6 us
    ppermute x9, waiting for transfers between devices, other(): return lax.ppermute(array, 'view', [(i, i ^ mask) for i in range(views)])  8.73 us
    ppermute x1, waiting for transfers between devices, body(): cost_top = lax.ppermute(cost_last, 'tile', up)  7.52 us
    ppermute x1, starting transfers between devices, body(): bottom = lax.ppermute(initial, 'tile', down)  6.98 us
    ppermute x1, starting transfers between devices, body(): cost_bottom = lax.ppermute(cost_initial, 'tile', down)  6.98 us
    all_to_all x1, starting transfers between devices, body(): lax.all_to_all(landed, 'tile', split_axis=0, concat_axis=0, tiled=True)  6.33 us
    pallas_call x1, Pallas kernels, land_first(): pl.pallas_call(functools.partial(land_first_kernel, views), in_specs=[sme...  5.3 us
    ppermute x1, waiting for transfers between devices, body(): top = lax.ppermute(last, 'tile', up)  5.29 us
  transfers between devices with their start and end apart: 15, of which 6 were waited for; matrix products, arithmetic and copies ran while one was open for 1% of the time, Pallas kernels for 18%

profile of v5, /device:TPU:32, one launch (start us, length us, event | category | flops | bytes accessed | tf_op | source)
XLA Modules:
  0.0 90.2 jit_solution(6242814474516813235)
XLA Ops:
  0.7 1.7 %collective-permute-start.1 = (bf16[2,8,1024]{2,1,0:T(8,128)(2,1)}, bf16[2,8,1024]{2,1,0:T(8,128)(2,1)S(1)}, u32[]{:S(2)}, u32[]{:S(2)}) collective-permute-start(bf16[2,8,1024]{2,1,0:T(8,128)(2,1)} %refs_0_.1), channel_id=1, source_target_pairs={{0,64},{32,96},{64,0},{96,32},{1,65},{33,97},{65,1},{97,33},{2,66}... | collective-permute-start | bytes 98312 | tf_op jit(solution)/shard_map/ppermute | solution.py:559
  2.6 1.0 %copy-done.2 = bf16[5,32,8,128]{3,2,1,0:T(8,128)(2,1)S(1)} copy-done((bf16[5,32,8,128]{3,2,1,0:T(8,128)(2,1)S(1)}, bf16[5,32,8,128]{3,2,1,0:T(8,128)(2,1)}, u32[]{:S(2)}) %copy-start.2) | copy-done | bytes 327704
  3.6 1.9 %strips.1 = bf16[256,1920]{1,0:T(8,128)(2,1)} custom-call(bf16[1280,128]{1,0:T(8,128)(2,1)S(1)} %bitcast.16), custom_call_target="tpu_custom_call" | custom-call | tf_op jit(solution)/shard_map/strips/pallas_call | solution.py:68
  6.0 10.6 %all-to-all-start = ((bf16[32,8,1920]{2,1,0:T(8,128)(2,1)}), bf16[32,8,1920]{2,1,0:T(8,128)(2,1)}, u32[]{:S(2)}, u32[]{:S(2)}) async-start(bf16[32,8,1920]{2,1,0:T(8,128)(2,1)} %bitcast.3), calls=%async_computation | async-start | bytes 1966080 | tf_op jit(solution)/shard_map/all_to_all | solution.py:574
  16.6 3.5 %collective-permute-start.3 = (bf16[4,2,8,256]{3,2,1,0:T(8,128)(2,1)S(1)}, bf16[4,2,8,256]{3,2,1,0:T(8,128)(2,1)S(1)}, u32[]{:S(2)}, u32[]{:S(2)}) collective-permute-start(bf16[4,2,8,256]{3,2,1,0:T(8,128)(2,1)S(1)} %get-tuple-element.41), channel_id=1, source_target_pairs={{0,1},{1,2},{2,3},{3,4},{4,5},{5,6},{6,7},{7,8},{8,9},{9,10},{10,1... | collective-permute-start | bytes 98312 | tf_op jit(solution)/shard_map/ppermute | solution.py:575
  20.2 7.0 %collective-permute-start.4 = (bf16[4,2,8,256]{3,2,1,0:T(8,128)(2,1)S(1)}, bf16[4,2,8,256]{3,2,1,0:T(8,128)(2,1)S(1)}, u32[]{:S(2)}, u32[]{:S(2)}) collective-permute-start(bf16[4,2,8,256]{3,2,1,0:T(8,128)(2,1)S(1)} %get-tuple-element.42), channel_id=1, source_target_pairs={{1,0},{2,1},{3,2},{4,3},{5,4},{6,5},{7,6},{8,7},{9,8},{10,9},{11,1... | collective-permute-start | bytes 98312 | tf_op jit(solution)/shard_map/ppermute | solution.py:576
  28.1 5.3 %collective-permute-done.3.top_ref = bf16[4,2,8,256]{3,2,1,0:T(8,128)(2,1)S(1)} collective-permute-done((bf16[4,2,8,256]{3,2,1,0:T(8,128)(2,1)S(1)}, bf16[4,2,8,256]{3,2,1,0:T(8,128)(2,1)S(1)}, u32[]{:S(2)}, u32[]{:S(2)}) %collective-permute-start.3) | collective-permute-done | bytes 32800 | tf_op jit(solution)/shard_map/ppermute | solution.py:575
  33.4 1.7 %grad_cost.1.refs_7_ = f32[8,256,128]{2,1,0:T(8,128)} custom-call(s32[1]{0:T(128)} %bitcast.5.view_ref, bf16[4,2,8,1024]{3,2,1,0:T(8,128)(2,1)S(1)} %get-tuple-element.40.own_ref, bf16[4,2,8,256]{3,2,1,0:T(8,128)(2,1)S(1)} %collective-permute-done.3.top_ref, bf16[4,2,8,256]{3,2,1,0:T(8,128)(2,1)S(1)} %collective-permute-done.4.bottom_ref, ...), custom_call_target="tpu_custom_call" | custom-call | tf_op jit(solution)/shard_map/grad_cost/pallas_call | solution.py:493
  35.1 3.6 %warp_other.1 = (bf16[240,16,128]{2,1,0:T(8,128)(2,1)S(1)}, f32[4,256,128]{2,1,0:T(8,128)S(1)}, f32[4,256,128]{2,1,0:T(8,128)S(1)}, bf16[5,4,256,128]{3,2,1,0:T(8,128)(2,1)S(1)}) custom-call(s32[2560]{0:T(1024)S(1)} %reshape.26.place_ref.refs_0_, s32[8]{0:T(128)S(1)} %fusion.order_ref.refs_1_, bf16[256,1920]{1,0:T(8,128)(2,1)} %bitcast.4.in_ref, ...), custom_call_target="tpu_custom_call" | custom-call | tf_op jit(solution)/shard_map/warp_other/pallas_call | solution.py:192
  39.3 2.5 %warp_mine.1 = (f32[4,256,128]{2,1,0:T(8,128)S(1)}, f32[4,256,128]{2,1,0:T(8,128)S(1)}, bf16[5,4,256,128]{3,2,1,0:T(8,128)(2,1)S(1)}) custom-call(s32[2560]{0:T(1024)S(1)} %reshape.26.place_ref.refs_0_, s32[8]{0:T(128)S(1)} %fusion.order_ref.refs_1_, bf16[240,16,128]{2,1,0:T(8,128)(2,1)S(1)} %get-tuple-element.44.blocks_ref, ...), custom_call_target="tpu_custom_call" | custom-call | tf_op jit(solution)/shard_map/warp_mine/pallas_call | solution.py:203
  42.0 0.8 collective-permute-start.6
  42.8 0.6 chip_second.1
  43.4 1.4 %collective-permute-start.9 = (f32[3,256,128]{2,1,0:T(8,128)S(1)}, f32[3,256,128]{2,1,0:T(8,128)S(1)}, u32[]{:S(2)}, u32[]{:S(2)}) collective-permute-start(f32[3,256,128]{2,1,0:T(8,128)S(1)} %get-tuple-element.57), channel_id=1, source_target_pairs={{0,64},{32,96},{64,0},{96,32},{1,65},{33,97},{65,1},{97,33},{2,66}... | collective-permute-start | bytes 1179656 | tf_op jit(solution)/shard_map/ppermute | solution.py:559
  44.9 6.3 %collective-permute-done.6.there_ref.first_there = bf16[4,256,128]{2,1,0:T(8,128)(2,1)S(1)} collective-permute-done((bf16[4,256,128]{2,1,0:T(8,128)(2,1)S(1)}, bf16[4,256,128]{2,1,0:T(8,128)(2,1)S(1)}, u32[]{:S(2)}, u32[]{:S(2)}) %collective-permute-start.6) | collective-permute-done | bytes 262176 | tf_op jit(solution)/shard_map/ppermute | solution.py:559
  51.6 1.5 %collective-permute-done.8.refs_5_ = bf16[4,256,128]{2,1,0:T(8,128)(2,1)S(1)} collective-permute-done((bf16[4,256,128]{2,1,0:T(8,128)(2,1)S(1)}, bf16[4,256,128]{2,1,0:T(8,128)(2,1)S(1)}, u32[]{:S(2)}, u32[]{:S(2)}) %collective-permute-start.8) | collective-permute-done | bytes 262176 | tf_op jit(solution)/shard_map/ppermute | solution.py:559
  53.1 5.3 %land_first.1.refs_8_ = bf16[256,1536]{1,0:T(8,128)(2,1)S(1)} custom-call(s32[2560]{0:T(1024)S(1)} %reshape.26.place_ref.refs_0_, s32[8]{0:T(128)S(1)} %fusion.order_ref.refs_1_, bf16[5,4,256,128]{3,2,1,0:T(8,128)(2,1)S(1)} %get-tuple-element.54.refs_2_, bf16[5,4,256,128]{3,2,1,0:T(8,128)(2,1)S(1)} %get-tuple-element.55.refs_3_, ...), custom_call_target="tpu_custom_call" | custom-call | flops 1000 | bytes 1000 | tf_op jit(solution)/shard_map/land_first/pallas_call | solution.py:271
  58.8 0.7 cost.1
  59.6 2.8 %land_last.1 = bf16[256,1920]{1,0:T(8,128)(2,1)} custom-call(s32[2560]{0:T(1024)S(1)} %reshape.26.place_ref.refs_0_, s32[8]{0:T(128)S(1)} %fusion.order_ref.refs_1_, bf16[5,4,256,128]{3,2,1,0:T(8,128)(2,1)S(1)} %get-tuple-element.54.refs_2_, bf16[5,4,256,128]{3,2,1,0:T(8,128)(2,1)S(1)} %get-tuple-element.55.refs_3_, bf16[5,8,4,64,64]{4,3,2,1,0:T(8,128)(2,1)S(1)} %copy-done, ...), custom_call_target="tpu_custom_call" | custom-call | flops 1000 | bytes 1000 | tf_op jit(solution)/shard_map/land_last/pallas_call | solution.py:284
  63.0 6.3 %all-to-all-start.1 = ((bf16[32,8,1920]{2,1,0:T(8,128)(2,1)}), bf16[32,8,1920]{2,1,0:T(8,128)(2,1)S(1)}, u32[]{:S(2)}, u32[]{:S(2)}) async-start(bf16[32,8,1920]{2,1,0:T(8,128)(2,1)} %bitcast.17), calls=%async_computation.1 | async-start | bytes 1966080 | tf_op jit(solution)/shard_map/all_to_all | solution.py:603
  69.3 3.4 %collective-permute-start.11 = (bf16[4,64,128]{2,1,0:T(8,128)(2,1)S(1)}, bf16[4,64,128]{2,1,0:T(8,128)(2,1)S(1)}, u32[]{:S(2)}, u32[]{:S(2)}) collective-permute-start(bf16[4,64,128]{2,1,0:T(8,128)(2,1)S(1)} %get-tuple-element.68), channel_id=1, source_target_pairs={{0,1},{1,2},{2,3},{3,4},{4,5},{5,6},{6,7},{7,8},{8,9},{9,10},{10,1... | collective-permute-start | bytes 196616 | tf_op jit(solution)/shard_map/ppermute | solution.py:604
  72.7 7.0 %collective-permute-start.12 = (bf16[4,64,128]{2,1,0:T(8,128)(2,1)S(1)}, bf16[4,64,128]{2,1,0:T(8,128)(2,1)S(1)}, u32[]{:S(2)}, u32[]{:S(2)}) collective-permute-start(bf16[4,64,128]{2,1,0:T(8,128)(2,1)S(1)} %get-tuple-element.69), channel_id=1, source_target_pairs={{1,0},{2,1},{3,2},{4,3},{5,4},{6,5},{7,6},{8,7},{9,8},{10,9},{11,1... | collective-permute-start | bytes 196616 | tf_op jit(solution)/shard_map/ppermute | solution.py:605
  79.7 7.5 %collective-permute-done.11.top_ref = bf16[4,64,128]{2,1,0:T(8,128)(2,1)S(1)} collective-permute-done((bf16[4,64,128]{2,1,0:T(8,128)(2,1)S(1)}, bf16[4,64,128]{2,1,0:T(8,128)(2,1)S(1)}, u32[]{:S(2)}, u32[]{:S(2)}) %collective-permute-start.11) | collective-permute-done | bytes 65568 | tf_op jit(solution)/shard_map/ppermute | solution.py:604
  87.2 1.5 %conv.1 = bf16[2,8,1024]{2,1,0:T(8,128)(2,1)} custom-call(bf16[2,256,128]{2,1,0:T(8,128)(2,1)S(1)} %get-tuple-element.64.outer_ref, bf16[1,256,128]{2,1,0:T(8,128)(2,1)S(1)} %get-tuple-element.59.low_ref, bf16[1,256,128]{2,1,0:T(8,128)(2,1)S(1)} %get-tuple-element.60.high_ref, bf16[4,64,128]{2,1,0:T(8,128)(2,1)S(1)} %collective-permute-done.11.top_ref, ...), custom_call_target="tpu_custom_call" | custom-call | tf_op jit(solution)/shard_map/conv/pallas_call | solution.py:533
  88.7 1.5 %unstrips.1 = f32[1280,128]{1,0:T(8,128)} custom-call(bf16[256,1920]{1,0:T(8,128)(2,1)S(1)} %bitcast.15), custom_call_target="tpu_custom_call" | custom-call | tf_op jit(solution)/shard_map/unstrips/pallas_call | solution.py:99
  (46 shorter events, 3.9 us)
Async XLA Ops:
  0.6 4.8 %collective-permute-start = (bf16[2,8,1024]{2,1,0:T(8,128)(2,1)}, bf16[2,8,1024]{2,1,0:T(8,128)(2,1)S(1)}, u32[]{:S(2)}, u32[]{:S(2)}) collective-permute-start(bf16[2,8,1024]{2,1,0:T(8,128)(2,1)} %refs_0_.1), channel_id=1, source_target_pairs={{0,32},{32,0},{64,96},{96,64},{1,33},{33,1},{65,97},{97,65},{2,34}... | collective-permute-start | bytes 98312 | tf_op jit(solution)/shard_map/ppermute | solution.py:559
  0.7 4.7 %collective-permute-start.1 = (bf16[2,8,1024]{2,1,0:T(8,128)(2,1)}, bf16[2,8,1024]{2,1,0:T(8,128)(2,1)S(1)}, u32[]{:S(2)}, u32[]{:S(2)}) collective-permute-start(bf16[2,8,1024]{2,1,0:T(8,128)(2,1)} %refs_0_.1), channel_id=1, source_target_pairs={{0,64},{32,96},{64,0},{96,32},{1,65},{33,97},{65,1},{97,33},{2,66}... | collective-permute-start | bytes 98312 | tf_op jit(solution)/shard_map/ppermute | solution.py:559
  2.4 3.6 %collective-permute-start.2 = (bf16[2,8,1024]{2,1,0:T(8,128)(2,1)}, bf16[2,8,1024]{2,1,0:T(8,128)(2,1)S(1)}, u32[]{:S(2)}, u32[]{:S(2)}) collective-permute-start(bf16[2,8,1024]{2,1,0:T(8,128)(2,1)} %refs_0_.1), channel_id=1, source_target_pairs={{0,96},{32,64},{64,32},{96,0},{1,97},{33,65},{65,33},{97,1},{2,98}... | collective-permute-start | bytes 98312 | tf_op jit(solution)/shard_map/ppermute | solution.py:559
  2.6 1.0 %copy-start.2 = (bf16[5,32,8,128]{3,2,1,0:T(8,128)(2,1)S(1)}, bf16[5,32,8,128]{3,2,1,0:T(8,128)(2,1)}, u32[]{:S(2)}) copy-start(bf16[5,32,8,128]{3,2,1,0:T(8,128)(2,1)} %param.7) | copy-start | bytes 983044
  3.6 2.4 %copy-start.4 = (bf16[2,8,1024]{2,1,0:T(8,128)(2,1)S(1)}, bf16[2,8,1024]{2,1,0:T(8,128)(2,1)}, u32[]{:S(2)}) copy-start(bf16[2,8,1024]{2,1,0:T(8,128)(2,1)} %refs_0_.1) | copy-start | bytes 98308
  5.4 11.2 %copy-start.6 = (s32[5,8,16,4]{2,3,1,0:T(4,128)S(1)}, s32[5,8,16,4]{2,3,1,0:T(4,128)}, u32[]{:S(2)}) copy-start(s32[5,8,16,4]{2,3,1,0:T(4,128)} %param.11) | copy-start | bytes 30724
  5.4 11.2 %copy-start.7 = (s32[5,8,16,4]{2,3,1,0:T(4,128)S(1)}, s32[5,8,16,4]{2,3,1,0:T(4,128)}, u32[]{:S(2)}) copy-start(s32[5,8,16,4]{2,3,1,0:T(4,128)} %param.10) | copy-start | bytes 30724
  6.0 21.7 %copy-start.5 = (bf16[3,3,3,8,32]{4,3,2,1,0:T(8,128)(2,1)S(1)}, bf16[3,3,3,8,32]{4,3,2,1,0:T(8,128)(2,1)}, u32[]{:S(2)}) copy-start(bf16[3,3,3,8,32]{4,3,2,1,0:T(8,128)(2,1)} %param.12) | copy-start | bytes 41476
  6.0 29.1 %all-to-all-start = ((bf16[32,8,1920]{2,1,0:T(8,128)(2,1)}), bf16[32,8,1920]{2,1,0:T(8,128)(2,1)}, u32[]{:S(2)}, u32[]{:S(2)}) async-start(bf16[32,8,1920]{2,1,0:T(8,128)(2,1)} %bitcast.3), calls=%async_computation | async-start | bytes 1966080 | tf_op jit(solution)/shard_map/all_to_all | solution.py:574
  16.6 18.5 %copy-start = (bf16[5,8,4,64,64]{4,3,2,1,0:T(8,128)(2,1)S(1)}, bf16[5,8,4,64,64]{4,3,2,1,0:T(8,128)(2,1)}, u32[]{:S(2)}) copy-start(bf16[5,8,4,64,64]{4,3,2,1,0:T(8,128)(2,1)} %refs_4_.3) | copy-start | bytes 3932164
  16.6 16.7 %collective-permute-start.3 = (bf16[4,2,8,256]{3,2,1,0:T(8,128)(2,1)S(1)}, bf16[4,2,8,256]{3,2,1,0:T(8,128)(2,1)S(1)}, u32[]{:S(2)}, u32[]{:S(2)}) collective-permute-start(bf16[4,2,8,256]{3,2,1,0:T(8,128)(2,1)S(1)} %get-tuple-element.41), channel_id=1, source_target_pairs={{0,1},{1,2},{2,3},{3,4},{4,5},{5,6},{6,7},{7,8},{8,9},{9,10},{10,1... | collective-permute-start | bytes 98312 | tf_op jit(solution)/shard_map/ppermute | solution.py:575
  20.2 13.2 %collective-permute-start.4 = (bf16[4,2,8,256]{3,2,1,0:T(8,128)(2,1)S(1)}, bf16[4,2,8,256]{3,2,1,0:T(8,128)(2,1)S(1)}, u32[]{:S(2)}, u32[]{:S(2)}) collective-permute-start(bf16[4,2,8,256]{3,2,1,0:T(8,128)(2,1)S(1)} %get-tuple-element.42), channel_id=1, source_target_pairs={{1,0},{2,1},{3,2},{4,3},{5,4},{6,5},{7,6},{8,7},{9,8},{10,9},{11,1... | collective-permute-start | bytes 98312 | tf_op jit(solution)/shard_map/ppermute | solution.py:576
  38.7 3.1 %collective-permute-start.5 = (f32[4,256,128]{2,1,0:T(8,128)S(1)}, f32[4,256,128]{2,1,0:T(8,128)S(1)}, u32[]{:S(2)}, u32[]{:S(2)}) collective-permute-start(f32[4,256,128]{2,1,0:T(8,128)S(1)} %get-tuple-element.46), channel_id=1, source_target_pairs={{0,32},{32,0},{64,96},{96,64},{1,33},{33,1},{65,97},{97,65},{2,34}... | collective-permute-start | bytes 1572872 | tf_op jit(solution)/shard_map/ppermute | solution.py:559
  38.8 4.0 %collective-permute-start.7 = (f32[4,256,128]{2,1,0:T(8,128)S(1)}, f32[4,256,128]{2,1,0:T(8,128)S(1)}, u32[]{:S(2)}, u32[]{:S(2)}) collective-permute-start(f32[4,256,128]{2,1,0:T(8,128)S(1)} %get-tuple-element.50), channel_id=1, source_target_pairs={{0,32},{32,0},{64,96},{96,64},{1,33},{33,1},{65,97},{97,65},{2,34}... | collective-permute-start | bytes 1572872 | tf_op jit(solution)/shard_map/ppermute | solution.py:559
  41.8 9.4 %copy-start.3 = (bf16[32,1024]{1,0:T(8,128)(2,1)S(1)}, bf16[32,1024]{1,0:T(8,128)(2,1)}, u32[]{:S(2)}) copy-start(bf16[32,1024]{1,0:T(8,128)(2,1)} %ref_ref.3) | copy-start | bytes 196612
  42.0 11.2 %copy-start.1 = (f32[8,256,128]{2,1,0:T(8,128)S(1)}, f32[8,256,128]{2,1,0:T(8,128)}, u32[]{:S(2)}) copy-start(f32[8,256,128]{2,1,0:T(8,128)} %grad_cost.1.refs_7_) | copy-start | bytes 3145732
  42.0 9.2 %collective-permute-start.6 = (bf16[4,256,128]{2,1,0:T(8,128)(2,1)S(1)}, bf16[4,256,128]{2,1,0:T(8,128)(2,1)S(1)}, u32[]{:S(2)}, u32[]{:S(2)}) collective-permute-start(bf16[4,256,128]{2,1,0:T(8,128)(2,1)S(1)} %get-tuple-element.48), channel_id=1, source_target_pairs={{0,64},{32,96},{64,0},{96,32},{1,65},{33,97},{65,1},{97,33},{2,66}... | collective-permute-start | bytes 786440 | tf_op jit(solution)/shard_map/ppermute | solution.py:559
  43.4 15.3 %collective-permute-start.9 = (f32[3,256,128]{2,1,0:T(8,128)S(1)}, f32[3,256,128]{2,1,0:T(8,128)S(1)}, u32[]{:S(2)}, u32[]{:S(2)}) collective-permute-start(f32[3,256,128]{2,1,0:T(8,128)S(1)} %get-tuple-element.57), channel_id=1, source_target_pairs={{0,64},{32,96},{64,0},{96,32},{1,65},{33,97},{65,1},{97,33},{2,66}... | collective-permute-start | bytes 1179656 | tf_op jit(solution)/shard_map/ppermute | solution.py:559
  51.3 1.8 %collective-permute-start.8 = (bf16[4,256,128]{2,1,0:T(8,128)(2,1)S(1)}, bf16[4,256,128]{2,1,0:T(8,128)(2,1)S(1)}, u32[]{:S(2)}, u32[]{:S(2)}) collective-permute-start(bf16[4,256,128]{2,1,0:T(8,128)(2,1)S(1)} %mean.1.refs_6_), channel_id=1, source_target_pairs={{0,32},{32,0},{64,96},{96,64},{1,33},{33,1},{65,97},{97,65},{2,34}... | collective-permute-start | bytes 786440 | tf_op jit(solution)/shard_map/ppermute | solution.py:559
  59.5 2.9 %collective-permute-start.10 = (bf16[2,256,128]{2,1,0:T(8,128)(2,1)S(1)}, bf16[2,256,128]{2,1,0:T(8,128)(2,1)S(1)}, u32[]{:S(2)}, u32[]{:S(2)}) collective-permute-start(bf16[2,256,128]{2,1,0:T(8,128)(2,1)S(1)} %get-tuple-element.62), channel_id=1, source_target_pairs={{0,32},{32,0},{64,96},{96,64},{1,33},{33,1},{65,97},{97,65},{2,34}... | collective-permute-start | bytes 393224 | tf_op jit(solution)/shard_map/ppermute | solution.py:559
  63.0 25.7 %all-to-all-start.1 = ((bf16[32,8,1920]{2,1,0:T(8,128)(2,1)}), bf16[32,8,1920]{2,1,0:T(8,128)(2,1)S(1)}, u32[]{:S(2)}, u32[]{:S(2)}) async-start(bf16[32,8,1920]{2,1,0:T(8,128)(2,1)} %bitcast.17), calls=%async_computation.1 | async-start | bytes 1966080 | tf_op jit(solution)/shard_map/all_to_all | solution.py:603
  69.3 17.9 %collective-permute-start.11 = (bf16[4,64,128]{2,1,0:T(8,128)(2,1)S(1)}, bf16[4,64,128]{2,1,0:T(8,128)(2,1)S(1)}, u32[]{:S(2)}, u32[]{:S(2)}) collective-permute-start(bf16[4,64,128]{2,1,0:T(8,128)(2,1)S(1)} %get-tuple-element.68), channel_id=1, source_target_pairs={{0,1},{1,2},{2,3},{3,4},{4,5},{5,6},{6,7},{7,8},{8,9},{9,10},{10,1... | collective-permute-start | bytes 196616 | tf_op jit(solution)/shard_map/ppermute | solution.py:604
  72.7 14.5 %collective-permute-start.12 = (bf16[4,64,128]{2,1,0:T(8,128)(2,1)S(1)}, bf16[4,64,128]{2,1,0:T(8,128)(2,1)S(1)}, u32[]{:S(2)}, u32[]{:S(2)}) collective-permute-start(bf16[4,64,128]{2,1,0:T(8,128)(2,1)S(1)} %get-tuple-element.69), channel_id=1, source_target_pairs={{1,0},{2,1},{3,2},{4,3},{5,4},{6,5},{7,6},{8,7},{9,8},{10,9},{11,1... | collective-permute-start | bytes 196616 | tf_op jit(solution)/shard_map/ppermute | solution.py:605

commit v6 on v5

--- a/solution.py
+++ b/solution.py
@@ -43,37 +43,55 @@
     return (iota((128, 128), 0) >> 5) == (iota((128, 128), 1) & 3)
 
 
-def strips_kernel(src_ref, out_ref, wide, stage):
-    wide[...] = src_ref[...].astype(F32)
+def strips_kernel(src_hbm, out_hbm, source, wide, stage, moved_out, in_sem, out_sem):
+    loads = []
+    for v in range(VIEWS):
+        rows = pl.ds(v * 256, 256)
+        loads.append(pltpu.make_async_copy(src_hbm.at[rows], source.at[rows], in_sem.at[v]))
+        loads[-1].start()
     table = band_table()
     mask = row_mask()
-    for x in range(8):
-        own = wide[pl.ds(x, 160, stride=8), :]
-        parts = []
-        for v in range(VIEWS):
-            part = own[v * 32 : (v + 1) * 32]
-            parts.append(jnp.where(mask, jnp.concatenate([part] * 4, axis=0), 0.0).astype(BF))
-        stacked = jnp.concatenate(parts, axis=0)
-        moved = lax.dot_general(table, stacked, NT, preferred_element_type=F32)
-        for v in range(VIEWS):
+    stores = []
+    for v in range(VIEWS):
+        loads[v].wait()
+        wide[v] = source[v * 256 : (v + 1) * 256].astype(F32)
+        for x in range(8):
+            own = wide[v, pl.ds(x, 32, stride=8), :]
+            tall = jnp.where(mask, jnp.concatenate([own] * 4, axis=0), 0.0).astype(BF)
+            moved = lax.dot_general(table, tall, NT, preferred_element_type=F32)
             for band in range(3):
                 stage[v * 3 + band, pl.ds(x, 32, stride=8), :] = moved[
-                    band * 32 : (band + 1) * 32, v * 128 : (v + 1) * 128
+                    band * 32 : (band + 1) * 32
                 ]
-    for piece in range(VIEWS * 3):
-        out_ref[:, piece * 128 : (piece + 1) * 128] = stage[piece].astype(BF)
+        for band in range(3):
+            moved_out[v, :, band * 128 : (band + 1) * 128] = stage[v * 3 + band].astype(BF)
+        stores.append(
+            pltpu.make_async_copy(
+                moved_out.at[v], out_hbm.at[:, v * 384 : (v + 1) * 384], out_sem.at[v]
+            )
+        )
+        stores[-1].start()
+    for store in stores:
+        store.wait()
 
 
 def strips(source):
     return pl.pallas_call(
         strips_kernel,
-        out_shape=jax.ShapeDtypeStruct((256, VIEWS * 384), BF),
-        in_specs=[whole()],
-        out_specs=whole(),
-        scratch_shapes=[pltpu.VMEM((1280, 128), F32), pltpu.VMEM((VIEWS * 3, 256, 128), F32)],
-        compiler_params=params(),
+        out_shape=pltpu.HBM((256, VIEWS * 384), BF),
+        in_specs=[pl.BlockSpec(memory_space=pltpu.HBM)],
+        out_specs=pl.BlockSpec(memory_space=pltpu.HBM),
+        scratch_shapes=[
+            pltpu.VMEM((1280, 128), BF),
+            pltpu.VMEM((VIEWS, 256, 128), F32),
+            pltpu.VMEM((VIEWS * 3, 256, 128), F32),
+            pltpu.VMEM((VIEWS, 256, 384), BF),
+            pltpu.SemaphoreType.DMA((VIEWS,)),
+            pltpu.SemaphoreType.DMA((VIEWS,)),
+        ],
+        compiler_params=pltpu.CompilerParams(vmem_limit_bytes=2 * VMEM_LIMIT),
         name="strips",
-    )(source)
+    )(pltpu.with_memory_space_constraint(source, pltpu.HBM))
 
 
 def unstrips_kernel(in_ref, out_ref, wide):
@@ -501,43 +519,82 @@
     )(view, own, top, bottom, weight)
 
 
-def conv_kernel(outer_ref, low_ref, high_ref, top_ref, bottom_ref, weight_ref, out_ref):
+def line_of(tall, pairs):
+    upper, lower = [], []
+    for pair in range(pairs):
+        up, low = pair_swap(
+            tall[pair * 32 : pair * 32 + 16], tall[pair * 32 + 16 : pair * 32 + 32]
+        )
+        upper.append(up)
+        lower.append(low)
+    return jnp.concatenate(
+        [jnp.concatenate(upper, axis=1), jnp.concatenate(lower, axis=1)], axis=0
+    )
+
+
+def convolved(weight, line):
+    wide = jnp.concatenate([shifted(line, -1), line, shifted(line, 1)], axis=0).astype(BF)
+    return lax.dot_general(weight, wide, NN, preferred_element_type=F32)
+
+
+def conv_kernel(outer_ref, low_ref, high_ref, weight_ref, out_ref):
+    weight = weight_ref[...]
+    results = []
+    for plane in (outer_ref[0], low_ref[0], high_ref[0], outer_ref[1]):
+        results.append(convolved(weight, line_of(plane.astype(F32), 8)))
+    zero = jnp.zeros((8, 256), F32)
+    for plane in range(2):
+        total = None
+        for a in range(3):
+            same = results[plane + a][a * 24 + 8 : a * 24 + 16]
+            above = results[plane + a][a * 24 : a * 24 + 8, 0:768]
+            below = results[plane + a][a * 24 + 16 : a * 24 + 24, 256:1024]
+            part = (
+                same
+                + jnp.concatenate([zero, above], axis=1)
+                + jnp.concatenate([below, zero], axis=1)
+            )
+            total = part if total is None else total + part
+        out_ref[plane] = total
+
+
+def conv_rows_kernel(main_ref, top_ref, bottom_ref, weight_ref, out_ref):
     weight = weight_ref[...]
     results = []
     for local in range(4):
-        middle = (outer_ref, low_ref, high_ref, outer_ref)[local][1 if local == 3 else 0]
-        tall = jnp.concatenate([top_ref[local], middle, bottom_ref[local]], axis=0).astype(F32)
-        upper, lower = [], []
-        for pair in range(12):
-            even = tall[pair * 32 : pair * 32 + 16]
-            odd = tall[pair * 32 + 16 : pair * 32 + 32]
-            up, low = pair_swap(even, odd)
-            upper.append(up)
-            lower.append(low)
-        line = jnp.concatenate(
-            [jnp.concatenate(upper, axis=1), jnp.concatenate(lower, axis=1)], axis=0
-        )
-        wide = jnp.concatenate([shifted(line, -1), line, shifted(line, 1)], axis=0).astype(BF)
-        results.append(lax.dot_general(weight, wide, NN, preferred_element_type=F32))
+        tall = jnp.concatenate([top_ref[local], bottom_ref[local]], axis=0).astype(F32)
+        results.append(convolved(weight, line_of(tall, 4)))
     for plane in range(2):
-        total = None
+        first = main_ref[plane, :, 0:256]
+        last = main_ref[plane, :, 768:1024]
         for a in range(3):
-            for b in range(3):
-                at = (a * 3 + b) * 8
-                part = results[plane + a][at : at + 8, b * 256 : b * 256 + 1024]
-                total = part if total is None else total + part
-        out_ref[plane] = total.astype(BF)
-
-
-def conv(outer, low, high, top, bottom, weight):
+            first = first + results[plane + a][a * 24 : a * 24 + 8, 0:256]
+            last = last + results[plane + a][a * 24 + 16 : a * 24 + 24, 256:512]
+        out_ref[plane] = jnp.concatenate(
+            [first, main_ref[plane, :, 256:768], last], axis=1
+        ).astype(BF)
+
+
+def conv(outer, low, high, weight):
     return pl.pallas_call(
         conv_kernel,
+        out_shape=jax.ShapeDtypeStruct((2, 8, 1024), F32),
+        in_specs=[whole()] * 4,
+        out_specs=whole(),
+        compiler_params=params(),
+        name="conv",
+    )(outer, low, high, weight)
+
+
+def conv_rows(main, top, bottom, weight):
+    return pl.pallas_call(
+        conv_rows_kernel,
         out_shape=jax.ShapeDtypeStruct((2, 8, 1024), BF),
-        in_specs=[whole()] * 6,
+        in_specs=[whole()] * 4,
         out_specs=whole(),
         compiler_params=params(),
-        name="conv",
-    )(outer, low, high, top, bottom, weight)
+        name="conv_rows",
+    )(main, top, bottom, weight)
 
 
 def body(
@@ -603,7 +660,7 @@
     returned = lax.all_to_all(landed, "tile", split_axis=0, concat_axis=0, tiled=True)
     cost_top = lax.ppermute(cost_last, "tile", up)
     cost_bottom = lax.ppermute(cost_initial, "tile", down)
-    regularized = conv(outer, low, high, cost_top, cost_bottom, weight)
+    regularized = conv_rows(conv(outer, low, high, weight), cost_top, cost_bottom, weight)
 
     grad_source = unstrips(returned).reshape(source_features.shape)
     return regularized, grad_source

time: 90.7 us -> 90.7 us (level)
  Pallas kernels: 22.9 us -> 24.5 us
  local copies, waits for them, and re-layouts: 1.88 us -> 0.92 us
    pallas_call x1 -> x2, Pallas kernels: 1.86 us -> 4.31 us  [the longest x1 3.27 us: strips(): pl.pallas_call(strips_kernel, out_shape=pltpu.HBM((256, VIEWS * 384), BF)...]
    unnamed x16 -> x14, local copies, waits for them, and re-layouts: 1.01 us -> 0.04 us
  transfers between devices with their start and end apart: 15 -> 15, of which waited for: 6 -> 5; matrix products, arithmetic and copies ran while one was open for 1% -> 1% of each run, Pallas kernels for 18% -> 20%
where the time goes in v6:
time: 90.7 us; the launch traced here: 90.2 us
  starting transfers between devices  43.1 us (48%)
  Pallas kernels  24.5 us (27%)
  waiting for transfers between devices  20.7 us (23%)
  between operations  0.97 us (1%)
  local copies, waits for them, and re-layouts  0.92 us (1%)
    all_to_all x1, starting transfers between devices, body(): lax.all_to_all(operand, 'tile', split_axis=0, concat_axis=0, tiled=True)  10.9 us
    ppermute x9, waiting for transfers between devices, other(): return lax.ppermute(array, 'view', [(i, i ^ mask) for i in range(views)])  8.26 us
    ppermute x1, starting transfers between devices, body(): bottom = lax.ppermute(initial, 'tile', down)  6.98 us
    ppermute x1, starting transfers between devices, body(): cost_bottom = lax.ppermute(cost_initial, 'tile', down)  6.98 us
    ppermute x1, waiting for transfers between devices, body(): cost_top = lax.ppermute(cost_last, 'tile', up)  6.92 us
    all_to_all x1, starting transfers between devices, body(): lax.all_to_all(landed, 'tile', split_axis=0, concat_axis=0, tiled=True)  6.29 us
    ppermute x1, waiting for transfers between devices, body(): top = lax.ppermute(last, 'tile', up)  5.47 us
    pallas_call x1, Pallas kernels, land_first(): pl.pallas_call(functools.partial(land_first_kernel, views), in_specs=[sme...  5.28 us
  transfers between devices with their start and end apart: 15, of which 5 were waited for; matrix products, arithmetic and copies ran while one was open for 1% of the time, Pallas kernels for 20%

profile of v6, /device:TPU:32, one launch (start us, length us, event | category | flops | bytes accessed | tf_op | source)
XLA Modules:
  0.0 90.2 jit_solution(11042323979501823750)
XLA Ops:
  0.7 1.7 %collective-permute-start.1 = (bf16[2,8,1024]{2,1,0:T(8,128)(2,1)}, bf16[2,8,1024]{2,1,0:T(8,128)(2,1)S(1)}, u32[]{:S(2)}, u32[]{:S(2)}) collective-permute-start(bf16[2,8,1024]{2,1,0:T(8,128)(2,1)} %refs_0_.1), channel_id=1, source_target_pairs={{0,64},{32,96},{64,0},{96,32},{1,65},{33,97},{65,1},{97,33},{2,66}... | collective-permute-start | bytes 98312 | tf_op jit(solution)/shard_map/ppermute | solution.py:616
  2.6 3.3 %strips.1 = bf16[256,1920]{1,0:T(8,128)(2,1)} custom-call(bf16[1280,128]{1,0:T(8,128)(2,1)} %bitcast.19), custom_call_target="tpu_custom_call" | custom-call | tf_op jit(solution)/shard_map/strips/pallas_call | solution.py:79
  6.0 10.9 %all-to-all-start = ((bf16[32,8,1920]{2,1,0:T(8,128)(2,1)}), bf16[32,8,1920]{2,1,0:T(8,128)(2,1)}, u32[]{:S(2)}, u32[]{:S(2)}) async-start(bf16[32,8,1920]{2,1,0:T(8,128)(2,1)} %bitcast.16), calls=%async_computation | async-start | bytes 1966080 | tf_op jit(solution)/shard_map/all_to_all | solution.py:631
  17.0 3.5 %collective-permute-start.3 = (bf16[4,2,8,256]{3,2,1,0:T(8,128)(2,1)S(1)}, bf16[4,2,8,256]{3,2,1,0:T(8,128)(2,1)S(1)}, u32[]{:S(2)}, u32[]{:S(2)}) collective-permute-start(bf16[4,2,8,256]{3,2,1,0:T(8,128)(2,1)S(1)} %get-tuple-element.41), channel_id=1, source_target_pairs={{0,1},{1,2},{2,3},{3,4},{4,5},{5,6},{6,7},{7,8},{8,9},{9,10},{10,1... | collective-permute-start | bytes 98312 | tf_op jit(solution)/shard_map/ppermute | solution.py:632
  20.5 7.0 %collective-permute-start.4 = (bf16[4,2,8,256]{3,2,1,0:T(8,128)(2,1)S(1)}, bf16[4,2,8,256]{3,2,1,0:T(8,128)(2,1)S(1)}, u32[]{:S(2)}, u32[]{:S(2)}) collective-permute-start(bf16[4,2,8,256]{3,2,1,0:T(8,128)(2,1)S(1)} %get-tuple-element.42), channel_id=1, source_target_pairs={{1,0},{2,1},{3,2},{4,3},{5,4},{6,5},{7,6},{8,7},{9,8},{10,9},{11,1... | collective-permute-start | bytes 98312 | tf_op jit(solution)/shard_map/ppermute | solution.py:633
  28.4 5.5 %collective-permute-done.3.top_ref = bf16[4,2,8,256]{3,2,1,0:T(8,128)(2,1)S(1)} collective-permute-done((bf16[4,2,8,256]{3,2,1,0:T(8,128)(2,1)S(1)}, bf16[4,2,8,256]{3,2,1,0:T(8,128)(2,1)S(1)}, u32[]{:S(2)}, u32[]{:S(2)}) %collective-permute-start.3) | collective-permute-done | bytes 32800 | tf_op jit(solution)/shard_map/ppermute | solution.py:632
  33.9 1.7 %grad_cost.1.refs_7_ = f32[8,256,128]{2,1,0:T(8,128)} custom-call(s32[1]{0:T(128)} %bitcast.5.view_ref, bf16[4,2,8,1024]{3,2,1,0:T(8,128)(2,1)S(1)} %get-tuple-element.40.own_ref, bf16[4,2,8,256]{3,2,1,0:T(8,128)(2,1)S(1)} %collective-permute-done.3.top_ref, bf16[4,2,8,256]{3,2,1,0:T(8,128)(2,1)S(1)} %collective-permute-done.4.bottom_ref, ...), custom_call_target="tpu_custom_call" | custom-call | tf_op jit(solution)/shard_map/grad_cost/pallas_call | solution.py:511
  35.6 3.6 %warp_other.1 = (bf16[240,16,128]{2,1,0:T(8,128)(2,1)S(1)}, f32[4,256,128]{2,1,0:T(8,128)S(1)}, f32[4,256,128]{2,1,0:T(8,128)S(1)}, bf16[5,4,256,128]{3,2,1,0:T(8,128)(2,1)S(1)}) custom-call(s32[2560]{0:T(1024)S(1)} %reshape.26.place_ref.refs_0_, s32[8]{0:T(128)S(1)} %fusion.order_ref.refs_1_, bf16[256,1920]{1,0:T(8,128)(2,1)} %bitcast.4.in_ref, ...), custom_call_target="tpu_custom_call" | custom-call | tf_op jit(solution)/shard_map/warp_other/pallas_call | solution.py:210
  39.8 2.5 %warp_mine.1 = (f32[4,256,128]{2,1,0:T(8,128)S(1)}, f32[4,256,128]{2,1,0:T(8,128)S(1)}, bf16[5,4,256,128]{3,2,1,0:T(8,128)(2,1)S(1)}) custom-call(s32[2560]{0:T(1024)S(1)} %reshape.26.place_ref.refs_0_, s32[8]{0:T(128)S(1)} %fusion.order_ref.refs_1_, bf16[240,16,128]{2,1,0:T(8,128)(2,1)S(1)} %get-tuple-element.44.blocks_ref, ...), custom_call_target="tpu_custom_call" | custom-call | tf_op jit(solution)/shard_map/warp_mine/pallas_call | solution.py:221
  42.5 0.8 collective-permute-start.6
  43.3 0.6 chip_second.1
  43.9 1.4 %collective-permute-start.9 = (f32[3,256,128]{2,1,0:T(8,128)S(1)}, f32[3,256,128]{2,1,0:T(8,128)S(1)}, u32[]{:S(2)}, u32[]{:S(2)}) collective-permute-start(f32[3,256,128]{2,1,0:T(8,128)S(1)} %get-tuple-element.57), channel_id=1, source_target_pairs={{0,64},{32,96},{64,0},{96,32},{1,65},{33,97},{65,1},{97,33},{2,66}... | collective-permute-start | bytes 1179656 | tf_op jit(solution)/shard_map/ppermute | solution.py:616
  45.3 6.3 %collective-permute-done.6.there_ref.first_there = bf16[4,256,128]{2,1,0:T(8,128)(2,1)S(1)} collective-permute-done((bf16[4,256,128]{2,1,0:T(8,128)(2,1)S(1)}, bf16[4,256,128]{2,1,0:T(8,128)(2,1)S(1)}, u32[]{:S(2)}, u32[]{:S(2)}) %collective-permute-start.6) | collective-permute-done | bytes 262176 | tf_op jit(solution)/shard_map/ppermute | solution.py:616
  52.1 1.5 %collective-permute-done.8.refs_5_ = bf16[4,256,128]{2,1,0:T(8,128)(2,1)S(1)} collective-permute-done((bf16[4,256,128]{2,1,0:T(8,128)(2,1)S(1)}, bf16[4,256,128]{2,1,0:T(8,128)(2,1)S(1)}, u32[]{:S(2)}, u32[]{:S(2)}) %collective-permute-start.8) | collective-permute-done | bytes 262176 | tf_op jit(solution)/shard_map/ppermute | solution.py:616
  53.6 5.3 %land_first.1.refs_8_ = bf16[256,1536]{1,0:T(8,128)(2,1)S(1)} custom-call(s32[2560]{0:T(1024)S(1)} %reshape.26.place_ref.refs_0_, s32[8]{0:T(128)S(1)} %fusion.order_ref.refs_1_, bf16[5,4,256,128]{3,2,1,0:T(8,128)(2,1)S(1)} %get-tuple-element.54.refs_2_, bf16[5,4,256,128]{3,2,1,0:T(8,128)(2,1)S(1)} %get-tuple-element.55.refs_3_, ...), custom_call_target="tpu_custom_call" | custom-call | flops 1000 | bytes 1000 | tf_op jit(solution)/shard_map/land_first/pallas_call | solution.py:289
  59.3 0.7 cost.1
  60.1 2.8 %land_last.1 = bf16[256,1920]{1,0:T(8,128)(2,1)} custom-call(s32[2560]{0:T(1024)S(1)} %reshape.26.place_ref.refs_0_, s32[8]{0:T(128)S(1)} %fusion.order_ref.refs_1_, bf16[5,4,256,128]{3,2,1,0:T(8,128)(2,1)S(1)} %get-tuple-element.54.refs_2_, bf16[5,4,256,128]{3,2,1,0:T(8,128)(2,1)S(1)} %get-tuple-element.55.refs_3_, bf16[5,8,4,64,64]{4,3,2,1,0:T(8,128)(2,1)S(1)} %copy-done, ...), custom_call_target="tpu_custom_call" | custom-call | flops 1000 | bytes 1000 | tf_op jit(solution)/shard_map/land_last/pallas_call | solution.py:302
  63.5 6.3 %all-to-all-start.1 = ((bf16[32,8,1920]{2,1,0:T(8,128)(2,1)}), bf16[32,8,1920]{2,1,0:T(8,128)(2,1)S(1)}, u32[]{:S(2)}, u32[]{:S(2)}) async-start(bf16[32,8,1920]{2,1,0:T(8,128)(2,1)} %bitcast.17), calls=%async_computation.1 | async-start | bytes 1966080 | tf_op jit(solution)/shard_map/all_to_all | solution.py:660
  69.8 3.4 %collective-permute-start.11 = (bf16[4,64,128]{2,1,0:T(8,128)(2,1)S(1)}, bf16[4,64,128]{2,1,0:T(8,128)(2,1)S(1)}, u32[]{:S(2)}, u32[]{:S(2)}) collective-permute-start(bf16[4,64,128]{2,1,0:T(8,128)(2,1)S(1)} %get-tuple-element.69), channel_id=1, source_target_pairs={{0,1},{1,2},{2,3},{3,4},{4,5},{5,6},{6,7},{7,8},{8,9},{9,10},{10,1... | collective-permute-start | bytes 196616 | tf_op jit(solution)/shard_map/ppermute | solution.py:661
  73.1 7.0 %collective-permute-start.12 = (bf16[4,64,128]{2,1,0:T(8,128)(2,1)S(1)}, bf16[4,64,128]{2,1,0:T(8,128)(2,1)S(1)}, u32[]{:S(2)}, u32[]{:S(2)}) collective-permute-start(bf16[4,64,128]{2,1,0:T(8,128)(2,1)S(1)} %get-tuple-element.70), channel_id=1, source_target_pairs={{1,0},{2,1},{3,2},{4,3},{5,4},{6,5},{7,6},{8,7},{9,8},{10,9},{11,1... | collective-permute-start | bytes 196616 | tf_op jit(solution)/shard_map/ppermute | solution.py:662
  80.1 0.6 conv.1.main_ref
  80.7 6.9 %collective-permute-done.11.top_ref = bf16[4,64,128]{2,1,0:T(8,128)(2,1)S(1)} collective-permute-done((bf16[4,64,128]{2,1,0:T(8,128)(2,1)S(1)}, bf16[4,64,128]{2,1,0:T(8,128)(2,1)S(1)}, u32[]{:S(2)}, u32[]{:S(2)}) %collective-permute-start.11) | collective-permute-done | bytes 65568 | tf_op jit(solution)/shard_map/ppermute | solution.py:661
  87.6 1.0 %conv_rows.1 = bf16[2,8,1024]{2,1,0:T(8,128)(2,1)} custom-call(f32[2,8,1024]{2,1,0:T(8,128)S(1)} %conv.1.main_ref, bf16[4,64,128]{2,1,0:T(8,128)(2,1)S(1)} %collective-permute-done.11.top_ref, bf16[4,64,128]{2,1,0:T(8,128)(2,1)S(1)} %collective-permute-done.12.bottom_ref, bf16[72,96]{1,0:T(8,128)(2,1)S(1)} %reshape.30.weight_ref), custom_call_target="tpu_custom_call" | custom-call | tf_op jit(solution)/shard_map/conv_rows/pallas_call | solution.py:590
  88.7 1.5 %unstrips.1 = f32[1280,128]{1,0:T(8,128)} custom-call(bf16[256,1920]{1,0:T(8,128)(2,1)S(1)} %bitcast.15), custom_call_target="tpu_custom_call" | custom-call | tf_op jit(solution)/shard_map/unstrips/pallas_call | solution.py:117
  (45 shorter events, 3.5 us)
Async XLA Ops:
  0.6 5.3 %copy-start.3 = (bf16[2,8,1024]{2,1,0:T(8,128)(2,1)S(1)}, bf16[2,8,1024]{2,1,0:T(8,128)(2,1)}, u32[]{:S(2)}) copy-start(bf16[2,8,1024]{2,1,0:T(8,128)(2,1)} %refs_0_.1) | copy-start | bytes 98308
  0.6 5.3 %collective-permute-start = (bf16[2,8,1024]{2,1,0:T(8,128)(2,1)}, bf16[2,8,1024]{2,1,0:T(8,128)(2,1)S(1)}, u32[]{:S(2)}, u32[]{:S(2)}) collective-permute-start(bf16[2,8,1024]{2,1,0:T(8,128)(2,1)} %refs_0_.1), channel_id=1, source_target_pairs={{0,32},{32,0},{64,96},{96,64},{1,33},{33,1},{65,97},{97,65},{2,34}... | collective-permute-start | bytes 98312 | tf_op jit(solution)/shard_map/ppermute | solution.py:616
  0.7 5.2 %collective-permute-start.1 = (bf16[2,8,1024]{2,1,0:T(8,128)(2,1)}, bf16[2,8,1024]{2,1,0:T(8,128)(2,1)S(1)}, u32[]{:S(2)}, u32[]{:S(2)}) collective-permute-start(bf16[2,8,1024]{2,1,0:T(8,128)(2,1)} %refs_0_.1), channel_id=1, source_target_pairs={{0,64},{32,96},{64,0},{96,32},{1,65},{33,97},{65,1},{97,33},{2,66}... | collective-permute-start | bytes 98312 | tf_op jit(solution)/shard_map/ppermute | solution.py:616
  2.4 3.6 %collective-permute-start.2 = (bf16[2,8,1024]{2,1,0:T(8,128)(2,1)}, bf16[2,8,1024]{2,1,0:T(8,128)(2,1)S(1)}, u32[]{:S(2)}, u32[]{:S(2)}) collective-permute-start(bf16[2,8,1024]{2,1,0:T(8,128)(2,1)} %refs_0_.1), channel_id=1, source_target_pairs={{0,96},{32,64},{64,32},{96,0},{1,97},{33,65},{65,33},{97,1},{2,98}... | collective-permute-start | bytes 98312 | tf_op jit(solution)/shard_map/ppermute | solution.py:616
  5.9 11.0 %copy-start.5 = (s32[5,8,16,4]{2,3,1,0:T(4,128)S(1)}, s32[5,8,16,4]{2,3,1,0:T(4,128)}, u32[]{:S(2)}) copy-start(s32[5,8,16,4]{2,3,1,0:T(4,128)} %param.11) | copy-start | bytes 30724
  5.9 11.0 %copy-start.6 = (s32[5,8,16,4]{2,3,1,0:T(4,128)S(1)}, s32[5,8,16,4]{2,3,1,0:T(4,128)}, u32[]{:S(2)}) copy-start(s32[5,8,16,4]{2,3,1,0:T(4,128)} %param.10) | copy-start | bytes 30724
  6.0 22.0 %copy-start.4 = (bf16[3,3,3,8,32]{4,3,2,1,0:T(8,128)(2,1)S(1)}, bf16[3,3,3,8,32]{4,3,2,1,0:T(8,128)(2,1)}, u32[]{:S(2)}) copy-start(bf16[3,3,3,8,32]{4,3,2,1,0:T(8,128)(2,1)} %param.12) | copy-start | bytes 41476
  6.0 29.6 %all-to-all-start = ((bf16[32,8,1920]{2,1,0:T(8,128)(2,1)}), bf16[32,8,1920]{2,1,0:T(8,128)(2,1)}, u32[]{:S(2)}, u32[]{:S(2)}) async-start(bf16[32,8,1920]{2,1,0:T(8,128)(2,1)} %bitcast.16), calls=%async_computation | async-start | bytes 1966080 | tf_op jit(solution)/shard_map/all_to_all | solution.py:631
  16.9 18.7 %copy-start = (bf16[5,8,4,64,64]{4,3,2,1,0:T(8,128)(2,1)S(1)}, bf16[5,8,4,64,64]{4,3,2,1,0:T(8,128)(2,1)}, u32[]{:S(2)}) copy-start(bf16[5,8,4,64,64]{4,3,2,1,0:T(8,128)(2,1)} %refs_4_.3) | copy-start | bytes 3932164
  17.0 16.9 %collective-permute-start.3 = (bf16[4,2,8,256]{3,2,1,0:T(8,128)(2,1)S(1)}, bf16[4,2,8,256]{3,2,1,0:T(8,128)(2,1)S(1)}, u32[]{:S(2)}, u32[]{:S(2)}) collective-permute-start(bf16[4,2,8,256]{3,2,1,0:T(8,128)(2,1)S(1)} %get-tuple-element.41), channel_id=1, source_target_pairs={{0,1},{1,2},{2,3},{3,4},{4,5},{5,6},{6,7},{7,8},{8,9},{9,10},{10,1... | collective-permute-start | bytes 98312 | tf_op jit(solution)/shard_map/ppermute | solution.py:632
  20.5 13.4 %collective-permute-start.4 = (bf16[4,2,8,256]{3,2,1,0:T(8,128)(2,1)S(1)}, bf16[4,2,8,256]{3,2,1,0:T(8,128)(2,1)S(1)}, u32[]{:S(2)}, u32[]{:S(2)}) collective-permute-start(bf16[4,2,8,256]{3,2,1,0:T(8,128)(2,1)S(1)} %get-tuple-element.42), channel_id=1, source_target_pairs={{1,0},{2,1},{3,2},{4,3},{5,4},{6,5},{7,6},{8,7},{9,8},{10,9},{11,1... | collective-permute-start | bytes 98312 | tf_op jit(solution)/shard_map/ppermute | solution.py:633
  39.2 3.1 %collective-permute-start.5 = (f32[4,256,128]{2,1,0:T(8,128)S(1)}, f32[4,256,128]{2,1,0:T(8,128)S(1)}, u32[]{:S(2)}, u32[]{:S(2)}) collective-permute-start(f32[4,256,128]{2,1,0:T(8,128)S(1)} %get-tuple-element.46), channel_id=1, source_target_pairs={{0,32},{32,0},{64,96},{96,64},{1,33},{33,1},{65,97},{97,65},{2,34}... | collective-permute-start | bytes 1572872 | tf_op jit(solution)/shard_map/ppermute | solution.py:616
  39.3 4.0 %collective-permute-start.7 = (f32[4,256,128]{2,1,0:T(8,128)S(1)}, f32[4,256,128]{2,1,0:T(8,128)S(1)}, u32[]{:S(2)}, u32[]{:S(2)}) collective-permute-start(f32[4,256,128]{2,1,0:T(8,128)S(1)} %get-tuple-element.50), channel_id=1, source_target_pairs={{0,32},{32,0},{64,96},{96,64},{1,33},{33,1},{65,97},{97,65},{2,34}... | collective-permute-start | bytes 1572872 | tf_op jit(solution)/shard_map/ppermute | solution.py:616
  42.3 9.4 %copy-start.2 = (bf16[32,1024]{1,0:T(8,128)(2,1)S(1)}, bf16[32,1024]{1,0:T(8,128)(2,1)}, u32[]{:S(2)}) copy-start(bf16[32,1024]{1,0:T(8,128)(2,1)} %ref_ref.3) | copy-start | bytes 196612
  42.4 11.2 %copy-start.1 = (f32[8,256,128]{2,1,0:T(8,128)S(1)}, f32[8,256,128]{2,1,0:T(8,128)}, u32[]{:S(2)}) copy-start(f32[8,256,128]{2,1,0:T(8,128)} %grad_cost.1.refs_7_) | copy-start | bytes 3145732
  42.5 9.2 %collective-permute-start.6 = (bf16[4,256,128]{2,1,0:T(8,128)(2,1)S(1)}, bf16[4,256,128]{2,1,0:T(8,128)(2,1)S(1)}, u32[]{:S(2)}, u32[]{:S(2)}) collective-permute-start(bf16[4,256,128]{2,1,0:T(8,128)(2,1)S(1)} %get-tuple-element.48), channel_id=1, source_target_pairs={{0,64},{32,96},{64,0},{96,32},{1,65},{33,97},{65,1},{97,33},{2,66}... | collective-permute-start | bytes 786440 | tf_op jit(solution)/shard_map/ppermute | solution.py:616
  43.9 15.4 %collective-permute-start.9 = (f32[3,256,128]{2,1,0:T(8,128)S(1)}, f32[3,256,128]{2,1,0:T(8,128)S(1)}, u32[]{:S(2)}, u32[]{:S(2)}) collective-permute-start(f32[3,256,128]{2,1,0:T(8,128)S(1)} %get-tuple-element.57), channel_id=1, source_target_pairs={{0,64},{32,96},{64,0},{96,32},{1,65},{33,97},{65,1},{97,33},{2,66}... | collective-permute-start | bytes 1179656 | tf_op jit(solution)/shard_map/ppermute | solution.py:616
  51.8 1.8 %collective-permute-start.8 = (bf16[4,256,128]{2,1,0:T(8,128)(2,1)S(1)}, bf16[4,256,128]{2,1,0:T(8,128)(2,1)S(1)}, u32[]{:S(2)}, u32[]{:S(2)}) collective-permute-start(bf16[4,256,128]{2,1,0:T(8,128)(2,1)S(1)} %mean.1.refs_6_), channel_id=1, source_target_pairs={{0,32},{32,0},{64,96},{96,64},{1,33},{33,1},{65,97},{97,65},{2,34}... | collective-permute-start | bytes 786440 | tf_op jit(solution)/shard_map/ppermute | solution.py:616
  60.0 2.9 %collective-permute-start.10 = (bf16[2,256,128]{2,1,0:T(8,128)(2,1)S(1)}, bf16[2,256,128]{2,1,0:T(8,128)(2,1)S(1)}, u32[]{:S(2)}, u32[]{:S(2)}) collective-permute-start(bf16[2,256,128]{2,1,0:T(8,128)(2,1)S(1)} %get-tuple-element.62), channel_id=1, source_target_pairs={{0,32},{32,0},{64,96},{96,64},{1,33},{33,1},{65,97},{97,65},{2,34}... | collective-permute-start | bytes 393224 | tf_op jit(solution)/shard_map/ppermute | solution.py:616
  63.5 25.2 %all-to-all-start.1 = ((bf16[32,8,1920]{2,1,0:T(8,128)(2,1)}), bf16[32,8,1920]{2,1,0:T(8,128)(2,1)S(1)}, u32[]{:S(2)}, u32[]{:S(2)}) async-start(bf16[32,8,1920]{2,1,0:T(8,128)(2,1)} %bitcast.17), calls=%async_computation.1 | async-start | bytes 1966080 | tf_op jit(solution)/shard_map/all_to_all | solution.py:660
  69.8 17.9 %collective-permute-start.11 = (bf16[4,64,128]{2,1,0:T(8,128)(2,1)S(1)}, bf16[4,64,128]{2,1,0:T(8,128)(2,1)S(1)}, u32[]{:S(2)}, u32[]{:S(2)}) collective-permute-start(bf16[4,64,128]{2,1,0:T(8,128)(2,1)S(1)} %get-tuple-element.69), channel_id=1, source_target_pairs={{0,1},{1,2},{2,3},{3,4},{4,5},{5,6},{6,7},{7,8},{8,9},{9,10},{10,1... | collective-permute-start | bytes 196616 | tf_op jit(solution)/shard_map/ppermute | solution.py:661
  73.1 14.5 %collective-permute-start.12 = (bf16[4,64,128]{2,1,0:T(8,128)(2,1)S(1)}, bf16[4,64,128]{2,1,0:T(8,128)(2,1)S(1)}, u32[]{:S(2)}, u32[]{:S(2)}) collective-permute-start(bf16[4,64,128]{2,1,0:T(8,128)(2,1)S(1)} %get-tuple-element.70), channel_id=1, source_target_pairs={{1,0},{2,1},{3,2},{4,3},{5,4},{6,5},{7,6},{8,7},{9,8},{10,9},{11,1... | collective-permute-start | bytes 196616 | tf_op jit(solution)/shard_map/ppermute | solution.py:662

commit v7 on v6

--- a/solution.py
+++ b/solution.py
@@ -43,55 +43,37 @@
     return (iota((128, 128), 0) >> 5) == (iota((128, 128), 1) & 3)
 
 
-def strips_kernel(src_hbm, out_hbm, source, wide, stage, moved_out, in_sem, out_sem):
-    loads = []
-    for v in range(VIEWS):
-        rows = pl.ds(v * 256, 256)
-        loads.append(pltpu.make_async_copy(src_hbm.at[rows], source.at[rows], in_sem.at[v]))
-        loads[-1].start()
+def strips_kernel(src_ref, out_ref, wide, stage):
+    wide[...] = src_ref[...].astype(F32)
     table = band_table()
     mask = row_mask()
-    stores = []
-    for v in range(VIEWS):
-        loads[v].wait()
-        wide[v] = source[v * 256 : (v + 1) * 256].astype(F32)
-        for x in range(8):
-            own = wide[v, pl.ds(x, 32, stride=8), :]
-            tall = jnp.where(mask, jnp.concatenate([own] * 4, axis=0), 0.0).astype(BF)
-            moved = lax.dot_general(table, tall, NT, preferred_element_type=F32)
+    for x in range(8):
+        own = wide[pl.ds(x, 160, stride=8), :]
+        parts = []
+        for v in range(VIEWS):
+            part = own[v * 32 : (v + 1) * 32]
+            parts.append(jnp.where(mask, jnp.concatenate([part] * 4, axis=0), 0.0).astype(BF))
+        stacked = jnp.concatenate(parts, axis=0)
+        moved = lax.dot_general(table, stacked, NT, preferred_element_type=F32)
+        for v in range(VIEWS):
             for band in range(3):
                 stage[v * 3 + band, pl.ds(x, 32, stride=8), :] = moved[
-                    band * 32 : (band + 1) * 32
+                    band * 32 : (band + 1) * 32, v * 128 : (v + 1) * 128
                 ]
-        for band in range(3):
-            moved_out[v, :, band * 128 : (band + 1) * 128] = stage[v * 3 + band].astype(BF)
-        stores.append(
-            pltpu.make_async_copy(
-                moved_out.at[v], out_hbm.at[:, v * 384 : (v + 1) * 384], out_sem.at[v]
-            )
-        )
-        stores[-1].start()
-    for store in stores:
-        store.wait()
+    for piece in range(VIEWS * 3):
+        out_ref[:, piece * 128 : (piece + 1) * 128] = stage[piece].astype(BF)
 
 
 def strips(source):
     return pl.pallas_call(
         strips_kernel,
-        out_shape=pltpu.HBM((256, VIEWS * 384), BF),
-        in_specs=[pl.BlockSpec(memory_space=pltpu.HBM)],
-        out_specs=pl.BlockSpec(memory_space=pltpu.HBM),
-        scratch_shapes=[
-            pltpu.VMEM((1280, 128), BF),
-            pltpu.VMEM((VIEWS, 256, 128), F32),
-            pltpu.VMEM((VIEWS * 3, 256, 128), F32),
-            pltpu.VMEM((VIEWS, 256, 384), BF),
-            pltpu.SemaphoreType.DMA((VIEWS,)),
-            pltpu.SemaphoreType.DMA((VIEWS,)),
-        ],
-        compiler_params=pltpu.CompilerParams(vmem_limit_bytes=2 * VMEM_LIMIT),
+        out_shape=jax.ShapeDtypeStruct((256, VIEWS * 384), BF),
+        in_specs=[whole()],
+        out_specs=whole(),
+        scratch_shapes=[pltpu.VMEM((1280, 128), F32), pltpu.VMEM((VIEWS * 3, 256, 128), F32)],
+        compiler_params=params(),
         name="strips",
-    )(pltpu.with_memory_space_constraint(source, pltpu.HBM))
+    )(source)
 
 
 def unstrips_kernel(in_ref, out_ref, wide):
@@ -497,10 +479,10 @@
             even, odd = pair_swap(upper, lower)
             out_ref[plane, pair * 32 : pair * 32 + 16] = even
             out_ref[plane, pair * 32 + 16 : pair * 32 + 32] = odd
-        if plane % 4 == 3:
-            part = pl.ds(plane - 3, 4)
+        if plane % 2 == 1:
+            part = pl.ds(plane - 1, 2)
             stores.append(
-                pltpu.make_async_copy(out_ref.at[part], out_hbm.at[part], sem.at[plane // 4])
+                pltpu.make_async_copy(out_ref.at[part], out_hbm.at[part], sem.at[plane // 2])
             )
             stores[-1].start()
     for store in stores:
@@ -513,7 +495,7 @@
         out_shape=pltpu.HBM((PLANES, 256, 128), F32),
         in_specs=[pl.BlockSpec(memory_space=pltpu.SMEM)] + [whole()] * 4,
         out_specs=pl.BlockSpec(memory_space=pltpu.HBM),
-        scratch_shapes=[pltpu.VMEM((PLANES, 256, 128), F32), pltpu.SemaphoreType.DMA((2,))],
+        scratch_shapes=[pltpu.VMEM((PLANES, 256, 128), F32), pltpu.SemaphoreType.DMA((4,))],
         compiler_params=params(),
         name="grad_cost",
     )(view, own, top, bottom, weight)

time: 90.7 us -> 90.2 us (level)
  Pallas kernels: 24.5 us -> 23 us
  local copies, waits for them, and re-layouts: 0.92 us -> 1.88 us
    pallas_call x1, Pallas kernels: 3.27 us -> 1.86 us  [strips(): pl.pallas_call(strips_kernel, out_shape=jax.ShapeDtypeStruct((256, VIEWS...]
    unnamed x14 -> x16, local copies, waits for them, and re-layouts: 0.04 us -> 1.01 us
  transfers between devices with their start and end apart: 15 -> 15, of which waited for: 5 -> 6; matrix products, arithmetic and copies ran while one was open for 1% -> 1% of each run, Pallas kernels for 20% -> 18%
where the time goes in v7:
time: 90.2 us; the launch traced here: 89.7 us
  starting transfers between devices  42.8 us (47%)
  Pallas kernels  23 us (25%)
  waiting for transfers between devices  21 us (23%)
  local copies, waits for them, and re-layouts  1.88 us (2%)
  between operations  0.93 us (1%)
    all_to_all x1, starting transfers between devices, body(): lax.all_to_all(operand, 'tile', split_axis=0, concat_axis=0, tiled=True)  10.6 us
    ppermute x9, waiting for transfers between devices, other(): return lax.ppermute(array, 'view', [(i, i ^ mask) for i in range(views)])  8.73 us
    ppermute x1, starting transfers between devices, body(): bottom = lax.ppermute(initial, 'tile', down)  6.98 us
    ppermute x1, starting transfers between devices, body(): cost_bottom = lax.ppermute(cost_initial, 'tile', down)  6.98 us
    ppermute x1, waiting for transfers between devices, body(): cost_top = lax.ppermute(cost_last, 'tile', up)  6.92 us
    all_to_all x1, starting transfers between devices, body(): lax.all_to_all(landed, 'tile', split_axis=0, concat_axis=0, tiled=True)  6.34 us
    ppermute x1, waiting for transfers between devices, body(): top = lax.ppermute(last, 'tile', up)  5.29 us
    pallas_call x1, Pallas kernels, land_first(): pl.pallas_call(functools.partial(land_first_kernel, views), in_specs=[sme...  5.29 us
  transfers between devices with their start and end apart: 15, of which 6 were waited for; matrix products, arithmetic and copies ran while one was open for 1% of the time, Pallas kernels for 18%

profile of v7, /device:TPU:32, one launch (start us, length us, event | category | flops | bytes accessed | tf_op | source)
XLA Modules:
  0.0 89.7 jit_solution(9826644094583506275)
XLA Ops:
  0.7 1.7 %collective-permute-start.1 = (bf16[2,8,1024]{2,1,0:T(8,128)(2,1)}, bf16[2,8,1024]{2,1,0:T(8,128)(2,1)S(1)}, u32[]{:S(2)}, u32[]{:S(2)}) collective-permute-start(bf16[2,8,1024]{2,1,0:T(8,128)(2,1)} %refs_0_.1), channel_id=1, source_target_pairs={{0,64},{32,96},{64,0},{96,32},{1,65},{33,97},{65,1},{97,33},{2,66}... | collective-permute-start | bytes 98312 | tf_op jit(solution)/shard_map/ppermute | solution.py:598
  2.6 1.0 %copy-done.2 = bf16[5,32,8,128]{3,2,1,0:T(8,128)(2,1)S(1)} copy-done((bf16[5,32,8,128]{3,2,1,0:T(8,128)(2,1)S(1)}, bf16[5,32,8,128]{3,2,1,0:T(8,128)(2,1)}, u32[]{:S(2)}) %copy-start.2) | copy-done | bytes 327704
  3.6 1.9 %strips.1 = bf16[256,1920]{1,0:T(8,128)(2,1)} custom-call(bf16[1280,128]{1,0:T(8,128)(2,1)S(1)} %bitcast.16), custom_call_target="tpu_custom_call" | custom-call | tf_op jit(solution)/shard_map/strips/pallas_call | solution.py:68
  6.0 10.6 %all-to-all-start = ((bf16[32,8,1920]{2,1,0:T(8,128)(2,1)}), bf16[32,8,1920]{2,1,0:T(8,128)(2,1)}, u32[]{:S(2)}, u32[]{:S(2)}) async-start(bf16[32,8,1920]{2,1,0:T(8,128)(2,1)} %bitcast.3), calls=%async_computation | async-start | bytes 1966080 | tf_op jit(solution)/shard_map/all_to_all | solution.py:613
  16.6 3.5 %collective-permute-start.3 = (bf16[4,2,8,256]{3,2,1,0:T(8,128)(2,1)S(1)}, bf16[4,2,8,256]{3,2,1,0:T(8,128)(2,1)S(1)}, u32[]{:S(2)}, u32[]{:S(2)}) collective-permute-start(bf16[4,2,8,256]{3,2,1,0:T(8,128)(2,1)S(1)} %get-tuple-element.41), channel_id=1, source_target_pairs={{0,1},{1,2},{2,3},{3,4},{4,5},{5,6},{6,7},{7,8},{8,9},{9,10},{10,1... | collective-permute-start | bytes 98312 | tf_op jit(solution)/shard_map/ppermute | solution.py:614
  20.2 7.0 %collective-permute-start.4 = (bf16[4,2,8,256]{3,2,1,0:T(8,128)(2,1)S(1)}, bf16[4,2,8,256]{3,2,1,0:T(8,128)(2,1)S(1)}, u32[]{:S(2)}, u32[]{:S(2)}) collective-permute-start(bf16[4,2,8,256]{3,2,1,0:T(8,128)(2,1)S(1)} %get-tuple-element.42), channel_id=1, source_target_pairs={{1,0},{2,1},{3,2},{4,3},{5,4},{6,5},{7,6},{8,7},{9,8},{10,9},{11,1... | collective-permute-start | bytes 98312 | tf_op jit(solution)/shard_map/ppermute | solution.py:615
  28.1 5.3 %collective-permute-done.3.top_ref = bf16[4,2,8,256]{3,2,1,0:T(8,128)(2,1)S(1)} collective-permute-done((bf16[4,2,8,256]{3,2,1,0:T(8,128)(2,1)S(1)}, bf16[4,2,8,256]{3,2,1,0:T(8,128)(2,1)S(1)}, u32[]{:S(2)}, u32[]{:S(2)}) %collective-permute-start.3) | collective-permute-done | bytes 32800 | tf_op jit(solution)/shard_map/ppermute | solution.py:614
  33.4 1.6 %grad_cost.1.refs_7_ = f32[8,256,128]{2,1,0:T(8,128)} custom-call(s32[1]{0:T(128)} %bitcast.5.view_ref, bf16[4,2,8,1024]{3,2,1,0:T(8,128)(2,1)S(1)} %get-tuple-element.40.own_ref, bf16[4,2,8,256]{3,2,1,0:T(8,128)(2,1)S(1)} %collective-permute-done.3.top_ref, bf16[4,2,8,256]{3,2,1,0:T(8,128)(2,1)S(1)} %collective-permute-done.4.bottom_ref, ...), custom_call_target="tpu_custom_call" | custom-call | tf_op jit(solution)/shard_map/grad_cost/pallas_call | solution.py:493
  35.1 3.6 %warp_other.1 = (bf16[240,16,128]{2,1,0:T(8,128)(2,1)S(1)}, f32[4,256,128]{2,1,0:T(8,128)S(1)}, f32[4,256,128]{2,1,0:T(8,128)S(1)}, bf16[5,4,256,128]{3,2,1,0:T(8,128)(2,1)S(1)}) custom-call(s32[2560]{0:T(1024)S(1)} %reshape.26.place_ref.refs_0_, s32[8]{0:T(128)S(1)} %fusion.order_ref.refs_1_, bf16[256,1920]{1,0:T(8,128)(2,1)} %bitcast.4.in_ref, ...), custom_call_target="tpu_custom_call" | custom-call | tf_op jit(solution)/shard_map/warp_other/pallas_call | solution.py:192
  39.2 2.5 %warp_mine.1 = (f32[4,256,128]{2,1,0:T(8,128)S(1)}, f32[4,256,128]{2,1,0:T(8,128)S(1)}, bf16[5,4,256,128]{3,2,1,0:T(8,128)(2,1)S(1)}) custom-call(s32[2560]{0:T(1024)S(1)} %reshape.26.place_ref.refs_0_, s32[8]{0:T(128)S(1)} %fusion.order_ref.refs_1_, bf16[240,16,128]{2,1,0:T(8,128)(2,1)S(1)} %get-tuple-element.44.blocks_ref, ...), custom_call_target="tpu_custom_call" | custom-call | tf_op jit(solution)/shard_map/warp_mine/pallas_call | solution.py:203
  41.9 0.7 collective-permute-start.6
  42.7 0.6 chip_second.1
  43.4 1.4 %collective-permute-start.9 = (f32[3,256,128]{2,1,0:T(8,128)S(1)}, f32[3,256,128]{2,1,0:T(8,128)S(1)}, u32[]{:S(2)}, u32[]{:S(2)}) collective-permute-start(f32[3,256,128]{2,1,0:T(8,128)S(1)} %get-tuple-element.57), channel_id=1, source_target_pairs={{0,64},{32,96},{64,0},{96,32},{1,65},{33,97},{65,1},{97,33},{2,66}... | collective-permute-start | bytes 1179656 | tf_op jit(solution)/shard_map/ppermute | solution.py:598
  44.8 6.3 %collective-permute-done.6.there_ref.first_there = bf16[4,256,128]{2,1,0:T(8,128)(2,1)S(1)} collective-permute-done((bf16[4,256,128]{2,1,0:T(8,128)(2,1)S(1)}, bf16[4,256,128]{2,1,0:T(8,128)(2,1)S(1)}, u32[]{:S(2)}, u32[]{:S(2)}) %collective-permute-start.6) | collective-permute-done | bytes 262176 | tf_op jit(solution)/shard_map/ppermute | solution.py:598
  51.5 1.5 %collective-permute-done.8.refs_5_ = bf16[4,256,128]{2,1,0:T(8,128)(2,1)S(1)} collective-permute-done((bf16[4,256,128]{2,1,0:T(8,128)(2,1)S(1)}, bf16[4,256,128]{2,1,0:T(8,128)(2,1)S(1)}, u32[]{:S(2)}, u32[]{:S(2)}) %collective-permute-start.8) | collective-permute-done | bytes 262176 | tf_op jit(solution)/shard_map/ppermute | solution.py:598
  53.1 5.3 %land_first.1.refs_8_ = bf16[256,1536]{1,0:T(8,128)(2,1)S(1)} custom-call(s32[2560]{0:T(1024)S(1)} %reshape.26.place_ref.refs_0_, s32[8]{0:T(128)S(1)} %fusion.order_ref.refs_1_, bf16[5,4,256,128]{3,2,1,0:T(8,128)(2,1)S(1)} %get-tuple-element.54.refs_2_, bf16[5,4,256,128]{3,2,1,0:T(8,128)(2,1)S(1)} %get-tuple-element.55.refs_3_, ...), custom_call_target="tpu_custom_call" | custom-call | flops 1000 | bytes 1000 | tf_op jit(solution)/shard_map/land_first/pallas_call | solution.py:271
  58.7 0.7 cost.1
  59.5 2.8 %land_last.1 = bf16[256,1920]{1,0:T(8,128)(2,1)} custom-call(s32[2560]{0:T(1024)S(1)} %reshape.26.place_ref.refs_0_, s32[8]{0:T(128)S(1)} %fusion.order_ref.refs_1_, bf16[5,4,256,128]{3,2,1,0:T(8,128)(2,1)S(1)} %get-tuple-element.54.refs_2_, bf16[5,4,256,128]{3,2,1,0:T(8,128)(2,1)S(1)} %get-tuple-element.55.refs_3_, bf16[5,8,4,64,64]{4,3,2,1,0:T(8,128)(2,1)S(1)} %copy-done, ...), custom_call_target="tpu_custom_call" | custom-call | flops 1000 | bytes 1000 | tf_op jit(solution)/shard_map/land_last/pallas_call | solution.py:284
  62.9 6.3 %all-to-all-start.1 = ((bf16[32,8,1920]{2,1,0:T(8,128)(2,1)}), bf16[32,8,1920]{2,1,0:T(8,128)(2,1)S(1)}, u32[]{:S(2)}, u32[]{:S(2)}) async-start(bf16[32,8,1920]{2,1,0:T(8,128)(2,1)} %bitcast.17), calls=%async_computation.1 | async-start | bytes 1966080 | tf_op jit(solution)/shard_map/all_to_all | solution.py:642
  69.3 3.4 %collective-permute-start.11 = (bf16[4,64,128]{2,1,0:T(8,128)(2,1)S(1)}, bf16[4,64,128]{2,1,0:T(8,128)(2,1)S(1)}, u32[]{:S(2)}, u32[]{:S(2)}) collective-permute-start(bf16[4,64,128]{2,1,0:T(8,128)(2,1)S(1)} %get-tuple-element.69), channel_id=1, source_target_pairs={{0,1},{1,2},{2,3},{3,4},{4,5},{5,6},{6,7},{7,8},{8,9},{9,10},{10,1... | collective-permute-start | bytes 196616 | tf_op jit(solution)/shard_map/ppermute | solution.py:643
  72.6 7.0 %collective-permute-start.12 = (bf16[4,64,128]{2,1,0:T(8,128)(2,1)S(1)}, bf16[4,64,128]{2,1,0:T(8,128)(2,1)S(1)}, u32[]{:S(2)}, u32[]{:S(2)}) collective-permute-start(bf16[4,64,128]{2,1,0:T(8,128)(2,1)S(1)} %get-tuple-element.70), channel_id=1, source_target_pairs={{1,0},{2,1},{3,2},{4,3},{5,4},{6,5},{7,6},{8,7},{9,8},{10,9},{11,1... | collective-permute-start | bytes 196616 | tf_op jit(solution)/shard_map/ppermute | solution.py:644
  80.2 6.9 %collective-permute-done.11.top_ref = bf16[4,64,128]{2,1,0:T(8,128)(2,1)S(1)} collective-permute-done((bf16[4,64,128]{2,1,0:T(8,128)(2,1)S(1)}, bf16[4,64,128]{2,1,0:T(8,128)(2,1)S(1)}, u32[]{:S(2)}, u32[]{:S(2)}) %collective-permute-start.11) | collective-permute-done | bytes 65568 | tf_op jit(solution)/shard_map/ppermute | solution.py:643
  87.2 1.0 %conv_rows.1 = bf16[2,8,1024]{2,1,0:T(8,128)(2,1)} custom-call(f32[2,8,1024]{2,1,0:T(8,128)S(1)} %conv.1.main_ref, bf16[4,64,128]{2,1,0:T(8,128)(2,1)S(1)} %collective-permute-done.11.top_ref, bf16[4,64,128]{2,1,0:T(8,128)(2,1)S(1)} %collective-permute-done.12.bottom_ref, bf16[72,96]{1,0:T(8,128)(2,1)S(1)} %reshape.30.weight_ref), custom_call_target="tpu_custom_call" | custom-call | tf_op jit(solution)/shard_map/conv_rows/pallas_call | solution.py:572
  88.2 1.5 %unstrips.1 = f32[1280,128]{1,0:T(8,128)} custom-call(bf16[256,1920]{1,0:T(8,128)(2,1)S(1)} %bitcast.15), custom_call_target="tpu_custom_call" | custom-call | tf_op jit(solution)/shard_map/unstrips/pallas_call | solution.py:99
  (47 shorter events, 4.5 us)
Async XLA Ops:
  0.6 4.8 %collective-permute-start = (bf16[2,8,1024]{2,1,0:T(8,128)(2,1)}, bf16[2,8,1024]{2,1,0:T(8,128)(2,1)S(1)}, u32[]{:S(2)}, u32[]{:S(2)}) collective-permute-start(bf16[2,8,1024]{2,1,0:T(8,128)(2,1)} %refs_0_.1), channel_id=1, source_target_pairs={{0,32},{32,0},{64,96},{96,64},{1,33},{33,1},{65,97},{97,65},{2,34}... | collective-permute-start | bytes 98312 | tf_op jit(solution)/shard_map/ppermute | solution.py:598
  0.7 4.7 %collective-permute-start.1 = (bf16[2,8,1024]{2,1,0:T(8,128)(2,1)}, bf16[2,8,1024]{2,1,0:T(8,128)(2,1)S(1)}, u32[]{:S(2)}, u32[]{:S(2)}) collective-permute-start(bf16[2,8,1024]{2,1,0:T(8,128)(2,1)} %refs_0_.1), channel_id=1, source_target_pairs={{0,64},{32,96},{64,0},{96,32},{1,65},{33,97},{65,1},{97,33},{2,66}... | collective-permute-start | bytes 98312 | tf_op jit(solution)/shard_map/ppermute | solution.py:598
  2.4 3.6 %collective-permute-start.2 = (bf16[2,8,1024]{2,1,0:T(8,128)(2,1)}, bf16[2,8,1024]{2,1,0:T(8,128)(2,1)S(1)}, u32[]{:S(2)}, u32[]{:S(2)}) collective-permute-start(bf16[2,8,1024]{2,1,0:T(8,128)(2,1)} %refs_0_.1), channel_id=1, source_target_pairs={{0,96},{32,64},{64,32},{96,0},{1,97},{33,65},{65,33},{97,1},{2,98}... | collective-permute-start | bytes 98312 | tf_op jit(solution)/shard_map/ppermute | solution.py:598
  2.6 1.0 %copy-start.2 = (bf16[5,32,8,128]{3,2,1,0:T(8,128)(2,1)S(1)}, bf16[5,32,8,128]{3,2,1,0:T(8,128)(2,1)}, u32[]{:S(2)}) copy-start(bf16[5,32,8,128]{3,2,1,0:T(8,128)(2,1)} %param.7) | copy-start | bytes 983044
  3.6 2.4 %copy-start.4 = (bf16[2,8,1024]{2,1,0:T(8,128)(2,1)S(1)}, bf16[2,8,1024]{2,1,0:T(8,128)(2,1)}, u32[]{:S(2)}) copy-start(bf16[2,8,1024]{2,1,0:T(8,128)(2,1)} %refs_0_.1) | copy-start | bytes 98308
  5.4 11.2 %copy-start.6 = (s32[5,8,16,4]{2,3,1,0:T(4,128)S(1)}, s32[5,8,16,4]{2,3,1,0:T(4,128)}, u32[]{:S(2)}) copy-start(s32[5,8,16,4]{2,3,1,0:T(4,128)} %param.11) | copy-start | bytes 30724
  5.4 11.2 %copy-start.7 = (s32[5,8,16,4]{2,3,1,0:T(4,128)S(1)}, s32[5,8,16,4]{2,3,1,0:T(4,128)}, u32[]{:S(2)}) copy-start(s32[5,8,16,4]{2,3,1,0:T(4,128)} %param.10) | copy-start | bytes 30724
  6.0 21.7 %copy-start.5 = (bf16[3,3,3,8,32]{4,3,2,1,0:T(8,128)(2,1)S(1)}, bf16[3,3,3,8,32]{4,3,2,1,0:T(8,128)(2,1)}, u32[]{:S(2)}) copy-start(bf16[3,3,3,8,32]{4,3,2,1,0:T(8,128)(2,1)} %param.12) | copy-start | bytes 41476
  6.0 29.1 %all-to-all-start = ((bf16[32,8,1920]{2,1,0:T(8,128)(2,1)}), bf16[32,8,1920]{2,1,0:T(8,128)(2,1)}, u32[]{:S(2)}, u32[]{:S(2)}) async-start(bf16[32,8,1920]{2,1,0:T(8,128)(2,1)} %bitcast.3), calls=%async_computation | async-start | bytes 1966080 | tf_op jit(solution)/shard_map/all_to_all | solution.py:613
  16.6 18.4 %copy-start = (bf16[5,8,4,64,64]{4,3,2,1,0:T(8,128)(2,1)S(1)}, bf16[5,8,4,64,64]{4,3,2,1,0:T(8,128)(2,1)}, u32[]{:S(2)}) copy-start(bf16[5,8,4,64,64]{4,3,2,1,0:T(8,128)(2,1)} %refs_4_.3) | copy-start | bytes 3932164
  16.6 16.7 %collective-permute-start.3 = (bf16[4,2,8,256]{3,2,1,0:T(8,128)(2,1)S(1)}, bf16[4,2,8,256]{3,2,1,0:T(8,128)(2,1)S(1)}, u32[]{:S(2)}, u32[]{:S(2)}) collective-permute-start(bf16[4,2,8,256]{3,2,1,0:T(8,128)(2,1)S(1)} %get-tuple-element.41), channel_id=1, source_target_pairs={{0,1},{1,2},{2,3},{3,4},{4,5},{5,6},{6,7},{7,8},{8,9},{9,10},{10,1... | collective-permute-start | bytes 98312 | tf_op jit(solution)/shard_map/ppermute | solution.py:614
  20.2 13.2 %collective-permute-start.4 = (bf16[4,2,8,256]{3,2,1,0:T(8,128)(2,1)S(1)}, bf16[4,2,8,256]{3,2,1,0:T(8,128)(2,1)S(1)}, u32[]{:S(2)}, u32[]{:S(2)}) collective-permute-start(bf16[4,2,8,256]{3,2,1,0:T(8,128)(2,1)S(1)} %get-tuple-element.42), channel_id=1, source_target_pairs={{1,0},{2,1},{3,2},{4,3},{5,4},{6,5},{7,6},{8,7},{9,8},{10,9},{11,1... | collective-permute-start | bytes 98312 | tf_op jit(solution)/shard_map/ppermute | solution.py:615
  38.7 3.1 %collective-permute-start.5 = (f32[4,256,128]{2,1,0:T(8,128)S(1)}, f32[4,256,128]{2,1,0:T(8,128)S(1)}, u32[]{:S(2)}, u32[]{:S(2)}) collective-permute-start(f32[4,256,128]{2,1,0:T(8,128)S(1)} %get-tuple-element.46), channel_id=1, source_target_pairs={{0,32},{32,0},{64,96},{96,64},{1,33},{33,1},{65,97},{97,65},{2,34}... | collective-permute-start | bytes 1572872 | tf_op jit(solution)/shard_map/ppermute | solution.py:598
  38.8 4.0 %collective-permute-start.7 = (f32[4,256,128]{2,1,0:T(8,128)S(1)}, f32[4,256,128]{2,1,0:T(8,128)S(1)}, u32[]{:S(2)}, u32[]{:S(2)}) collective-permute-start(f32[4,256,128]{2,1,0:T(8,128)S(1)} %get-tuple-element.50), channel_id=1, source_target_pairs={{0,32},{32,0},{64,96},{96,64},{1,33},{33,1},{65,97},{97,65},{2,34}... | collective-permute-start | bytes 1572872 | tf_op jit(solution)/shard_map/ppermute | solution.py:598
  41.8 9.4 %copy-start.3 = (bf16[32,1024]{1,0:T(8,128)(2,1)S(1)}, bf16[32,1024]{1,0:T(8,128)(2,1)}, u32[]{:S(2)}) copy-start(bf16[32,1024]{1,0:T(8,128)(2,1)} %ref_ref.3) | copy-start | bytes 196612
  41.9 11.2 %copy-start.1 = (f32[8,256,128]{2,1,0:T(8,128)S(1)}, f32[8,256,128]{2,1,0:T(8,128)}, u32[]{:S(2)}) copy-start(f32[8,256,128]{2,1,0:T(8,128)} %grad_cost.1.refs_7_) | copy-start | bytes 3145732
  41.9 9.2 %collective-permute-start.6 = (bf16[4,256,128]{2,1,0:T(8,128)(2,1)S(1)}, bf16[4,256,128]{2,1,0:T(8,128)(2,1)S(1)}, u32[]{:S(2)}, u32[]{:S(2)}) collective-permute-start(bf16[4,256,128]{2,1,0:T(8,128)(2,1)S(1)} %get-tuple-element.48), channel_id=1, source_target_pairs={{0,64},{32,96},{64,0},{96,32},{1,65},{33,97},{65,1},{97,33},{2,66}... | collective-permute-start | bytes 786440 | tf_op jit(solution)/shard_map/ppermute | solution.py:598
  43.4 15.3 %collective-permute-start.9 = (f32[3,256,128]{2,1,0:T(8,128)S(1)}, f32[3,256,128]{2,1,0:T(8,128)S(1)}, u32[]{:S(2)}, u32[]{:S(2)}) collective-permute-start(f32[3,256,128]{2,1,0:T(8,128)S(1)} %get-tuple-element.57), channel_id=1, source_target_pairs={{0,64},{32,96},{64,0},{96,32},{1,65},{33,97},{65,1},{97,33},{2,66}... | collective-permute-start | bytes 1179656 | tf_op jit(solution)/shard_map/ppermute | solution.py:598
  51.3 1.8 %collective-permute-start.8 = (bf16[4,256,128]{2,1,0:T(8,128)(2,1)S(1)}, bf16[4,256,128]{2,1,0:T(8,128)(2,1)S(1)}, u32[]{:S(2)}, u32[]{:S(2)}) collective-permute-start(bf16[4,256,128]{2,1,0:T(8,128)(2,1)S(1)} %mean.1.refs_6_), channel_id=1, source_target_pairs={{0,32},{32,0},{64,96},{96,64},{1,33},{33,1},{65,97},{97,65},{2,34}... | collective-permute-start | bytes 786440 | tf_op jit(solution)/shard_map/ppermute | solution.py:598
  59.5 2.9 %collective-permute-start.10 = (bf16[2,256,128]{2,1,0:T(8,128)(2,1)S(1)}, bf16[2,256,128]{2,1,0:T(8,128)(2,1)S(1)}, u32[]{:S(2)}, u32[]{:S(2)}) collective-permute-start(bf16[2,256,128]{2,1,0:T(8,128)(2,1)S(1)} %get-tuple-element.62), channel_id=1, source_target_pairs={{0,32},{32,0},{64,96},{96,64},{1,33},{33,1},{65,97},{97,65},{2,34}... | collective-permute-start | bytes 393224 | tf_op jit(solution)/shard_map/ppermute | solution.py:598
  62.9 25.3 %all-to-all-start.1 = ((bf16[32,8,1920]{2,1,0:T(8,128)(2,1)}), bf16[32,8,1920]{2,1,0:T(8,128)(2,1)S(1)}, u32[]{:S(2)}, u32[]{:S(2)}) async-start(bf16[32,8,1920]{2,1,0:T(8,128)(2,1)} %bitcast.17), calls=%async_computation.1 | async-start | bytes 1966080 | tf_op jit(solution)/shard_map/all_to_all | solution.py:642
  69.3 17.9 %collective-permute-start.11 = (bf16[4,64,128]{2,1,0:T(8,128)(2,1)S(1)}, bf16[4,64,128]{2,1,0:T(8,128)(2,1)S(1)}, u32[]{:S(2)}, u32[]{:S(2)}) collective-permute-start(bf16[4,64,128]{2,1,0:T(8,128)(2,1)S(1)} %get-tuple-element.69), channel_id=1, source_target_pairs={{0,1},{1,2},{2,3},{3,4},{4,5},{5,6},{6,7},{7,8},{8,9},{9,10},{10,1... | collective-permute-start | bytes 196616 | tf_op jit(solution)/shard_map/ppermute | solution.py:643
  72.6 14.5 %collective-permute-start.12 = (bf16[4,64,128]{2,1,0:T(8,128)(2,1)S(1)}, bf16[4,64,128]{2,1,0:T(8,128)(2,1)S(1)}, u32[]{:S(2)}, u32[]{:S(2)}) collective-permute-start(bf16[4,64,128]{2,1,0:T(8,128)(2,1)S(1)} %get-tuple-element.70), channel_id=1, source_target_pairs={{1,0},{2,1},{3,2},{4,3},{5,4},{6,5},{7,6},{8,7},{9,8},{10,9},{11,1... | collective-permute-start | bytes 196616 | tf_op jit(solution)/shard_map/ppermute | solution.py:644

commit v8 on v7

--- a/solution.py
+++ b/solution.py
@@ -210,7 +210,7 @@
     )(place, order, blocks, interp)
 
 
-CHAINS = 4
+CHAINS = 2
 
 
 def land_views(
@@ -231,14 +231,14 @@
             for g in range(16):
                 for k in range(4):
                     where = place_ref[base + g * 4 + k]
-                    accs[k][where] += spread[g * 16 : (g + 1) * 16, k * 128 : (k + 1) * 128]
+                    accs[k % 2][where] += spread[g * 16 : (g + 1) * 16, k * 128 : (k + 1) * 128]
         bands = []
         for band_row in range(12):
             columns_up, columns_low = [], []
             for half in range(2):
                 at = band_row * 4 + half * 2
-                even = (accs[0][at] + accs[1][at]) + (accs[2][at] + accs[3][at])
-                odd = (accs[0][at + 1] + accs[1][at + 1]) + (accs[2][at + 1] + accs[3][at + 1])
+                even = accs[0][at] + accs[1][at]
+                odd = accs[0][at + 1] + accs[1][at + 1]
                 up, low = pair_swap(even, odd)
                 columns_up.append(up)
                 columns_low.append(low)

time: 90.2 us -> 92.2 us (1.022)
  Pallas kernels: 23 us -> 25.2 us
    pallas_call x1, Pallas kernels: 5.29 us -> 7.02 us  [land_first(): pl.pallas_call(functools.partial(land_first_kernel, views), in_specs=[sme...]
  transfers between devices with their start and end apart: 15 -> 15, of which waited for: 6 -> 5; matrix products, arithmetic and copies ran while one was open for 1% -> 1% of each run, Pallas kernels for 18% -> 21%
where the time goes in v8:
time: 92.2 us; the launch traced here: 91.6 us
  starting transfers between devices  43 us (47%)
  Pallas kernels  25.2 us (27%)
  waiting for transfers between devices  20.5 us (22%)
  local copies, waits for them, and re-layouts  1.88 us (2%)
  between operations  0.93 us (1%)
    all_to_all x1, starting transfers between devices, body(): lax.all_to_all(operand, 'tile', split_axis=0, concat_axis=0, tiled=True)  10.6 us
    ppermute x9, waiting for transfers between devices, other(): return lax.ppermute(array, 'view', [(i, i ^ mask) for i in range(views)])  8.39 us
    pallas_call x1, Pallas kernels, land_first(): pl.pallas_call(functools.partial(land_first_kernel, views), in_specs=[sme...  7.02 us
    ppermute x1, starting transfers between devices, body(): bottom = lax.ppermute(initial, 'tile', down)  6.98 us
    ppermute x1, starting transfers between devices, body(): cost_bottom = lax.ppermute(cost_initial, 'tile', down)  6.98 us
    ppermute x1, waiting for transfers between devices, body(): cost_top = lax.ppermute(cost_last, 'tile', up)  6.79 us
    all_to_all x1, starting transfers between devices, body(): lax.all_to_all(landed, 'tile', split_axis=0, concat_axis=0, tiled=True)  6.37 us
    ppermute x1, waiting for transfers between devices, body(): top = lax.ppermute(last, 'tile', up)  5.29 us
  transfers between devices with their start and end apart: 15, of which 5 were waited for; matrix products, arithmetic and copies ran while one was open for 1% of the time, Pallas kernels for 21%

profile of v8, /device:TPU:32, one launch (start us, length us, event | category | flops | bytes accessed | tf_op | source)
XLA Modules:
  0.0 91.6 jit_solution(1612973692677055035)
XLA Ops:
  0.7 1.7 %collective-permute-start.1 = (bf16[2,8,1024]{2,1,0:T(8,128)(2,1)}, bf16[2,8,1024]{2,1,0:T(8,128)(2,1)S(1)}, u32[]{:S(2)}, u32[]{:S(2)}) collective-permute-start(bf16[2,8,1024]{2,1,0:T(8,128)(2,1)} %refs_0_.1), channel_id=1, source_target_pairs={{0,64},{32,96},{64,0},{96,32},{1,65},{33,97},{65,1},{97,33},{2,66}... | collective-permute-start | bytes 98312 | tf_op jit(solution)/shard_map/ppermute | solution.py:598
  2.6 1.0 %copy-done.2 = bf16[5,32,8,128]{3,2,1,0:T(8,128)(2,1)S(1)} copy-done((bf16[5,32,8,128]{3,2,1,0:T(8,128)(2,1)S(1)}, bf16[5,32,8,128]{3,2,1,0:T(8,128)(2,1)}, u32[]{:S(2)}) %copy-start.2) | copy-done | bytes 327704
  3.6 1.9 %strips.1 = bf16[256,1920]{1,0:T(8,128)(2,1)} custom-call(bf16[1280,128]{1,0:T(8,128)(2,1)S(1)} %bitcast.16), custom_call_target="tpu_custom_call" | custom-call | tf_op jit(solution)/shard_map/strips/pallas_call | solution.py:68
  6.0 10.6 %all-to-all-start = ((bf16[32,8,1920]{2,1,0:T(8,128)(2,1)}), bf16[32,8,1920]{2,1,0:T(8,128)(2,1)}, u32[]{:S(2)}, u32[]{:S(2)}) async-start(bf16[32,8,1920]{2,1,0:T(8,128)(2,1)} %bitcast.3), calls=%async_computation | async-start | bytes 1966080 | tf_op jit(solution)/shard_map/all_to_all | solution.py:613
  16.6 3.5 %collective-permute-start.3 = (bf16[4,2,8,256]{3,2,1,0:T(8,128)(2,1)S(1)}, bf16[4,2,8,256]{3,2,1,0:T(8,128)(2,1)S(1)}, u32[]{:S(2)}, u32[]{:S(2)}) collective-permute-start(bf16[4,2,8,256]{3,2,1,0:T(8,128)(2,1)S(1)} %get-tuple-element.41), channel_id=1, source_target_pairs={{0,1},{1,2},{2,3},{3,4},{4,5},{5,6},{6,7},{7,8},{8,9},{9,10},{10,1... | collective-permute-start | bytes 98312 | tf_op jit(solution)/shard_map/ppermute | solution.py:614
  20.2 7.0 %collective-permute-start.4 = (bf16[4,2,8,256]{3,2,1,0:T(8,128)(2,1)S(1)}, bf16[4,2,8,256]{3,2,1,0:T(8,128)(2,1)S(1)}, u32[]{:S(2)}, u32[]{:S(2)}) collective-permute-start(bf16[4,2,8,256]{3,2,1,0:T(8,128)(2,1)S(1)} %get-tuple-element.42), channel_id=1, source_target_pairs={{1,0},{2,1},{3,2},{4,3},{5,4},{6,5},{7,6},{8,7},{9,8},{10,9},{11,1... | collective-permute-start | bytes 98312 | tf_op jit(solution)/shard_map/ppermute | solution.py:615
  28.1 5.3 %collective-permute-done.3.top_ref = bf16[4,2,8,256]{3,2,1,0:T(8,128)(2,1)S(1)} collective-permute-done((bf16[4,2,8,256]{3,2,1,0:T(8,128)(2,1)S(1)}, bf16[4,2,8,256]{3,2,1,0:T(8,128)(2,1)S(1)}, u32[]{:S(2)}, u32[]{:S(2)}) %collective-permute-start.3) | collective-permute-done | bytes 32800 | tf_op jit(solution)/shard_map/ppermute | solution.py:614
  33.4 1.6 %grad_cost.1.refs_7_ = f32[8,256,128]{2,1,0:T(8,128)} custom-call(s32[1]{0:T(128)} %bitcast.5.view_ref, bf16[4,2,8,1024]{3,2,1,0:T(8,128)(2,1)S(1)} %get-tuple-element.40.own_ref, bf16[4,2,8,256]{3,2,1,0:T(8,128)(2,1)S(1)} %collective-permute-done.3.top_ref, bf16[4,2,8,256]{3,2,1,0:T(8,128)(2,1)S(1)} %collective-permute-done.4.bottom_ref, ...), custom_call_target="tpu_custom_call" | custom-call | tf_op jit(solution)/shard_map/grad_cost/pallas_call | solution.py:493
  35.1 3.6 %warp_other.1 = (bf16[240,16,128]{2,1,0:T(8,128)(2,1)S(1)}, f32[4,256,128]{2,1,0:T(8,128)S(1)}, f32[4,256,128]{2,1,0:T(8,128)S(1)}, bf16[5,4,256,128]{3,2,1,0:T(8,128)(2,1)S(1)}) custom-call(s32[2560]{0:T(1024)S(1)} %reshape.26.place_ref.refs_0_, s32[8]{0:T(128)S(1)} %fusion.order_ref.refs_1_, bf16[256,1920]{1,0:T(8,128)(2,1)} %bitcast.4.in_ref, ...), custom_call_target="tpu_custom_call" | custom-call | tf_op jit(solution)/shard_map/warp_other/pallas_call | solution.py:192
  39.2 2.5 %warp_mine.1 = (f32[4,256,128]{2,1,0:T(8,128)S(1)}, f32[4,256,128]{2,1,0:T(8,128)S(1)}, bf16[5,4,256,128]{3,2,1,0:T(8,128)(2,1)S(1)}) custom-call(s32[2560]{0:T(1024)S(1)} %reshape.26.place_ref.refs_0_, s32[8]{0:T(128)S(1)} %fusion.order_ref.refs_1_, bf16[240,16,128]{2,1,0:T(8,128)(2,1)S(1)} %get-tuple-element.44.blocks_ref, ...), custom_call_target="tpu_custom_call" | custom-call | tf_op jit(solution)/shard_map/warp_mine/pallas_call | solution.py:203
  41.9 0.8 collective-permute-start.6
  42.7 0.6 chip_second.1
  43.4 1.4 %collective-permute-start.9 = (f32[3,256,128]{2,1,0:T(8,128)S(1)}, f32[3,256,128]{2,1,0:T(8,128)S(1)}, u32[]{:S(2)}, u32[]{:S(2)}) collective-permute-start(f32[3,256,128]{2,1,0:T(8,128)S(1)} %get-tuple-element.57), channel_id=1, source_target_pairs={{0,64},{32,96},{64,0},{96,32},{1,65},{33,97},{65,1},{97,33},{2,66}... | collective-permute-start | bytes 1179656 | tf_op jit(solution)/shard_map/ppermute | solution.py:598
  44.8 6.3 %collective-permute-done.6.there_ref.first_there = bf16[4,256,128]{2,1,0:T(8,128)(2,1)S(1)} collective-permute-done((bf16[4,256,128]{2,1,0:T(8,128)(2,1)S(1)}, bf16[4,256,128]{2,1,0:T(8,128)(2,1)S(1)}, u32[]{:S(2)}, u32[]{:S(2)}) %collective-permute-start.6) | collective-permute-done | bytes 262176 | tf_op jit(solution)/shard_map/ppermute | solution.py:598
  51.5 1.5 %collective-permute-done.8.refs_5_ = bf16[4,256,128]{2,1,0:T(8,128)(2,1)S(1)} collective-permute-done((bf16[4,256,128]{2,1,0:T(8,128)(2,1)S(1)}, bf16[4,256,128]{2,1,0:T(8,128)(2,1)S(1)}, u32[]{:S(2)}, u32[]{:S(2)}) %collective-permute-start.8) | collective-permute-done | bytes 262176 | tf_op jit(solution)/shard_map/ppermute | solution.py:598
  53.1 7.0 %land_first.1.refs_8_ = bf16[256,1536]{1,0:T(8,128)(2,1)S(1)} custom-call(s32[2560]{0:T(1024)S(1)} %reshape.26.place_ref.refs_0_, s32[8]{0:T(128)S(1)} %fusion.order_ref.refs_1_, bf16[5,4,256,128]{3,2,1,0:T(8,128)(2,1)S(1)} %get-tuple-element.54.refs_2_, bf16[5,4,256,128]{3,2,1,0:T(8,128)(2,1)S(1)} %get-tuple-element.55.refs_3_, ...), custom_call_target="tpu_custom_call" | custom-call | flops 1000 | bytes 1000 | tf_op jit(solution)/shard_map/land_first/pallas_call | solution.py:271
  60.1 0.7 cost.1
  61.1 3.3 %land_last.1 = bf16[256,1920]{1,0:T(8,128)(2,1)} custom-call(s32[2560]{0:T(1024)S(1)} %reshape.26.place_ref.refs_0_, s32[8]{0:T(128)S(1)} %fusion.order_ref.refs_1_, bf16[5,4,256,128]{3,2,1,0:T(8,128)(2,1)S(1)} %get-tuple-element.54.refs_2_, bf16[5,4,256,128]{3,2,1,0:T(8,128)(2,1)S(1)} %get-tuple-element.55.refs_3_, bf16[5,8,4,64,64]{4,3,2,1,0:T(8,128)(2,1)S(1)} %copy-done, ...), custom_call_target="tpu_custom_call" | custom-call | flops 1000 | bytes 1000 | tf_op jit(solution)/shard_map/land_last/pallas_call | solution.py:284
  64.9 6.4 %all-to-all-start.1 = ((bf16[32,8,1920]{2,1,0:T(8,128)(2,1)}), bf16[32,8,1920]{2,1,0:T(8,128)(2,1)S(1)}, u32[]{:S(2)}, u32[]{:S(2)}) async-start(bf16[32,8,1920]{2,1,0:T(8,128)(2,1)} %bitcast.17), calls=%async_computation.1 | async-start | bytes 1966080 | tf_op jit(solution)/shard_map/all_to_all | solution.py:642
  71.3 3.4 %collective-permute-start.11 = (bf16[4,64,128]{2,1,0:T(8,128)(2,1)S(1)}, bf16[4,64,128]{2,1,0:T(8,128)(2,1)S(1)}, u32[]{:S(2)}, u32[]{:S(2)}) collective-permute-start(bf16[4,64,128]{2,1,0:T(8,128)(2,1)S(1)} %get-tuple-element.69), channel_id=1, source_target_pairs={{0,1},{1,2},{2,3},{3,4},{4,5},{5,6},{6,7},{7,8},{8,9},{9,10},{10,1... | collective-permute-start | bytes 196616 | tf_op jit(solution)/shard_map/ppermute | solution.py:643
  74.7 7.0 %collective-permute-start.12 = (bf16[4,64,128]{2,1,0:T(8,128)(2,1)S(1)}, bf16[4,64,128]{2,1,0:T(8,128)(2,1)S(1)}, u32[]{:S(2)}, u32[]{:S(2)}) collective-permute-start(bf16[4,64,128]{2,1,0:T(8,128)(2,1)S(1)} %get-tuple-element.70), channel_id=1, source_target_pairs={{1,0},{2,1},{3,2},{4,3},{5,4},{6,5},{7,6},{8,7},{9,8},{10,9},{11,1... | collective-permute-start | bytes 196616 | tf_op jit(solution)/shard_map/ppermute | solution.py:644
  82.3 6.8 %collective-permute-done.11.top_ref = bf16[4,64,128]{2,1,0:T(8,128)(2,1)S(1)} collective-permute-done((bf16[4,64,128]{2,1,0:T(8,128)(2,1)S(1)}, bf16[4,64,128]{2,1,0:T(8,128)(2,1)S(1)}, u32[]{:S(2)}, u32[]{:S(2)}) %collective-permute-start.11) | collective-permute-done | bytes 65568 | tf_op jit(solution)/shard_map/ppermute | solution.py:643
  89.1 1.0 %conv_rows.1 = bf16[2,8,1024]{2,1,0:T(8,128)(2,1)} custom-call(f32[2,8,1024]{2,1,0:T(8,128)S(1)} %conv.1.main_ref, bf16[4,64,128]{2,1,0:T(8,128)(2,1)S(1)} %collective-permute-done.11.top_ref, bf16[4,64,128]{2,1,0:T(8,128)(2,1)S(1)} %collective-permute-done.12.bottom_ref, bf16[72,96]{1,0:T(8,128)(2,1)S(1)} %reshape.30.weight_ref), custom_call_target="tpu_custom_call" | custom-call | tf_op jit(solution)/shard_map/conv_rows/pallas_call | solution.py:572
  90.1 1.5 %unstrips.1 = f32[1280,128]{1,0:T(8,128)} custom-call(bf16[256,1920]{1,0:T(8,128)(2,1)S(1)} %bitcast.15), custom_call_target="tpu_custom_call" | custom-call | tf_op jit(solution)/shard_map/unstrips/pallas_call | solution.py:99
  (47 shorter events, 4.3 us)
Async XLA Ops:
  0.6 4.8 %collective-permute-start = (bf16[2,8,1024]{2,1,0:T(8,128)(2,1)}, bf16[2,8,1024]{2,1,0:T(8,128)(2,1)S(1)}, u32[]{:S(2)}, u32[]{:S(2)}) collective-permute-start(bf16[2,8,1024]{2,1,0:T(8,128)(2,1)} %refs_0_.1), channel_id=1, source_target_pairs={{0,32},{32,0},{64,96},{96,64},{1,33},{33,1},{65,97},{97,65},{2,34}... | collective-permute-start | bytes 98312 | tf_op jit(solution)/shard_map/ppermute | solution.py:598
  0.7 4.7 %collective-permute-start.1 = (bf16[2,8,1024]{2,1,0:T(8,128)(2,1)}, bf16[2,8,1024]{2,1,0:T(8,128)(2,1)S(1)}, u32[]{:S(2)}, u32[]{:S(2)}) collective-permute-start(bf16[2,8,1024]{2,1,0:T(8,128)(2,1)} %refs_0_.1), channel_id=1, source_target_pairs={{0,64},{32,96},{64,0},{96,32},{1,65},{33,97},{65,1},{97,33},{2,66}... | collective-permute-start | bytes 98312 | tf_op jit(solution)/shard_map/ppermute | solution.py:598
  2.4 3.6 %collective-permute-start.2 = (bf16[2,8,1024]{2,1,0:T(8,128)(2,1)}, bf16[2,8,1024]{2,1,0:T(8,128)(2,1)S(1)}, u32[]{:S(2)}, u32[]{:S(2)}) collective-permute-start(bf16[2,8,1024]{2,1,0:T(8,128)(2,1)} %refs_0_.1), channel_id=1, source_target_pairs={{0,96},{32,64},{64,32},{96,0},{1,97},{33,65},{65,33},{97,1},{2,98}... | collective-permute-start | bytes 98312 | tf_op jit(solution)/shard_map/ppermute | solution.py:598
  2.6 1.0 %copy-start.2 = (bf16[5,32,8,128]{3,2,1,0:T(8,128)(2,1)S(1)}, bf16[5,32,8,128]{3,2,1,0:T(8,128)(2,1)}, u32[]{:S(2)}) copy-start(bf16[5,32,8,128]{3,2,1,0:T(8,128)(2,1)} %param.7) | copy-start | bytes 983044
  3.6 2.4 %copy-start.4 = (bf16[2,8,1024]{2,1,0:T(8,128)(2,1)S(1)}, bf16[2,8,1024]{2,1,0:T(8,128)(2,1)}, u32[]{:S(2)}) copy-start(bf16[2,8,1024]{2,1,0:T(8,128)(2,1)} %refs_0_.1) | copy-start | bytes 98308
  5.4 11.2 %copy-start.6 = (s32[5,8,16,4]{2,3,1,0:T(4,128)S(1)}, s32[5,8,16,4]{2,3,1,0:T(4,128)}, u32[]{:S(2)}) copy-start(s32[5,8,16,4]{2,3,1,0:T(4,128)} %param.11) | copy-start | bytes 30724
  5.4 11.2 %copy-start.7 = (s32[5,8,16,4]{2,3,1,0:T(4,128)S(1)}, s32[5,8,16,4]{2,3,1,0:T(4,128)}, u32[]{:S(2)}) copy-start(s32[5,8,16,4]{2,3,1,0:T(4,128)} %param.10) | copy-start | bytes 30724
  6.0 21.7 %copy-start.5 = (bf16[3,3,3,8,32]{4,3,2,1,0:T(8,128)(2,1)S(1)}, bf16[3,3,3,8,32]{4,3,2,1,0:T(8,128)(2,1)}, u32[]{:S(2)}) copy-start(bf16[3,3,3,8,32]{4,3,2,1,0:T(8,128)(2,1)} %param.12) | copy-start | bytes 41476
  6.0 29.1 %all-to-all-start = ((bf16[32,8,1920]{2,1,0:T(8,128)(2,1)}), bf16[32,8,1920]{2,1,0:T(8,128)(2,1)}, u32[]{:S(2)}, u32[]{:S(2)}) async-start(bf16[32,8,1920]{2,1,0:T(8,128)(2,1)} %bitcast.3), calls=%async_computation | async-start | bytes 1966080 | tf_op jit(solution)/shard_map/all_to_all | solution.py:613
  16.6 18.4 %copy-start = (bf16[5,8,4,64,64]{4,3,2,1,0:T(8,128)(2,1)S(1)}, bf16[5,8,4,64,64]{4,3,2,1,0:T(8,128)(2,1)}, u32[]{:S(2)}) copy-start(bf16[5,8,4,64,64]{4,3,2,1,0:T(8,128)(2,1)} %refs_4_.3) | copy-start | bytes 3932164
  16.6 16.7 %collective-permute-start.3 = (bf16[4,2,8,256]{3,2,1,0:T(8,128)(2,1)S(1)}, bf16[4,2,8,256]{3,2,1,0:T(8,128)(2,1)S(1)}, u32[]{:S(2)}, u32[]{:S(2)}) collective-permute-start(bf16[4,2,8,256]{3,2,1,0:T(8,128)(2,1)S(1)} %get-tuple-element.41), channel_id=1, source_target_pairs={{0,1},{1,2},{2,3},{3,4},{4,5},{5,6},{6,7},{7,8},{8,9},{9,10},{10,1... | collective-permute-start | bytes 98312 | tf_op jit(solution)/shard_map/ppermute | solution.py:614
  20.2 13.2 %collective-permute-start.4 = (bf16[4,2,8,256]{3,2,1,0:T(8,128)(2,1)S(1)}, bf16[4,2,8,256]{3,2,1,0:T(8,128)(2,1)S(1)}, u32[]{:S(2)}, u32[]{:S(2)}) collective-permute-start(bf16[4,2,8,256]{3,2,1,0:T(8,128)(2,1)S(1)} %get-tuple-element.42), channel_id=1, source_target_pairs={{1,0},{2,1},{3,2},{4,3},{5,4},{6,5},{7,6},{8,7},{9,8},{10,9},{11,1... | collective-permute-start | bytes 98312 | tf_op jit(solution)/shard_map/ppermute | solution.py:615
  38.7 3.1 %collective-permute-start.5 = (f32[4,256,128]{2,1,0:T(8,128)S(1)}, f32[4,256,128]{2,1,0:T(8,128)S(1)}, u32[]{:S(2)}, u32[]{:S(2)}) collective-permute-start(f32[4,256,128]{2,1,0:T(8,128)S(1)} %get-tuple-element.46), channel_id=1, source_target_pairs={{0,32},{32,0},{64,96},{96,64},{1,33},{33,1},{65,97},{97,65},{2,34}... | collective-permute-start | bytes 1572872 | tf_op jit(solution)/shard_map/ppermute | solution.py:598
  38.8 4.0 %collective-permute-start.7 = (f32[4,256,128]{2,1,0:T(8,128)S(1)}, f32[4,256,128]{2,1,0:T(8,128)S(1)}, u32[]{:S(2)}, u32[]{:S(2)}) collective-permute-start(f32[4,256,128]{2,1,0:T(8,128)S(1)} %get-tuple-element.50), channel_id=1, source_target_pairs={{0,32},{32,0},{64,96},{96,64},{1,33},{33,1},{65,97},{97,65},{2,34}... | collective-permute-start | bytes 1572872 | tf_op jit(solution)/shard_map/ppermute | solution.py:598
  41.8 9.4 %copy-start.3 = (bf16[32,1024]{1,0:T(8,128)(2,1)S(1)}, bf16[32,1024]{1,0:T(8,128)(2,1)}, u32[]{:S(2)}) copy-start(bf16[32,1024]{1,0:T(8,128)(2,1)} %ref_ref.3) | copy-start | bytes 196612
  41.9 11.2 %copy-start.1 = (f32[8,256,128]{2,1,0:T(8,128)S(1)}, f32[8,256,128]{2,1,0:T(8,128)}, u32[]{:S(2)}) copy-start(f32[8,256,128]{2,1,0:T(8,128)} %grad_cost.1.refs_7_) | copy-start | bytes 3145732
  41.9 9.2 %collective-permute-start.6 = (bf16[4,256,128]{2,1,0:T(8,128)(2,1)S(1)}, bf16[4,256,128]{2,1,0:T(8,128)(2,1)S(1)}, u32[]{:S(2)}, u32[]{:S(2)}) collective-permute-start(bf16[4,256,128]{2,1,0:T(8,128)(2,1)S(1)} %get-tuple-element.48), channel_id=1, source_target_pairs={{0,64},{32,96},{64,0},{96,32},{1,65},{33,97},{65,1},{97,33},{2,66}... | collective-permute-start | bytes 786440 | tf_op jit(solution)/shard_map/ppermute | solution.py:598
  43.4 16.7 %collective-permute-start.9 = (f32[3,256,128]{2,1,0:T(8,128)S(1)}, f32[3,256,128]{2,1,0:T(8,128)S(1)}, u32[]{:S(2)}, u32[]{:S(2)}) collective-permute-start(f32[3,256,128]{2,1,0:T(8,128)S(1)} %get-tuple-element.57), channel_id=1, source_target_pairs={{0,64},{32,96},{64,0},{96,32},{1,65},{33,97},{65,1},{97,33},{2,66}... | collective-permute-start | bytes 1179656 | tf_op jit(solution)/shard_map/ppermute | solution.py:598
  51.3 1.8 %collective-permute-start.8 = (bf16[4,256,128]{2,1,0:T(8,128)(2,1)S(1)}, bf16[4,256,128]{2,1,0:T(8,128)(2,1)S(1)}, u32[]{:S(2)}, u32[]{:S(2)}) collective-permute-start(bf16[4,256,128]{2,1,0:T(8,128)(2,1)S(1)} %mean.1.refs_6_), channel_id=1, source_target_pairs={{0,32},{32,0},{64,96},{96,64},{1,33},{33,1},{65,97},{97,65},{2,34}... | collective-permute-start | bytes 786440 | tf_op jit(solution)/shard_map/ppermute | solution.py:598
  60.8 3.5 %collective-permute-start.10 = (bf16[2,256,128]{2,1,0:T(8,128)(2,1)S(1)}, bf16[2,256,128]{2,1,0:T(8,128)(2,1)S(1)}, u32[]{:S(2)}, u32[]{:S(2)}) collective-permute-start(bf16[2,256,128]{2,1,0:T(8,128)(2,1)S(1)} %get-tuple-element.62), channel_id=1, source_target_pairs={{0,32},{32,0},{64,96},{96,64},{1,33},{33,1},{65,97},{97,65},{2,34}... | collective-permute-start | bytes 393224 | tf_op jit(solution)/shard_map/ppermute | solution.py:598
  64.9 25.2 %all-to-all-start.1 = ((bf16[32,8,1920]{2,1,0:T(8,128)(2,1)}), bf16[32,8,1920]{2,1,0:T(8,128)(2,1)S(1)}, u32[]{:S(2)}, u32[]{:S(2)}) async-start(bf16[32,8,1920]{2,1,0:T(8,128)(2,1)} %bitcast.17), calls=%async_computation.1 | async-start | bytes 1966080 | tf_op jit(solution)/shard_map/all_to_all | solution.py:642
  71.3 17.8 %collective-permute-start.11 = (bf16[4,64,128]{2,1,0:T(8,128)(2,1)S(1)}, bf16[4,64,128]{2,1,0:T(8,128)(2,1)S(1)}, u32[]{:S(2)}, u32[]{:S(2)}) collective-permute-start(bf16[4,64,128]{2,1,0:T(8,128)(2,1)S(1)} %get-tuple-element.69), channel_id=1, source_target_pairs={{0,1},{1,2},{2,3},{3,4},{4,5},{5,6},{6,7},{7,8},{8,9},{9,10},{10,1... | collective-permute-start | bytes 196616 | tf_op jit(solution)/shard_map/ppermute | solution.py:643
  74.7 14.4 %collective-permute-start.12 = (bf16[4,64,128]{2,1,0:T(8,128)(2,1)S(1)}, bf16[4,64,128]{2,1,0:T(8,128)(2,1)S(1)}, u32[]{:S(2)}, u32[]{:S(2)}) collective-permute-start(bf16[4,64,128]{2,1,0:T(8,128)(2,1)S(1)} %get-tuple-element.70), channel_id=1, source_target_pairs={{1,0},{2,1},{3,2},{4,3},{5,4},{6,5},{7,6},{8,7},{9,8},{10,9},{11,1... | collective-permute-start | bytes 196616 | tf_op jit(solution)/shard_map/ppermute | solution.py:644
